TPU v7x, 512 devices: a whole 4x4x16 slice. The times are simulated.
512 devices in a mesh: ctx: 64 (over z, x_hi, core), kvh: 8 (over y, x_lo).
Axes of the slice: x: 4 (x_hi: 2, x_lo: 2; x = x_hi * 2 + x_lo), y: 4, z: 16, core: 2. Of those that a mesh axis runs over, the one named last changes fastest.
Arguments:
- query: bfloat16 [24576, 4096], P('ctx', 'kvh'), may hold values from -256 to 256
- keys_values: bfloat16 [24576, 2048], P('ctx', 'kvh'), may hold values from -4 to 4
- doc_start: int32 [24576], P('ctx'), may hold values from 0 to 24528, as said below
- scale_index: int32 [192], replicated, may hold values from 0 to 63
- scale_table: float32 [64, 16], P(None, 'kvh'), may hold values from 0.5 to 2
- out_weight: bfloat16 [4096, 4096], P('kvh'), may hold values from -0.09375 to 0.09375
Outputs:
- projected: bfloat16 [24576, 4096], P(('ctx', 'kvh'))
Inputs may be any that keep to these rules, and one draw needn't show every extreme that they name: doc_start[i] is the first position of the document that holds token i; documents are consecutive runs of 48 to 6144 tokens, except that the document just before the last may be cut short; the last document is exactly the final 48 tokens, and one of the first three documents has exactly 6144 tokens.
All inputs are finite; a program needn't handle non-finite values.
Results may differ from a plain program's by a relative error of at most 0.019.
Values may be sent and summed in bfloat16 or wider, within the bound.
No kernel may reach another device: no remote copies, remote signals or barrier semaphores. Data moves between devices by JAX's collectives and lax.ppermute only.
A program may use at most 64 MiB of HBM per device.

v0:
```python
import math

import jax
import jax.numpy as jnp
from jax import lax
from jax.sharding import PartitionSpec as P

H = 32
KVH = 8
HD = 128
SBLK = 128
SCALES = 64


def passed_along(block, axis, distance):
    devices = range(lax.axis_size(axis))
    route = [(i - distance, i) for i in devices if i - distance in devices]
    return lax.ppermute(block, axis, route)


def local(query, keys_values, doc_start, scale_index, scale_table, out_weight):
    tok_rows = query.shape[0]
    kv_heads = keys_values.shape[1] // (2 * HD)
    q_groups = H // KVH
    ctx_count = lax.axis_size("ctx")
    reach_blocks = ctx_count // 4
    my_index = lax.axis_index("ctx")
    query_heads = query.reshape(tok_rows, kv_heads, q_groups, HD)
    local_rows = jnp.arange(tok_rows, dtype=jnp.int32)
    query_pos = my_index * tok_rows + local_rows
    score_factor = 1.0 / math.sqrt(HD)
    scale_blocks = tok_rows // SBLK
    scale_levels = jnp.arange(SCALES, dtype=jnp.int32)

    def lookup_scales(source_index):
        begin = jnp.clip(source_index, 0, ctx_count - 1) * scale_blocks
        picked = lax.dynamic_slice_in_dim(scale_index, begin, scale_blocks, 0)
        one_hot = (picked[:, None] == scale_levels[None, :]).astype(jnp.float32)
        per_block = jnp.dot(one_hot, scale_table, precision=lax.Precision.HIGHEST)
        per_key = jnp.broadcast_to(
            per_block[:, None, :], (scale_blocks, SBLK, 2 * kv_heads)
        ).reshape(tok_rows, 2 * kv_heads)
        return (per_key[:, 0::2].T, per_key[:, 1::2].T)

    def attend_block(softmax_state, kv_block, source_index):
        row_max, row_total, weighted = softmax_state
        key_scale, value_scale = lookup_scales(source_index)
        split_block = kv_block.reshape(tok_rows, kv_heads, 2, HD)
        key_rows = split_block[:, :, 0, :]
        value_rows = split_block[:, :, 1, :]
        key_pos = source_index * tok_rows + local_rows
        visible = (key_pos[None, :] >= doc_start[:, None]) & (
            key_pos[None, :] <= query_pos[:, None]
        )
        scores = jnp.einsum(
            "tkgd,skd->ktgs", query_heads, key_rows, preferred_element_type=jnp.float32
        )
        scores = scores * (key_scale * score_factor)[:, None, None, :]
        scores = jnp.where(visible[None, :, None, :], scores, -jnp.inf)
        new_max = jnp.maximum(row_max, jnp.max(scores, axis=3))
        carry_factor = jnp.exp(row_max - new_max)
        probs = jnp.exp(scores - new_max[..., None])
        row_total = row_total * carry_factor + jnp.sum(probs, axis=3)
        weights = (probs * value_scale[:, None, None, :]).astype(jnp.bfloat16)
        weighted = weighted * carry_factor[..., None] + jnp.einsum(
            "ktgs,skd->ktgd", weights, value_rows, preferred_element_type=jnp.float32
        )
        return (new_max, row_total, weighted)

    def remote_block(softmax_state, kv_block, source_index):
        return attend_block(softmax_state, kv_block, source_index)

    state_shape = (kv_heads, tok_rows, q_groups)
    softmax_state = (
        jnp.full(state_shape, -jnp.inf, jnp.float32),
        jnp.zeros(state_shape, jnp.float32),
        jnp.zeros(state_shape + (HD,), jnp.float32),
    )
    softmax_state = attend_block(softmax_state, keys_values, my_index)

    def forward_step(offset, carried):
        moving, state_in = carried
        moving = passed_along(moving, "ctx", 1)
        return (moving, remote_block(state_in, moving, my_index - offset))

    moving_end, softmax_state = lax.fori_loop(
        1, reach_blocks + 1, forward_step, (keys_values, softmax_state)
    )
    row_max, row_total, weighted = softmax_state
    attn_heads = (weighted / row_total[..., None]).astype(jnp.bfloat16)
    attn_rows = jnp.transpose(attn_heads, (1, 0, 2, 3)).reshape(tok_rows, kv_heads * q_groups * HD)
    picked = attn_rows
    return lax.psum_scatter(
        jnp.dot(picked, out_weight, preferred_element_type=jnp.float32).astype(jnp.bfloat16),
        "kvh",
        scatter_dimension=0,
        tiled=True,
    )


def solution(mesh):
    placed = (P("ctx", "kvh"), P("ctx", "kvh"), P("ctx"), P(), P(None, "kvh"), P("kvh", None))
    return jax.shard_map(
        local, mesh=mesh, in_specs=placed, out_specs=P(("ctx", "kvh"), None), check_vma=False
    )
```

profile of v0, /device:TPU:1, one launch (start us, length us, event | category | flops | bytes accessed | tf_op | source)
XLA Modules:
  0.0 335.1 jit_solution(9833951856811933602)
XLA Ops:
  9.4 1.2 copy.32
  11.5 1.6 fusion.20
  13.9 1.9 fusion.22
  15.8 192.5 %while.20 = (s32[]{:T(128)}, bf16[384,256]{0,1:T(8,128)(2,1)S(1)}, f32[1,384,4]{1,2,0:T(4,128)S(1)}, f32[1,384,4]{1,2,0:T(4,128)S(1)}, f32[1,384,4,128]{3,1,2,0:...) while((s32[]{:T(128)}, bf16[384,256]{0,1:T(8,128)(2,1)S(1)}, ...), condition=%wide.region_5.6_spmd.clone, body=%wide.region_2.5_spmd.clone.sunk | while | flops 309913920 | bytes 17431484 | solution.py:86
  15.8 6.0 %collective-permute-start = (bf16[384,256]{0,1:T(8,128)(2,1)S(1)}, bf16[384,256]{0,1:T(8,128)(2,1)S(1)}, u32[]{:S(2)}, u32[]{:S(2)}) collective-permute-start(bf16[384,256]{0,1:T(8,128)(2,1)S(1)} %get-tuple-element.406), channel_id=1, source_target_pairs={{0,8},{8,16},{16,24},{24,32},{32,40},{40,48},{48,56},{56,64},{64,7... | collective-permute-start | bytes 589832 | tf_op jit(solution)/shard_map/while/body/eval_jaxpr/ppermute | solution.py:18
  22.5 2.4 collective-permute-done
  26.1 1.2 fusion.47
  28.2 5.4 %collective-permute-start = (bf16[384,256]{0,1:T(8,128)(2,1)S(1)}, bf16[384,256]{0,1:T(8,128)(2,1)S(1)}, u32[]{:S(2)}, u32[]{:S(2)}) collective-permute-start(bf16[384,256]{0,1:T(8,128)(2,1)S(1)} %get-tuple-element.406), channel_id=1, source_target_pairs={{0,8},{8,16},{16,24},{24,32},{32,40},{40,48},{48,56},{56,64},{64,7... | collective-permute-start | bytes 589832 | tf_op jit(solution)/shard_map/while/body/eval_jaxpr/ppermute | solution.py:18
  34.2 2.0 collective-permute-done
  39.5 5.9 %collective-permute-start = (bf16[384,256]{0,1:T(8,128)(2,1)S(1)}, bf16[384,256]{0,1:T(8,128)(2,1)S(1)}, u32[]{:S(2)}, u32[]{:S(2)}) collective-permute-start(bf16[384,256]{0,1:T(8,128)(2,1)S(1)} %get-tuple-element.406), channel_id=1, source_target_pairs={{0,8},{8,16},{16,24},{24,32},{32,40},{40,48},{48,56},{56,64},{64,7... | collective-permute-start | bytes 589832 | tf_op jit(solution)/shard_map/while/body/eval_jaxpr/ppermute | solution.py:18
  46.0 2.0 collective-permute-done
  49.2 1.2 fusion.47
  51.3 5.9 %collective-permute-start = (bf16[384,256]{0,1:T(8,128)(2,1)S(1)}, bf16[384,256]{0,1:T(8,128)(2,1)S(1)}, u32[]{:S(2)}, u32[]{:S(2)}) collective-permute-start(bf16[384,256]{0,1:T(8,128)(2,1)S(1)} %get-tuple-element.406), channel_id=1, source_target_pairs={{0,8},{8,16},{16,24},{24,32},{32,40},{40,48},{48,56},{56,64},{64,7... | collective-permute-start | bytes 589832 | tf_op jit(solution)/shard_map/while/body/eval_jaxpr/ppermute | solution.py:18
  57.8 2.0 collective-permute-done
  61.0 1.2 fusion.47
  63.0 5.9 %collective-permute-start = (bf16[384,256]{0,1:T(8,128)(2,1)S(1)}, bf16[384,256]{0,1:T(8,128)(2,1)S(1)}, u32[]{:S(2)}, u32[]{:S(2)}) collective-permute-start(bf16[384,256]{0,1:T(8,128)(2,1)S(1)} %get-tuple-element.406), channel_id=1, source_target_pairs={{0,8},{8,16},{16,24},{24,32},{32,40},{40,48},{48,56},{56,64},{64,7... | collective-permute-start | bytes 589832 | tf_op jit(solution)/shard_map/while/body/eval_jaxpr/ppermute | solution.py:18
  69.5 2.0 collective-permute-done
  74.8 5.9 %collective-permute-start = (bf16[384,256]{0,1:T(8,128)(2,1)S(1)}, bf16[384,256]{0,1:T(8,128)(2,1)S(1)}, u32[]{:S(2)}, u32[]{:S(2)}) collective-permute-start(bf16[384,256]{0,1:T(8,128)(2,1)S(1)} %get-tuple-element.406), channel_id=1, source_target_pairs={{0,8},{8,16},{16,24},{24,32},{32,40},{40,48},{48,56},{56,64},{64,7... | collective-permute-start | bytes 589832 | tf_op jit(solution)/shard_map/while/body/eval_jaxpr/ppermute | solution.py:18
  81.3 2.0 collective-permute-done
  86.6 5.9 %collective-permute-start = (bf16[384,256]{0,1:T(8,128)(2,1)S(1)}, bf16[384,256]{0,1:T(8,128)(2,1)S(1)}, u32[]{:S(2)}, u32[]{:S(2)}) collective-permute-start(bf16[384,256]{0,1:T(8,128)(2,1)S(1)} %get-tuple-element.406), channel_id=1, source_target_pairs={{0,8},{8,16},{16,24},{24,32},{32,40},{40,48},{48,56},{56,64},{64,7... | collective-permute-start | bytes 589832 | tf_op jit(solution)/shard_map/while/body/eval_jaxpr/ppermute | solution.py:18
  93.0 2.0 collective-permute-done
  96.3 1.2 fusion.47
  98.3 5.9 %collective-permute-start = (bf16[384,256]{0,1:T(8,128)(2,1)S(1)}, bf16[384,256]{0,1:T(8,128)(2,1)S(1)}, u32[]{:S(2)}, u32[]{:S(2)}) collective-permute-start(bf16[384,256]{0,1:T(8,128)(2,1)S(1)} %get-tuple-element.406), channel_id=1, source_target_pairs={{0,8},{8,16},{16,24},{24,32},{32,40},{40,48},{48,56},{56,64},{64,7... | collective-permute-start | bytes 589832 | tf_op jit(solution)/shard_map/while/body/eval_jaxpr/ppermute | solution.py:18
  104.8 2.0 collective-permute-done
  110.1 5.9 %collective-permute-start = (bf16[384,256]{0,1:T(8,128)(2,1)S(1)}, bf16[384,256]{0,1:T(8,128)(2,1)S(1)}, u32[]{:S(2)}, u32[]{:S(2)}) collective-permute-start(bf16[384,256]{0,1:T(8,128)(2,1)S(1)} %get-tuple-element.406), channel_id=1, source_target_pairs={{0,8},{8,16},{16,24},{24,32},{32,40},{40,48},{48,56},{56,64},{64,7... | collective-permute-start | bytes 589832 | tf_op jit(solution)/shard_map/while/body/eval_jaxpr/ppermute | solution.py:18
  116.6 2.0 collective-permute-done
  119.8 1.2 fusion.47
  121.8 5.9 %collective-permute-start = (bf16[384,256]{0,1:T(8,128)(2,1)S(1)}, bf16[384,256]{0,1:T(8,128)(2,1)S(1)}, u32[]{:S(2)}, u32[]{:S(2)}) collective-permute-start(bf16[384,256]{0,1:T(8,128)(2,1)S(1)} %get-tuple-element.406), channel_id=1, source_target_pairs={{0,8},{8,16},{16,24},{24,32},{32,40},{40,48},{48,56},{56,64},{64,7... | collective-permute-start | bytes 589832 | tf_op jit(solution)/shard_map/while/body/eval_jaxpr/ppermute | solution.py:18
  128.3 2.0 collective-permute-done
  133.6 5.9 %collective-permute-start = (bf16[384,256]{0,1:T(8,128)(2,1)S(1)}, bf16[384,256]{0,1:T(8,128)(2,1)S(1)}, u32[]{:S(2)}, u32[]{:S(2)}) collective-permute-start(bf16[384,256]{0,1:T(8,128)(2,1)S(1)} %get-tuple-element.406), channel_id=1, source_target_pairs={{0,8},{8,16},{16,24},{24,32},{32,40},{40,48},{48,56},{56,64},{64,7... | collective-permute-start | bytes 589832 | tf_op jit(solution)/shard_map/while/body/eval_jaxpr/ppermute | solution.py:18
  140.1 2.0 collective-permute-done
  143.3 1.2 fusion.47
  145.4 6.4 %collective-permute-start = (bf16[384,256]{0,1:T(8,128)(2,1)S(1)}, bf16[384,256]{0,1:T(8,128)(2,1)S(1)}, u32[]{:S(2)}, u32[]{:S(2)}) collective-permute-start(bf16[384,256]{0,1:T(8,128)(2,1)S(1)} %get-tuple-element.406), channel_id=1, source_target_pairs={{0,8},{8,16},{16,24},{24,32},{32,40},{40,48},{48,56},{56,64},{64,7... | collective-permute-start | bytes 589832 | tf_op jit(solution)/shard_map/while/body/eval_jaxpr/ppermute | solution.py:18
  152.4 2.0 collective-permute-done
  155.6 1.2 fusion.47
  157.7 6.8 %collective-permute-start = (bf16[384,256]{0,1:T(8,128)(2,1)S(1)}, bf16[384,256]{0,1:T(8,128)(2,1)S(1)}, u32[]{:S(2)}, u32[]{:S(2)}) collective-permute-start(bf16[384,256]{0,1:T(8,128)(2,1)S(1)} %get-tuple-element.406), channel_id=1, source_target_pairs={{0,8},{8,16},{16,24},{24,32},{32,40},{40,48},{48,56},{56,64},{64,7... | collective-permute-start | bytes 589832 | tf_op jit(solution)/shard_map/while/body/eval_jaxpr/ppermute | solution.py:18
  165.1 2.0 collective-permute-done
  168.3 1.2 fusion.47
  170.3 6.8 %collective-permute-start = (bf16[384,256]{0,1:T(8,128)(2,1)S(1)}, bf16[384,256]{0,1:T(8,128)(2,1)S(1)}, u32[]{:S(2)}, u32[]{:S(2)}) collective-permute-start(bf16[384,256]{0,1:T(8,128)(2,1)S(1)} %get-tuple-element.406), channel_id=1, source_target_pairs={{0,8},{8,16},{16,24},{24,32},{32,40},{40,48},{48,56},{56,64},{64,7... | collective-permute-start | bytes 589832 | tf_op jit(solution)/shard_map/while/body/eval_jaxpr/ppermute | solution.py:18
  177.7 2.0 collective-permute-done
  181.0 1.2 fusion.47
  183.0 6.8 %collective-permute-start = (bf16[384,256]{0,1:T(8,128)(2,1)S(1)}, bf16[384,256]{0,1:T(8,128)(2,1)S(1)}, u32[]{:S(2)}, u32[]{:S(2)}) collective-permute-start(bf16[384,256]{0,1:T(8,128)(2,1)S(1)} %get-tuple-element.406), channel_id=1, source_target_pairs={{0,8},{8,16},{16,24},{24,32},{32,40},{40,48},{48,56},{56,64},{64,7... | collective-permute-start | bytes 589832 | tf_op jit(solution)/shard_map/while/body/eval_jaxpr/ppermute | solution.py:18
  190.4 2.0 collective-permute-done
  195.7 6.8 %collective-permute-start = (bf16[384,256]{0,1:T(8,128)(2,1)S(1)}, bf16[384,256]{0,1:T(8,128)(2,1)S(1)}, u32[]{:S(2)}, u32[]{:S(2)}) collective-permute-start(bf16[384,256]{0,1:T(8,128)(2,1)S(1)} %get-tuple-element.406), channel_id=1, source_target_pairs={{0,8},{8,16},{16,24},{24,32},{32,40},{40,48},{48,56},{56,64},{64,7... | collective-permute-start | bytes 589832 | tf_op jit(solution)/shard_map/while/body/eval_jaxpr/ppermute | solution.py:18
  203.1 2.0 collective-permute-done
  208.3 1.4 copy.35
  209.8 5.7 %convolution_convert_fusion = bf16[384,4096]{1,0:T(8,128)(2,1)} fusion(bf16[384,512]{0,1:T(8,128)(2,1)S(1)} %bitcast.110, bf16[512,4096]{1,0:T(8,128)(2,1)} %param.13), kind=kOutput, calls=%fused_computation.34 | convolution fusion | flops 1612185600 | bytes 7733248 | tf_op jit(solution)/shard_map/dot_general | solution.py:94
  215.5 112.7 %reduce-scatter.2.cloned.1.call-done = bf16[48,4096]{1,0:T(8,128)(2,1)} async-done(((bf16[384,4096]{1,0:T(8,128)(2,1)}), bf16[48,4096]{1,0:T(8,128)(2,1)}) %reduce-scatter.2.cloned.1.call-update) | async-done | bytes 393232 | tf_op jit(solution)/shard_map/reduce_scatter | solution.py:93
  (300 shorter events, 54.6 us)
Async XLA Ops:
  6.5 321.7 %reduce-scatter.2.cloned.1.call-start = ((), (), s32[]{:S(2)}) async-start(), calls=%async_computation.1 | async-start | bytes 3538944 | tf_op jit(solution)/shard_map/reduce_scatter | solution.py:93
  13.9 1.9 copy-start.2
  13.9 1.9 copy-start.3
  13.9 1.9 copy-start.4
  15.8 9.1 %collective-permute-start = (bf16[384,256]{0,1:T(8,128)(2,1)S(1)}, bf16[384,256]{0,1:T(8,128)(2,1)S(1)}, u32[]{:S(2)}, u32[]{:S(2)}) collective-permute-start(bf16[384,256]{0,1:T(8,128)(2,1)S(1)} %get-tuple-element.406), channel_id=1, source_target_pairs={{0,8},{8,16},{16,24},{24,32},{32,40},{40,48},{48,56},{56,64},{64,7... | collective-permute-start | bytes 589832 | tf_op jit(solution)/shard_map/while/body/eval_jaxpr/ppermute | solution.py:18
  24.9 1.2 copy-start
  27.3 0.9 copy-start.1
  28.2 8.0 %collective-permute-start = (bf16[384,256]{0,1:T(8,128)(2,1)S(1)}, bf16[384,256]{0,1:T(8,128)(2,1)S(1)}, u32[]{:S(2)}, u32[]{:S(2)}) collective-permute-start(bf16[384,256]{0,1:T(8,128)(2,1)S(1)} %get-tuple-element.406), channel_id=1, source_target_pairs={{0,8},{8,16},{16,24},{24,32},{32,40},{40,48},{48,56},{56,64},{64,7... | collective-permute-start | bytes 589832 | tf_op jit(solution)/shard_map/while/body/eval_jaxpr/ppermute | solution.py:18
  36.2 1.2 copy-start
  38.6 0.9 copy-start.1
  39.5 8.5 %collective-permute-start = (bf16[384,256]{0,1:T(8,128)(2,1)S(1)}, bf16[384,256]{0,1:T(8,128)(2,1)S(1)}, u32[]{:S(2)}, u32[]{:S(2)}) collective-permute-start(bf16[384,256]{0,1:T(8,128)(2,1)S(1)} %get-tuple-element.406), channel_id=1, source_target_pairs={{0,8},{8,16},{16,24},{24,32},{32,40},{40,48},{48,56},{56,64},{64,7... | collective-permute-start | bytes 589832 | tf_op jit(solution)/shard_map/while/body/eval_jaxpr/ppermute | solution.py:18
  48.0 1.2 copy-start
  50.4 0.9 copy-start.1
  51.3 8.5 %collective-permute-start = (bf16[384,256]{0,1:T(8,128)(2,1)S(1)}, bf16[384,256]{0,1:T(8,128)(2,1)S(1)}, u32[]{:S(2)}, u32[]{:S(2)}) collective-permute-start(bf16[384,256]{0,1:T(8,128)(2,1)S(1)} %get-tuple-element.406), channel_id=1, source_target_pairs={{0,8},{8,16},{16,24},{24,32},{32,40},{40,48},{48,56},{56,64},{64,7... | collective-permute-start | bytes 589832 | tf_op jit(solution)/shard_map/while/body/eval_jaxpr/ppermute | solution.py:18
  59.7 1.2 copy-start
  62.1 0.9 copy-start.1
  63.0 8.5 %collective-permute-start = (bf16[384,256]{0,1:T(8,128)(2,1)S(1)}, bf16[384,256]{0,1:T(8,128)(2,1)S(1)}, u32[]{:S(2)}, u32[]{:S(2)}) collective-permute-start(bf16[384,256]{0,1:T(8,128)(2,1)S(1)} %get-tuple-element.406), channel_id=1, source_target_pairs={{0,8},{8,16},{16,24},{24,32},{32,40},{40,48},{48,56},{56,64},{64,7... | collective-permute-start | bytes 589832 | tf_op jit(solution)/shard_map/while/body/eval_jaxpr/ppermute | solution.py:18
  71.5 1.2 copy-start
  73.9 0.9 copy-start.1
  74.8 8.5 %collective-permute-start = (bf16[384,256]{0,1:T(8,128)(2,1)S(1)}, bf16[384,256]{0,1:T(8,128)(2,1)S(1)}, u32[]{:S(2)}, u32[]{:S(2)}) collective-permute-start(bf16[384,256]{0,1:T(8,128)(2,1)S(1)} %get-tuple-element.406), channel_id=1, source_target_pairs={{0,8},{8,16},{16,24},{24,32},{32,40},{40,48},{48,56},{56,64},{64,7... | collective-permute-start | bytes 589832 | tf_op jit(solution)/shard_map/while/body/eval_jaxpr/ppermute | solution.py:18
  83.3 1.2 copy-start
  85.7 0.9 copy-start.1
  86.6 8.5 %collective-permute-start = (bf16[384,256]{0,1:T(8,128)(2,1)S(1)}, bf16[384,256]{0,1:T(8,128)(2,1)S(1)}, u32[]{:S(2)}, u32[]{:S(2)}) collective-permute-start(bf16[384,256]{0,1:T(8,128)(2,1)S(1)} %get-tuple-element.406), channel_id=1, source_target_pairs={{0,8},{8,16},{16,24},{24,32},{32,40},{40,48},{48,56},{56,64},{64,7... | collective-permute-start | bytes 589832 | tf_op jit(solution)/shard_map/while/body/eval_jaxpr/ppermute | solution.py:18
  95.0 1.2 copy-start
  97.4 0.9 copy-start.1
  98.3 8.5 %collective-permute-start = (bf16[384,256]{0,1:T(8,128)(2,1)S(1)}, bf16[384,256]{0,1:T(8,128)(2,1)S(1)}, u32[]{:S(2)}, u32[]{:S(2)}) collective-permute-start(bf16[384,256]{0,1:T(8,128)(2,1)S(1)} %get-tuple-element.406), channel_id=1, source_target_pairs={{0,8},{8,16},{16,24},{24,32},{32,40},{40,48},{48,56},{56,64},{64,7... | collective-permute-start | bytes 589832 | tf_op jit(solution)/shard_map/while/body/eval_jaxpr/ppermute | solution.py:18
  106.8 1.2 copy-start
  109.2 0.9 copy-start.1
  110.1 8.5 %collective-permute-start = (bf16[384,256]{0,1:T(8,128)(2,1)S(1)}, bf16[384,256]{0,1:T(8,128)(2,1)S(1)}, u32[]{:S(2)}, u32[]{:S(2)}) collective-permute-start(bf16[384,256]{0,1:T(8,128)(2,1)S(1)} %get-tuple-element.406), channel_id=1, source_target_pairs={{0,8},{8,16},{16,24},{24,32},{32,40},{40,48},{48,56},{56,64},{64,7... | collective-permute-start | bytes 589832 | tf_op jit(solution)/shard_map/while/body/eval_jaxpr/ppermute | solution.py:18
  118.6 1.2 copy-start
  121.0 0.9 copy-start.1
  121.8 8.5 %collective-permute-start = (bf16[384,256]{0,1:T(8,128)(2,1)S(1)}, bf16[384,256]{0,1:T(8,128)(2,1)S(1)}, u32[]{:S(2)}, u32[]{:S(2)}) collective-permute-start(bf16[384,256]{0,1:T(8,128)(2,1)S(1)} %get-tuple-element.406), channel_id=1, source_target_pairs={{0,8},{8,16},{16,24},{24,32},{32,40},{40,48},{48,56},{56,64},{64,7... | collective-permute-start | bytes 589832 | tf_op jit(solution)/shard_map/while/body/eval_jaxpr/ppermute | solution.py:18
  130.3 1.2 copy-start
  133.6 8.5 %collective-permute-start = (bf16[384,256]{0,1:T(8,128)(2,1)S(1)}, bf16[384,256]{0,1:T(8,128)(2,1)S(1)}, u32[]{:S(2)}, u32[]{:S(2)}) collective-permute-start(bf16[384,256]{0,1:T(8,128)(2,1)S(1)} %get-tuple-element.406), channel_id=1, source_target_pairs={{0,8},{8,16},{16,24},{24,32},{32,40},{40,48},{48,56},{56,64},{64,7... | collective-permute-start | bytes 589832 | tf_op jit(solution)/shard_map/while/body/eval_jaxpr/ppermute | solution.py:18
  142.1 1.2 copy-start
  145.4 9.0 %collective-permute-start = (bf16[384,256]{0,1:T(8,128)(2,1)S(1)}, bf16[384,256]{0,1:T(8,128)(2,1)S(1)}, u32[]{:S(2)}, u32[]{:S(2)}) collective-permute-start(bf16[384,256]{0,1:T(8,128)(2,1)S(1)} %get-tuple-element.406), channel_id=1, source_target_pairs={{0,8},{8,16},{16,24},{24,32},{32,40},{40,48},{48,56},{56,64},{64,7... | collective-permute-start | bytes 589832 | tf_op jit(solution)/shard_map/while/body/eval_jaxpr/ppermute | solution.py:18
  154.4 1.2 copy-start
  157.7 9.4 %collective-permute-start = (bf16[384,256]{0,1:T(8,128)(2,1)S(1)}, bf16[384,256]{0,1:T(8,128)(2,1)S(1)}, u32[]{:S(2)}, u32[]{:S(2)}) collective-permute-start(bf16[384,256]{0,1:T(8,128)(2,1)S(1)} %get-tuple-element.406), channel_id=1, source_target_pairs={{0,8},{8,16},{16,24},{24,32},{32,40},{40,48},{48,56},{56,64},{64,7... | collective-permute-start | bytes 589832 | tf_op jit(solution)/shard_map/while/body/eval_jaxpr/ppermute | solution.py:18
  167.1 1.2 copy-start
  169.5 0.9 copy-start.1
  170.3 9.4 %collective-permute-start = (bf16[384,256]{0,1:T(8,128)(2,1)S(1)}, bf16[384,256]{0,1:T(8,128)(2,1)S(1)}, u32[]{:S(2)}, u32[]{:S(2)}) collective-permute-start(bf16[384,256]{0,1:T(8,128)(2,1)S(1)} %get-tuple-element.406), channel_id=1, source_target_pairs={{0,8},{8,16},{16,24},{24,32},{32,40},{40,48},{48,56},{56,64},{64,7... | collective-permute-start | bytes 589832 | tf_op jit(solution)/shard_map/while/body/eval_jaxpr/ppermute | solution.py:18
  179.7 1.2 copy-start
  182.1 0.9 copy-start.1
  183.0 9.4 %collective-permute-start = (bf16[384,256]{0,1:T(8,128)(2,1)S(1)}, bf16[384,256]{0,1:T(8,128)(2,1)S(1)}, u32[]{:S(2)}, u32[]{:S(2)}) collective-permute-start(bf16[384,256]{0,1:T(8,128)(2,1)S(1)} %get-tuple-element.406), channel_id=1, source_target_pairs={{0,8},{8,16},{16,24},{24,32},{32,40},{40,48},{48,56},{56,64},{64,7... | collective-permute-start | bytes 589832 | tf_op jit(solution)/shard_map/while/body/eval_jaxpr/ppermute | solution.py:18
  192.4 1.2 copy-start
  194.8 0.9 copy-start.1
  195.7 9.4 %collective-permute-start = (bf16[384,256]{0,1:T(8,128)(2,1)S(1)}, bf16[384,256]{0,1:T(8,128)(2,1)S(1)}, u32[]{:S(2)}, u32[]{:S(2)}) collective-permute-start(bf16[384,256]{0,1:T(8,128)(2,1)S(1)} %get-tuple-element.406), channel_id=1, source_target_pairs={{0,8},{8,16},{16,24},{24,32},{32,40},{40,48},{48,56},{56,64},{64,7... | collective-permute-start | bytes 589832 | tf_op jit(solution)/shard_map/while/body/eval_jaxpr/ppermute | solution.py:18
  205.1 1.2 copy-start
  (4 other events, 3.5 us)
Sparse Core Ops, SparseCore 0:
  215.6 112.5 reduce-scatter.1
where the time goes:
time: 336 us; the launch traced here: 335 us
  waiting for transfers between devices  145 us (43%)
  starting transfers between devices  97.9 us (29%)
  matrix products  41 us (12%)
  local copies, waits for them, and re-layouts  21.1 us (6%)
  other arithmetic  14.7 us (4%)
  between operations  13.5 us (4%)
    reduce_scatter x1, waiting for transfers between devices, local(): lax.psum_scatter(jnp.dot(picked, out_weight, preferred_element_type=jnp.f...  113 us
    ppermute x16, starting transfers between devices, passed_along(): return lax.ppermute(block, axis, route)  97.9 us
    ppermute x16, waiting for transfers between devices, passed_along(): return lax.ppermute(block, axis, route)  32.3 us
    dot_general x17, matrix products, attend_block(): jnp.einsum('ktgs,skd->ktgd', weights, value_rows, preferred_element_type=...  20.6 us
    while x128, local copies, waits for them, and re-layouts  15.1 us
    dot_general x17, matrix products, attend_block(): jnp.einsum('tkgd,skd->ktgs', query_heads, key_rows, preferred_element_typ...  10.9 us
    reduce_sum x17, other arithmetic, attend_block(): row_total = row_total * carry_factor + jnp.sum(probs, axis=3)  9.81 us
  transfers between devices with their start and end apart: 17, of which 17 were waited for; matrix products, arithmetic and copies ran while one was open for 3% of the time, Pallas kernels for 0%

commit v1 on v0

v1 whole, which is shorter than its diff:
```python
import functools
import math

import jax
import jax.numpy as jnp
from jax import lax
from jax.experimental import pallas as pl
from jax.experimental.pallas import tpu as pltpu
from jax.sharding import PartitionSpec as P

H = 32
KVH = 8
HD = 128
SBLK = 128
SCALES = 64
GROUPS = H // KVH
PLANE = 4
NEG = -1e30
FACTOR = math.log2(math.e) / math.sqrt(HD)


def attend_kernel(
    counts, first, final, my_ref, src_ref, index_ref, table_ref, doc_ref, starts_ref, query_ref, *rest
):
    pieces, rest = rest[: len(counts)], rest[len(counts) :]
    if not first:
        (acc_in, max_in), rest = rest[:2], rest[2:]
    if final:
        out_ref, rest = rest[0], rest[1:]
    acc_ref, max_ref, bias_ref, held, sems = rest
    tok = query_ref.shape[0]
    blocks = sum(counts)
    copies = []
    at = 0
    for i, count in enumerate(counts):
        copies.append(pltpu.make_async_copy(pieces[i], held.at[pl.ds(at * tok, count * tok)], sems.at[i]))
        copies[-1].start()
        at += count
    my = my_ref[0]
    low, high = doc_ref[0], doc_ref[tok - 1]
    if first:
        acc_ref[...] = jnp.zeros_like(acc_ref)
        max_ref[...] = jnp.full(max_ref.shape, NEG, jnp.float32)
    else:
        acc_ref[...] = acc_in[...]
        max_ref[...] = max_in[...]
    for copy in copies:
        copy.wait()

    def attend_block(step, masked):
        src = src_ref[step]
        base = src * (tok // SBLK)
        key_scales, value_scales = [], []
        for t in range(tok // SBLK):
            row = index_ref[base + t]
            key_scales.append(jnp.full((1, SBLK), table_ref[2 * row] * FACTOR, jnp.float32))
            value_scales.append(jnp.full((SBLK, HD), table_ref[2 * row + 1], jnp.float32))
        scale = jnp.concatenate(key_scales, 1)
        kv_rows = pl.ds(pl.multiple_of(step * tok, tok), tok)
        keys = held[kv_rows, :HD]
        values = held[kv_rows, HD:].astype(jnp.float32) * jnp.concatenate(value_scales, 0)
        values = jnp.concatenate([values.astype(jnp.bfloat16), jnp.ones((tok, HD), jnp.bfloat16)], 1)
        if masked:
            key_pos = src * tok + lax.broadcasted_iota(jnp.int32, (tok, tok), 1)
            query_pos = my * tok + lax.broadcasted_iota(jnp.int32, (tok, tok), 0)
            starts = jnp.concatenate([starts_ref[...]] * (tok // HD), 1)
            bias_ref[...] = jnp.where((key_pos >= starts) & (key_pos <= query_pos), 0.0, NEG)
        for h in range(GROUPS):
            rows = pl.ds(h * tok, tok)
            scores = lax.dot_general(
                query_ref[:, h * HD : (h + 1) * HD],
                keys,
                (((1,), (1,)), ((), ())),
                preferred_element_type=jnp.float32,
            )
            scores = scores * scale
            if masked:
                scores = scores + bias_ref[...]
            old_max = max_ref[rows, :]
            new_max = jnp.maximum(old_max, jnp.max(scores, axis=1, keepdims=True))
            carry = jnp.exp2(old_max - new_max)
            max_ref[rows, :] = new_max
            probs = jnp.exp2(scores - jnp.concatenate([new_max] * (tok // HD), 1)).astype(jnp.bfloat16)
            mixed = jnp.dot(probs, values, preferred_element_type=jnp.float32)
            acc_ref[rows, :] = acc_ref[rows, :] * jnp.concatenate([carry, carry], 1) + mixed

    def one_step(step, _):
        src = src_ref[step]
        visible = (src >= 0) & (src * tok + tok - 1 >= low) & (src <= my)
        partial = (src == my) | (src * tok < high)

        @pl.when(visible & partial)
        def _():
            attend_block(step, True)

        @pl.when(visible & jnp.logical_not(partial))
        def _():
            attend_block(step, False)

        return 0

    lax.fori_loop(0, blocks, one_step, 0)
    if final:
        for h in range(GROUPS):
            acc = acc_ref[pl.ds(h * tok, tok), :]
            out_ref[:, h * HD : (h + 1) * HD] = (acc[:, :HD] / acc[:, HD:]).astype(jnp.bfloat16)


def attend(my, src, common, pieces, state=None, final=False):
    query = common[-1]
    tok = query.shape[0]
    counts = tuple(piece.shape[0] // tok for piece in pieces)
    vmem, smem = pl.BlockSpec(memory_space=pltpu.VMEM), pl.BlockSpec(memory_space=pltpu.SMEM)
    state_shape = (
        jax.ShapeDtypeStruct((GROUPS * tok, 2 * HD), jnp.float32),
        jax.ShapeDtypeStruct((GROUPS * tok, HD), jnp.float32),
    )
    scratch = [
        pltpu.VMEM((tok, tok), jnp.float32),
        pltpu.VMEM((sum(counts) * tok, 2 * HD), jnp.bfloat16),
        pltpu.SemaphoreType.DMA((len(counts),)),
    ]
    if final:
        out_shape, out_specs = jax.ShapeDtypeStruct((tok, GROUPS * HD), jnp.bfloat16), vmem
        scratch = [pltpu.VMEM(s.shape, s.dtype) for s in state_shape] + scratch
    else:
        out_shape, out_specs = state_shape, (vmem, vmem)
    flops = sum(counts) * GROUPS * tok * tok * HD * 4
    return pl.pallas_call(
        functools.partial(attend_kernel, counts, state is None, final),
        out_shape=out_shape,
        in_specs=[smem] * 5
        + [vmem] * 2
        + [pl.BlockSpec(memory_space=pl.ANY)] * len(pieces)
        + [vmem] * (0 if state is None else 2),
        out_specs=out_specs,
        scratch_shapes=scratch,
        compiler_params=pltpu.CompilerParams(vmem_limit_bytes=40 << 20),
        cost_estimate=pl.CostEstimate(flops=3 * flops, bytes_accessed=4 << 20, transcendentals=0),
    )(my, src, *common, *pieces, *(state or ()))


def local(query, keys_values, doc_start, scale_index, scale_table, out_weight):
    tok = query.shape[0]
    ctx_count = lax.axis_size("ctx")
    my = lax.axis_index("ctx").astype(jnp.int32)
    plane = my // PLANE
    groups = [[PLANE * i + j for j in range(PLANE)] for i in range(ctx_count // PLANE)]
    starts = jnp.broadcast_to(doc_start[:, None], (tok, HD))
    common = (scale_index, scale_table.reshape(-1), doc_start, starts, query)

    def forward(block):
        return lax.ppermute(block, "ctx", [(i, i + PLANE) for i in range(ctx_count - PLANE)])

    def gathered(block):
        return lax.all_gather(block, "ctx", axis_index_groups=groups, tiled=True)

    def sources(*back):
        src = jnp.concatenate([(plane - k) * PLANE + jnp.arange(PLANE, dtype=jnp.int32) for k in back])
        return jnp.where(src == my, -1, src)

    moving = keys_values
    planes = [gathered(moving)]
    for _ in range(PLANE):
        moving = forward(moving)
        planes.append(gathered(moving))
    state = attend(my[None], my[None], common, [keys_values])
    state = attend(my[None], sources(0, 1), common, planes[0:2], state)
    state = attend(my[None], sources(2, 3), common, planes[2:4], state)
    attn = attend(my[None], sources(4), common, planes[4:5], state, True)
    shares = lax.axis_size("kvh")
    partial = jnp.dot(attn, out_weight, preferred_element_type=jnp.float32).astype(jnp.bfloat16)
    pieces = lax.all_to_all(partial.reshape(shares, tok // shares, -1), "kvh", 0, 0)
    return jnp.sum(pieces.astype(jnp.float32), axis=0).astype(jnp.bfloat16)


def solution(mesh):
    placed = (P("ctx", "kvh"), P("ctx", "kvh"), P("ctx"), P(), P(None, "kvh"), P("kvh", None))
    return jax.shard_map(
        local, mesh=mesh, in_specs=placed, out_specs=P(("ctx", "kvh"), None), check_vma=False
    )
```

time: 336 us -> 144 us (0.43)
  the two profiles are of different devices: /device:TPU:1 before, /device:TPU:196 now
where the time goes in v1:
time: 144 us
  blocking collectives  94.1 us (65%)
  Pallas kernels  25.1 us (17%)
  starting transfers between devices  15 us (10%)
  local copies, waits for them, and re-layouts  6.15 us (4%)
  matrix products  1.79 us (1%)
  other arithmetic  1.49 us (1%)
    all_gather x5, blocking collectives, gathered(): return lax.all_gather(block, 'ctx', axis_index_groups=groups, tiled=True)  50.6 us
    all_to_all x1, blocking collectives, local(): lax.all_to_all(partial.reshape(shares, tok // shares, -1), 'kvh', 0, 0)  43.5 us
    pallas_call x4, Pallas kernels, attend(): pl.pallas_call(functools.partial(attend_kernel, counts, state is None, fi...  25.1 us
    ppermute x4, starting transfers between devices, forward(): lax.ppermute(block, 'ctx', [(i, i + PLANE) for i in range(ctx_count - PLA...  15 us
    unnamed x11, local copies, waits for them, and re-layouts  5.23 us
  transfers between devices with their start and end apart: 4, of which 0 were waited for; matrix products, arithmetic and copies ran while one was open for 1% of the time, Pallas kernels for 17%

profile of v1, /device:TPU:196, one launch (start us, length us, event | category | flops | bytes accessed | tf_op | source)
XLA Modules:
  0.0 143.8 jit_solution(16849295254566674145)
XLA Ops:
  0.0 3.8 %collective-permute-start = (bf16[384,256]{1,0:T(8,128)(2,1)}, bf16[384,256]{1,0:T(8,128)(2,1)S(1)}, u32[]{:S(2)}, u32[]{:S(2)}) collective-permute-start(bf16[384,256]{1,0:T(8,128)(2,1)} %rest_0_.1), channel_id=1, source_target_pairs={{0,32},{8,40},{16,48},{24,56},{32,64},{40,72},{48,80},{56,88},{64,... | collective-permute-start | bytes 589832 | tf_op jit(solution)/shard_map/ppermute | solution.py:153
  3.8 9.6 %all_gather.18.rest_0_ = bf16[1536,256]{1,0:T(8,128)(2,1)S(1)} all-gather(bf16[384,256]{1,0:T(8,128)(2,1)} %rest_0_.1), channel_id=1, replica_groups={{0,8,16,24},{32,40,48,56},{64,72,80,88},{96,104,112,120},{128,136,144,1..., dimensions={0}, use_global_device_ids=true | all-gather | bytes 983040 | tf_op jit(solution)/shard_map/all_gather | solution.py:156
  13.5 0.8 copy.8
  14.2 0.1 reshape.7.table_ref
  14.4 0.1 compare_select_fusion.src_ref
  14.5 0.8 broadcast_in_dim.24.starts_ref
  15.3 0.0 copy-start
  15.3 0.9 copy-done
  16.2 0.0 copy-start.1
  16.2 0.7 copy-done.1
  16.9 0.0 copy-start.2
  16.9 1.0 copy-done.2
  17.9 0.0 copy-start.3
  17.9 0.7 copy-done.3
  18.6 2.4 %shard_map.64 = (f32[1536,256]{1,0:T(8,128)S(1)}, f32[1536,128]{1,0:T(8,128)S(1)}) custom-call(s32[1]{0:T(128)} %bitcast.my_ref.src_ref, s32[1]{0:T(128)} %bitcast.my_ref.src_ref, s32[192]{0:T(256)S(1)} %copy-done.3, f32[128]{0:T(128)S(1)} %reshape.7.table_ref, s32[384]{0:T(512)S(1)} %copy-done.1, s32[384,128]{1,0:T(8,128)S(1)} %broadcast_in_dim.24.starts_ref, ...), custom_call_target="tpu_custom_call" | custom-call | flops 905969664 | bytes 4194304 | tf_op jit(solution)/shard_map/pallas_call | solution.py:129
  21.0 0.1 compare_select_fusion.1.src_ref
  21.1 0.0 collective-permute-done
  21.1 10.2 %all_gather.19.rest_1_ = bf16[1536,256]{1,0:T(8,128)(2,1)S(1)} all-gather(bf16[384,256]{1,0:T(8,128)(2,1)S(1)} %collective-permute-done), channel_id=1, replica_groups={{0,8,16,24},{32,40,48,56},{64,72,80,88},{96,104,112,120},{128,136,144,1..., dimensions={0}, use_global_device_ids=true | all-gather | bytes 983040 | tf_op jit(solution)/shard_map/all_gather | solution.py:156
  31.3 5.0 %collective-permute-start.1 = (bf16[384,256]{1,0:T(8,128)(2,1)S(1)}, bf16[384,256]{1,0:T(8,128)(2,1)S(1)}, u32[]{:S(2)}, u32[]{:S(2)}) collective-permute-start(bf16[384,256]{1,0:T(8,128)(2,1)S(1)} %collective-permute-done), channel_id=1, source_target_pairs={{0,32},{8,40},{16,48},{24,56},{32,64},{40,72},{48,80},{56,88},{64,... | collective-permute-start | bytes 589832 | tf_op jit(solution)/shard_map/ppermute | solution.py:153
  36.3 9.4 %shard_map.65 = (f32[1536,256]{1,0:T(8,128)S(1)}, f32[1536,128]{1,0:T(8,128)S(1)}) custom-call(s32[1]{0:T(128)} %bitcast.my_ref.src_ref, s32[8]{0:T(128)S(1)} %compare_select_fusion.src_ref, s32[192]{0:T(256)S(1)} %copy-done.3, f32[128]{0:T(128)S(1)} %reshape.7.table_ref, s32[384]{0:T(512)S(1)} %copy-done.1, s32[384,128]{1,0:T(8,128)S(1)} %broadcast_in_dim.24.starts_ref, ...), custom_call_target="tpu_custom_call" | custom-call | flops 7247757312 | bytes 4194304 | tf_op jit(solution)/shard_map/pallas_call | solution.py:129
  45.7 0.0 collective-permute-done.1
  45.7 1.9 %collective-permute-start.2 = (bf16[384,256]{1,0:T(8,128)(2,1)S(1)}, bf16[384,256]{1,0:T(8,128)(2,1)S(1)}, u32[]{:S(2)}, u32[]{:S(2)}) collective-permute-start(bf16[384,256]{1,0:T(8,128)(2,1)S(1)} %collective-permute-done.1), channel_id=1, source_target_pairs={{0,32},{8,40},{16,48},{24,56},{32,64},{40,72},{48,80},{56,88},{64,... | collective-permute-start | bytes 589832 | tf_op jit(solution)/shard_map/ppermute | solution.py:153
  47.7 10.5 %all_gather.16.rest_0_ = bf16[1536,256]{1,0:T(8,128)(2,1)S(1)} all-gather(bf16[384,256]{1,0:T(8,128)(2,1)S(1)} %collective-permute-done.1), channel_id=1, replica_groups={{0,8,16,24},{32,40,48,56},{64,72,80,88},{96,104,112,120},{128,136,144,1..., dimensions={0}, use_global_device_ids=true | all-gather | bytes 983040 | tf_op jit(solution)/shard_map/all_gather | solution.py:156
  58.2 0.0 collective-permute-done.2
  58.2 10.1 %all_gather.17.rest_1_ = bf16[1536,256]{1,0:T(8,128)(2,1)S(1)} all-gather(bf16[384,256]{1,0:T(8,128)(2,1)S(1)} %collective-permute-done.2), channel_id=1, replica_groups={{0,8,16,24},{32,40,48,56},{64,72,80,88},{96,104,112,120},{128,136,144,1..., dimensions={0}, use_global_device_ids=true | all-gather | bytes 983040 | tf_op jit(solution)/shard_map/all_gather | solution.py:156
  68.3 4.2 %collective-permute-start.3 = (bf16[384,256]{1,0:T(8,128)(2,1)S(1)}, bf16[384,256]{1,0:T(8,128)(2,1)S(1)}, u32[]{:S(2)}, u32[]{:S(2)}) collective-permute-start(bf16[384,256]{1,0:T(8,128)(2,1)S(1)} %collective-permute-done.2), channel_id=1, source_target_pairs={{0,32},{8,40},{16,48},{24,56},{32,64},{40,72},{48,80},{56,88},{64,... | collective-permute-start | bytes 589832 | tf_op jit(solution)/shard_map/ppermute | solution.py:153
  72.5 12.3 %shard_map.66 = (f32[1536,256]{1,0:T(8,128)S(1)}, f32[1536,128]{1,0:T(8,128)S(1)}) custom-call(s32[1]{0:T(128)} %bitcast.my_ref.src_ref, s32[8]{0:T(128)S(1)} %compare_select_fusion.1.src_ref, s32[192]{0:T(256)S(1)} %copy-done.3, f32[128]{0:T(128)S(1)} %reshape.7.table_ref, s32[384]{0:T(512)S(1)} %copy-done.1, s32[384,128]{1,0:T(8,128)S(1)} %broadcast_in_dim.24.starts_ref, ...), custom_call_target="tpu_custom_call" | custom-call | flops 7247757312 | bytes 4194304 | tf_op jit(solution)/shard_map/pallas_call | solution.py:129
  84.8 0.0 collective-permute-done.3
  84.8 10.2 %all_gather.15.rest_0_ = bf16[1536,256]{1,0:T(8,128)(2,1)S(1)} all-gather(bf16[384,256]{1,0:T(8,128)(2,1)S(1)} %collective-permute-done.3), channel_id=1, replica_groups={{0,8,16,24},{32,40,48,56},{64,72,80,88},{96,104,112,120},{128,136,144,1..., dimensions={0}, use_global_device_ids=true | all-gather | bytes 983040 | tf_op jit(solution)/shard_map/all_gather | solution.py:156
  95.0 0.0 copy-start.4
  95.0 1.0 shard_map.67
  96.0 1.2 copy-done.4
  97.2 1.8 %convolution_convert_fusion = bf16[384,4096]{1,0:T(8,128)(2,1)S(1)} fusion(bf16[384,512]{1,0:T(8,128)(2,1)S(1)} %shard_map.67, bf16[512,4096]{1,0:T(8,128)(2,1)S(1)} %copy-done.4), kind=kOutput, calls=%fused_computation | convolution fusion | flops 1612185600 | bytes 7733248 | tf_op jit(solution)/shard_map/dot_general | solution.py:172
  99.0 43.5 %all_to_all.5 = bf16[8,48,4096]{2,1,0:T(8,128)(2,1)S(1)} all-to-all(bf16[8,48,4096]{2,1,0:T(8,128)(2,1)S(1)} %bitcast.4), channel_id=1, replica_groups=mesh['ctx'=64,'kvh'=8] {'kvh'}, dimensions={0} | all-to-all | bytes 6291456 | tf_op jit(solution)/shard_map/all_to_all | solution.py:173
  142.4 1.3 reduce_sum.12
  (3 shorter events, 0.0 us)
Async XLA Ops:
  0.0 21.1 %collective-permute-start = (bf16[384,256]{1,0:T(8,128)(2,1)}, bf16[384,256]{1,0:T(8,128)(2,1)S(1)}, u32[]{:S(2)}, u32[]{:S(2)}) collective-permute-start(bf16[384,256]{1,0:T(8,128)(2,1)} %rest_0_.1), channel_id=1, source_target_pairs={{0,32},{8,40},{16,48},{24,56},{32,64},{40,72},{48,80},{56,88},{64,... | collective-permute-start | bytes 589832 | tf_op jit(solution)/shard_map/ppermute | solution.py:153
  15.3 0.9 copy-start
  16.2 0.7 copy-start.1
  16.9 1.0 copy-start.2
  17.9 0.7 copy-start.3
  31.3 14.5 %collective-permute-start.1 = (bf16[384,256]{1,0:T(8,128)(2,1)S(1)}, bf16[384,256]{1,0:T(8,128)(2,1)S(1)}, u32[]{:S(2)}, u32[]{:S(2)}) collective-permute-start(bf16[384,256]{1,0:T(8,128)(2,1)S(1)} %collective-permute-done), channel_id=1, source_target_pairs={{0,32},{8,40},{16,48},{24,56},{32,64},{40,72},{48,80},{56,88},{64,... | collective-permute-start | bytes 589832 | tf_op jit(solution)/shard_map/ppermute | solution.py:153
  45.7 12.4 %collective-permute-start.2 = (bf16[384,256]{1,0:T(8,128)(2,1)S(1)}, bf16[384,256]{1,0:T(8,128)(2,1)S(1)}, u32[]{:S(2)}, u32[]{:S(2)}) collective-permute-start(bf16[384,256]{1,0:T(8,128)(2,1)S(1)} %collective-permute-done.1), channel_id=1, source_target_pairs={{0,32},{8,40},{16,48},{24,56},{32,64},{40,72},{48,80},{56,88},{64,... | collective-permute-start | bytes 589832 | tf_op jit(solution)/shard_map/ppermute | solution.py:153
  68.3 16.5 %collective-permute-start.3 = (bf16[384,256]{1,0:T(8,128)(2,1)S(1)}, bf16[384,256]{1,0:T(8,128)(2,1)S(1)}, u32[]{:S(2)}, u32[]{:S(2)}) collective-permute-start(bf16[384,256]{1,0:T(8,128)(2,1)S(1)} %collective-permute-done.2), channel_id=1, source_target_pairs={{0,32},{8,40},{16,48},{24,56},{32,64},{40,72},{48,80},{56,88},{64,... | collective-permute-start | bytes 589832 | tf_op jit(solution)/shard_map/ppermute | solution.py:153
  95.0 2.2 %copy-start.4 = (bf16[512,4096]{1,0:T(8,128)(2,1)S(1)}, bf16[512,4096]{1,0:T(8,128)(2,1)}, u32[]{:S(2)}) copy-start(bf16[512,4096]{1,0:T(8,128)(2,1)} %param.11) | copy-start | bytes 12582916

commit v2 on v1

v2 whole, which is shorter than its diff:
```python
import functools
import math

import jax
import jax.numpy as jnp
from jax import lax
from jax.experimental import pallas as pl
from jax.experimental.pallas import tpu as pltpu
from jax.sharding import PartitionSpec as P

H = 32
KVH = 8
HD = 128
SBLK = 128
SCALES = 64
GROUPS = H // KVH
PLANE = 4
NEG = -1e30
FACTOR = math.log2(math.e) / math.sqrt(HD)


def attend_kernel(
    counts, groups, first, final, index_ref, table_ref, starts_ref, query_ref, *rest
):
    pieces, rest = rest[: len(counts)], rest[len(counts) :]
    if not first:
        (acc_in, max_in), rest = rest[:2], rest[2:]
    if final:
        out_ref, rest = rest[0], rest[1:]
    acc_ref, max_ref, bias_ref, held, sems = rest
    tok = query_ref.shape[0]
    copies = []
    at = 0
    for i, count in enumerate(counts):
        copies.append(pltpu.make_async_copy(pieces[i], held.at[pl.ds(at * tok, count * tok)], sems.at[i]))
        copies[-1].start()
        at += count
    low, high, my = [index_ref[index_ref.shape[0] - 3 + i] for i in range(3)]
    if first:
        acc_ref[...] = jnp.zeros_like(acc_ref)
        max_ref[...] = jnp.full(max_ref.shape, NEG, jnp.float32)
    else:
        acc_ref[...] = acc_in[...]
        max_ref[...] = max_in[...]
    for copy in copies:
        copy.wait()

    def attend_blocks(step, src, count, masked):
        key_scales, value_scales = [], []
        for t in range(count * tok // SBLK):
            row = index_ref[(src - 2 * (t // (tok // SBLK))) * (tok // SBLK) + t % (tok // SBLK)]
            key_scales.append(jnp.full((1, SBLK), table_ref[2 * row] * FACTOR, jnp.float32))
            value_scales.append(jnp.full((SBLK, HD), table_ref[2 * row + 1], jnp.float32))
        scale = jnp.concatenate(key_scales, 1)
        width = count * tok
        kv_rows = pl.ds(pl.multiple_of(step * tok, tok), width)
        keys = held[kv_rows, :HD]
        values = held[kv_rows, HD:].astype(jnp.float32) * jnp.concatenate(value_scales, 0)
        values = jnp.concatenate([values.astype(jnp.bfloat16), jnp.ones((width, HD), jnp.bfloat16)], 1)
        if masked:
            key_pos = src * tok + lax.broadcasted_iota(jnp.int32, (tok, tok), 1)
            query_pos = my * tok + lax.broadcasted_iota(jnp.int32, (tok, tok), 0)
            starts = jnp.concatenate([starts_ref[...]] * (tok // HD), 1)
            bias_ref[...] = jnp.where((key_pos >= starts) & (key_pos <= query_pos), 0.0, NEG)
        for h in range(GROUPS):
            rows = pl.ds(h * tok, tok)
            scores = lax.dot_general(
                query_ref[:, h * HD : (h + 1) * HD],
                keys,
                (((1,), (1,)), ((), ())),
                preferred_element_type=jnp.float32,
            )
            scores = scores * scale
            if masked:
                scores = scores + bias_ref[...]
            old_max = max_ref[rows, :]
            new_max = jnp.maximum(old_max, jnp.max(scores, axis=1, keepdims=True))
            carry = jnp.exp2(old_max - new_max)
            max_ref[rows, :] = new_max
            probs = jnp.exp2(scores - jnp.concatenate([new_max] * (width // HD), 1)).astype(jnp.bfloat16)
            mixed = jnp.dot(probs, values, preferred_element_type=jnp.float32)
            acc_ref[rows, :] = acc_ref[rows, :] * jnp.concatenate([carry, carry], 1) + mixed

    def one_block(step, src):
        @pl.when((src >= 0) & (src * tok + tok - 1 >= low) & (src <= my))
        def _():
            attend_blocks(step, src, 1, True)

    at = 0
    for count, mine, back in groups:
        newest = (my if mine else my ^ 1) - back
        if count == 1:
            one_block(at, newest)
        else:
            oldest = newest - 2 * (count - 1)
            whole = (oldest >= 0) & (oldest * tok >= high) & (newest < my)

            @pl.when(whole)
            def _(at=at, newest=newest, count=count):
                attend_blocks(at, newest, count, False)

            @pl.when(jnp.logical_not(whole))
            def _(at=at, newest=newest, count=count):
                def one_step(step, _):
                    one_block(at + step, newest - 2 * step)
                    return 0

                lax.fori_loop(0, count, one_step, 0)

        at += count
    if final:
        for h in range(GROUPS):
            acc = acc_ref[pl.ds(h * tok, tok), :]
            out_ref[:, h * HD : (h + 1) * HD] = (acc[:, :HD] / acc[:, HD:]).astype(jnp.bfloat16)


def attend(common, pieces, groups, state=None, final=False):
    query = common[-1]
    tok = query.shape[0]
    counts = tuple(piece.shape[0] // tok for piece in pieces)
    vmem, smem = pl.BlockSpec(memory_space=pltpu.VMEM), pl.BlockSpec(memory_space=pltpu.SMEM)
    state_shape = (
        jax.ShapeDtypeStruct((GROUPS * tok, 2 * HD), jnp.float32),
        jax.ShapeDtypeStruct((GROUPS * tok, HD), jnp.float32),
    )
    scratch = [
        pltpu.VMEM((tok, tok), jnp.float32),
        pltpu.VMEM((sum(counts) * tok, 2 * HD), jnp.bfloat16),
        pltpu.SemaphoreType.DMA((len(counts),)),
    ]
    if final:
        out_shape, out_specs = jax.ShapeDtypeStruct((tok, GROUPS * HD), jnp.bfloat16), vmem
        scratch = [pltpu.VMEM(s.shape, s.dtype) for s in state_shape] + scratch
    else:
        out_shape, out_specs = state_shape, (vmem, vmem)
    flops = sum(counts) * GROUPS * tok * tok * HD * 4
    return pl.pallas_call(
        functools.partial(attend_kernel, counts, groups, state is None, final),
        out_shape=out_shape,
        in_specs=[smem] * 2
        + [vmem] * 2
        + [pl.BlockSpec(memory_space=pl.ANY)] * len(pieces)
        + [vmem] * (0 if state is None else 2),
        out_specs=out_specs,
        scratch_shapes=scratch,
        compiler_params=pltpu.CompilerParams(vmem_limit_bytes=40 << 20),
        cost_estimate=pl.CostEstimate(flops=10 * flops, bytes_accessed=4 << 20, transcendentals=0),
    )(*common, *pieces, *(state or ()))


def local(query, keys_values, doc_start, scale_index, scale_table, out_weight):
    tok = query.shape[0]
    ctx_count = lax.axis_size("ctx")
    my = lax.axis_index("ctx").astype(jnp.int32)
    starts = jnp.broadcast_to(doc_start[:, None], (tok, HD))
    places = jnp.concatenate([scale_index, doc_start[:1], doc_start[-1:], my[None]])
    common = (places, scale_table.reshape(-1), starts, query)

    def shifted(block, distance):
        return lax.ppermute(block, "ctx", [(i, i + distance) for i in range(ctx_count - distance)])

    def swapped(*blocks):
        return lax.ppermute(jnp.concatenate(blocks), "ctx", [(i, i ^ 1) for i in range(ctx_count)])

    def after(block, *others):
        return lax.optimization_barrier((block, *others))[0]

    even, odd = [keys_values], []
    odd.append(shifted(even[0], 2))
    even.append(shifted(even[0], 4))
    state = attend(common, [even[0]], ((1, True, 0),))
    odd.append(shifted(even[1], 2))
    even.append(shifted(even[1], 4))
    state = attend(common, [odd[0], even[1]], ((2, True, 2),), state)
    odd.append(shifted(even[2], 2))
    even.append(shifted(even[2], 4))
    first_swap = swapped(even[0], odd[0], even[1], after(odd[1], even[2]))
    state = attend(common, [odd[1], even[2]], ((2, True, 6),), state)
    odd.append(shifted(even[3], 2))
    even.append(shifted(even[3], 4))
    groups = ((1, False, 0), (3, False, 2), (2, True, 10))
    state = attend(common, [first_swap, odd[2], even[3]], groups, state)
    second_swap = swapped(even[2], odd[2], even[3], after(odd[3], *state), even[4])
    state = attend(common, [odd[3], even[4]], ((2, True, 14),), state)
    attn = attend(common, [second_swap], ((4, False, 8), (1, False, 16)), state, True)
    shares = lax.axis_size("kvh")
    partial = jnp.dot(attn, out_weight, preferred_element_type=jnp.float32).astype(jnp.bfloat16)
    pieces = lax.all_to_all(partial.reshape(shares, tok // shares, -1), "kvh", 0, 0)
    return jnp.sum(pieces.astype(jnp.float32), axis=0).astype(jnp.bfloat16)


def solution(mesh):
    placed = (P("ctx", "kvh"), P("ctx", "kvh"), P("ctx"), P(), P(None, "kvh"), P("kvh", None))
    return jax.shard_map(
        local, mesh=mesh, in_specs=placed, out_specs=P(("ctx", "kvh"), None), check_vma=False
    )
```

time: 144 us -> 121 us (0.84)
  the two profiles are of different devices: /device:TPU:196 before, /device:TPU:193 now
where the time goes in v2:
time: 121 us
  blocking collectives  42.1 us (35%)
  starting transfers between devices  33.4 us (28%)
  Pallas kernels  32.1 us (27%)
  local copies, waits for them, and re-layouts  5.12 us (4%)
  other arithmetic  3.51 us (3%)
  waiting for transfers between devices  2.4 us (2%)
  matrix products  1.88 us (2%)
    all_to_all x1, blocking collectives, local(): lax.all_to_all(partial.reshape(shares, tok // shares, -1), 'kvh', 0, 0)  42.1 us
    pallas_call x6, Pallas kernels, attend(): pl.pallas_call(functools.partial(attend_kernel, counts, groups, state is...  32.1 us
    ppermute x8, starting transfers between devices, shifted(): lax.ppermute(block, 'ctx', [(i, i + distance) for i in range(ctx_count -...  27.1 us
    ppermute x2, starting transfers between devices, swapped(): lax.ppermute(jnp.concatenate(blocks), 'ctx', [(i, i ^ 1) for i in range(c...  6.26 us
    unnamed x15, local copies, waits for them, and re-layouts  2.76 us
  transfers between devices with their start and end apart: 10, of which 1 were waited for; matrix products, arithmetic and copies ran while one was open for 4% of the time, Pallas kernels for 21%

profile of v2, /device:TPU:193, one launch (start us, length us, event | category | flops | bytes accessed | tf_op | source)
XLA Modules:
  0.0 120.7 jit_solution(17417999567236065904)
XLA Ops:
  0.0 3.5 %collective-permute-start = (bf16[384,256]{1,0:T(8,128)(2,1)}, bf16[384,256]{1,0:T(8,128)(2,1)S(1)}, u32[]{:S(2)}, u32[]{:S(2)}) collective-permute-start(bf16[384,256]{1,0:T(8,128)(2,1)} %rest_0_.1), channel_id=1, source_target_pairs={{0,32},{8,40},{16,48},{24,56},{32,64},{40,72},{48,80},{56,88},{64,... | collective-permute-start | bytes 589832 | tf_op jit(solution)/shard_map/ppermute | solution.py:160
  3.5 4.7 %collective-permute-start.5 = (bf16[384,256]{1,0:T(8,128)(2,1)}, bf16[384,256]{1,0:T(8,128)(2,1)S(1)}, u32[]{:S(2)}, u32[]{:S(2)}) collective-permute-start(bf16[384,256]{1,0:T(8,128)(2,1)} %rest_0_.1), channel_id=1, source_target_pairs={{0,16},{8,24},{16,32},{24,40},{32,48},{40,56},{48,64},{56,72},{64,... | collective-permute-start | bytes 589832 | tf_op jit(solution)/shard_map/ppermute | solution.py:160
  8.2 1.4 %fusion = (s32[1]{0:T(128)}, s32[1]{0:T(128)}) fusion(s32[384]{0:T(512)} %param.8), kind=kLoop, calls=%fused_computation.8 | loop fusion | bytes 16 | tf_op jit(solution)/shard_map/slice | solution.py:156
  9.6 0.8 copy.8
  10.4 0.1 reshape.7.table_ref
  10.5 2.1 %pad_add_fusion.index_ref = s32[195]{0:T(256)S(1)} fusion(s32[1]{0:T(128)} %bitcast, s32[1]{0:T(128)} %get-tuple-element.30, s32[1]{0:T(128)} %get-tuple-element.29, s32[192]{0:T(256)} %param.9), kind=kLoop, calls=%fused_computation.7 | loop fusion | flops 585 | bytes 1560 | tf_op jit(solution)/shard_map/concatenate | solution.py:156
  12.7 0.8 broadcast_in_dim.10.starts_ref
  13.5 0.0 copy-start
  13.5 0.9 copy-done
  14.4 0.0 copy-start.2
  14.4 1.0 copy-done.2
  15.4 0.0 copy-start.3
  15.4 2.4 %shard_map.64 = (f32[1536,256]{1,0:T(8,128)S(1)}, f32[1536,128]{1,0:T(8,128)S(1)}) custom-call(s32[195]{0:T(256)S(1)} %pad_add_fusion.index_ref, f32[128]{0:T(128)S(1)} %reshape.7.table_ref, s32[384,128]{1,0:T(8,128)S(1)} %broadcast_in_dim.10.starts_ref, bf16[384,512]{1,0:T(8,128)(2,1)S(1)} %copy-done.2, bf16[384,256]{1,0:T(8,128)(2,1)S(1)} %copy-done), custom_call_target="tpu_custom_call" | custom-call | flops 3019898880 | bytes 4194304 | tf_op jit(solution)/shard_map/pallas_call | solution.py:137
  17.8 0.0 collective-permute-done.rest_1_
  17.8 4.8 %collective-permute-start.1 = (bf16[384,256]{1,0:T(8,128)(2,1)S(1)}, bf16[384,256]{1,0:T(8,128)(2,1)S(1)}, u32[]{:S(2)}, u32[]{:S(2)}) collective-permute-start(bf16[384,256]{1,0:T(8,128)(2,1)S(1)} %collective-permute-done.rest_1_), channel_id=1, source_target_pairs={{0,32},{8,40},{16,48},{24,56},{32,64},{40,72},{48,80},{56,88},{64,... | collective-permute-start | bytes 589832 | tf_op jit(solution)/shard_map/ppermute | solution.py:160
  22.6 2.6 %collective-permute-start.6 = (bf16[384,256]{1,0:T(8,128)(2,1)S(1)}, bf16[384,256]{1,0:T(8,128)(2,1)S(1)}, u32[]{:S(2)}, u32[]{:S(2)}) collective-permute-start(bf16[384,256]{1,0:T(8,128)(2,1)S(1)} %collective-permute-done.rest_1_), channel_id=1, source_target_pairs={{0,16},{8,24},{16,32},{24,40},{32,48},{40,56},{48,64},{56,72},{64,... | collective-permute-start | bytes 589832 | tf_op jit(solution)/shard_map/ppermute | solution.py:160
  25.2 0.0 collective-permute-done.5.rest_0_
  25.2 0.0 copy-done.3
  25.2 0.0 copy-start.1
  25.2 4.2 %shard_map.65 = (f32[1536,256]{1,0:T(8,128)S(1)}, f32[1536,128]{1,0:T(8,128)S(1)}) custom-call(s32[195]{0:T(256)S(1)} %pad_add_fusion.index_ref, f32[128]{0:T(128)S(1)} %reshape.7.table_ref, s32[384,128]{1,0:T(8,128)S(1)} %broadcast_in_dim.10.starts_ref, bf16[384,512]{1,0:T(8,128)(2,1)S(1)} %copy-done.3, ...), custom_call_target="tpu_custom_call" | custom-call | flops 6039797760 | bytes 4194304 | tf_op jit(solution)/shard_map/pallas_call | solution.py:137
  29.4 0.0 collective-permute-done.1.rest_1_
  29.4 2.4 %collective-permute-done.6.rest_0_ = bf16[384,256]{1,0:T(8,128)(2,1)S(1)} collective-permute-done((bf16[384,256]{1,0:T(8,128)(2,1)S(1)}, bf16[384,256]{1,0:T(8,128)(2,1)S(1)}, u32[]{:S(2)}, u32[]{:S(2)}) %collective-permute-start.6) | collective-permute-done | bytes 196640 | tf_op jit(solution)/shard_map/ppermute | solution.py:160
  31.8 0.0 copy-done.1
  31.8 0.1 pad_maximum_fusion
  31.8 4.3 %collective-permute-start.7 = (bf16[1536,256]{1,0:T(8,128)(2,1)S(1)}, bf16[1536,256]{1,0:T(8,128)(2,1)S(1)}, u32[]{:S(2)}, u32[]{:S(2)}) collective-permute-start(bf16[1536,256]{1,0:T(8,128)(2,1)S(1)} %pad_maximum_fusion), channel_id=1, source_target_pairs={{0,8},{8,0},{16,24},{24,16},{32,40},{40,32},{48,56},{56,48},{64,72... | collective-permute-start | bytes 2359304 | tf_op jit(solution)/shard_map/ppermute | solution.py:163
  36.2 2.6 %collective-permute-start.3 = (bf16[384,256]{1,0:T(8,128)(2,1)S(1)}, bf16[384,256]{1,0:T(8,128)(2,1)S(1)}, u32[]{:S(2)}, u32[]{:S(2)}) collective-permute-start(bf16[384,256]{1,0:T(8,128)(2,1)S(1)} %collective-permute-done.1.rest_1_), channel_id=1, source_target_pairs={{0,32},{8,40},{16,48},{24,56},{32,64},{40,72},{48,80},{56,88},{64,... | collective-permute-start | bytes 589832 | tf_op jit(solution)/shard_map/ppermute | solution.py:160
  38.8 1.9 %collective-permute-start.2 = (bf16[384,256]{1,0:T(8,128)(2,1)S(1)}, bf16[384,256]{1,0:T(8,128)(2,1)S(1)}, u32[]{:S(2)}, u32[]{:S(2)}) collective-permute-start(bf16[384,256]{1,0:T(8,128)(2,1)S(1)} %collective-permute-done.1.rest_1_), channel_id=1, source_target_pairs={{0,16},{8,24},{16,32},{24,40},{32,48},{40,56},{48,64},{56,72},{64,... | collective-permute-start | bytes 589832 | tf_op jit(solution)/shard_map/ppermute | solution.py:160
  40.8 4.2 %shard_map.66 = (f32[1536,256]{1,0:T(8,128)S(1)}, f32[1536,128]{1,0:T(8,128)S(1)}) custom-call(s32[195]{0:T(256)S(1)} %pad_add_fusion.index_ref, f32[128]{0:T(128)S(1)} %reshape.7.table_ref, s32[384,128]{1,0:T(8,128)S(1)} %broadcast_in_dim.10.starts_ref, bf16[384,512]{1,0:T(8,128)(2,1)S(1)} %copy-done.3, ...), custom_call_target="tpu_custom_call" | custom-call | flops 6039797760 | bytes 4194304 | tf_op jit(solution)/shard_map/pallas_call | solution.py:137
  45.0 0.0 collective-permute-done.3.rest_2_
  45.0 3.6 %collective-permute-start.4 = (bf16[384,256]{1,0:T(8,128)(2,1)S(1)}, bf16[384,256]{1,0:T(8,128)(2,1)S(1)}, u32[]{:S(2)}, u32[]{:S(2)}) collective-permute-start(bf16[384,256]{1,0:T(8,128)(2,1)S(1)} %collective-permute-done.3.rest_2_), channel_id=1, source_target_pairs={{0,16},{8,24},{16,32},{24,40},{32,48},{40,56},{48,64},{56,72},{64,... | collective-permute-start | bytes 589832 | tf_op jit(solution)/shard_map/ppermute | solution.py:160
  48.6 3.4 %collective-permute-start.8 = (bf16[384,256]{1,0:T(8,128)(2,1)S(1)}, bf16[384,256]{1,0:T(8,128)(2,1)S(1)}, u32[]{:S(2)}, u32[]{:S(2)}) collective-permute-start(bf16[384,256]{1,0:T(8,128)(2,1)S(1)} %collective-permute-done.3.rest_2_), channel_id=1, source_target_pairs={{0,32},{8,40},{16,48},{24,56},{32,64},{40,72},{48,80},{56,88},{64,... | collective-permute-start | bytes 589832 | tf_op jit(solution)/shard_map/ppermute | solution.py:160
  52.0 0.0 collective-permute-done.2.rest_1_
  52.1 0.0 collective-permute-done.7.rest_0_
  52.1 10.1 %shard_map.67 = (f32[1536,256]{1,0:T(8,128)S(1)}, f32[1536,128]{1,0:T(8,128)S(1)}) custom-call(s32[195]{0:T(256)S(1)} %pad_add_fusion.index_ref, f32[128]{0:T(128)S(1)} %reshape.7.table_ref, s32[384,128]{1,0:T(8,128)S(1)} %broadcast_in_dim.10.starts_ref, bf16[384,512]{1,0:T(8,128)(2,1)S(1)} %copy-done.3, ...), custom_call_target="tpu_custom_call" | custom-call | flops 18119393280 | bytes 4194304 | tf_op jit(solution)/shard_map/pallas_call | solution.py:137
  62.1 0.0 collective-permute-done.4.rest_0_
  62.2 0.0 collective-permute-done.8.rest_1_
  62.2 1.9 %collective-permute-start.9 = (bf16[1920,256]{1,0:T(8,128)(2,1)S(1)}, bf16[1920,256]{1,0:T(8,128)(2,1)S(1)}, u32[]{:S(2)}, u32[]{:S(2)}) collective-permute-start(bf16[1920,256]{1,0:T(8,128)(2,1)S(1)} %constant_dynamic-update-slice_fusion), channel_id=1, source_target_pairs={{0,8},{8,0},{16,24},{24,16},{32,40},{40,32},{48,56},{56,48},{64,72... | collective-permute-start | bytes 2949128 | tf_op jit(solution)/shard_map/ppermute | solution.py:163
  64.1 4.2 %shard_map.68 = (f32[1536,256]{1,0:T(8,128)S(1)}, f32[1536,128]{1,0:T(8,128)S(1)}) custom-call(s32[195]{0:T(256)S(1)} %pad_add_fusion.index_ref, f32[128]{0:T(128)S(1)} %reshape.7.table_ref, s32[384,128]{1,0:T(8,128)S(1)} %broadcast_in_dim.10.starts_ref, bf16[384,512]{1,0:T(8,128)(2,1)S(1)} %copy-done.3, ...), custom_call_target="tpu_custom_call" | custom-call | flops 6039797760 | bytes 4194304 | tf_op jit(solution)/shard_map/pallas_call | solution.py:137
  68.3 0.0 collective-permute-done.9.rest_0_
  68.3 0.0 copy-start.4
  68.3 7.1 %shard_map.69 = bf16[384,512]{1,0:T(8,128)(2,1)S(1)} custom-call(s32[195]{0:T(256)S(1)} %pad_add_fusion.index_ref, f32[128]{0:T(128)S(1)} %reshape.7.table_ref, s32[384,128]{1,0:T(8,128)S(1)} %broadcast_in_dim.10.starts_ref, bf16[384,512]{1,0:T(8,128)(2,1)S(1)} %copy-done.3, bf16[1920,256]{1,0:T(8,128)(2,1)S(1)} %collective-permute-done.9.rest_0_, ...), custom_call_target="tpu_custom_call" | custom-call | flops 15099494400 | bytes 4194304 | tf_op jit(solution)/shard_map/pallas_call | solution.py:137
  75.4 0.0 copy-done.4
  75.4 1.9 %convolution_convert_fusion = bf16[384,4096]{1,0:T(8,128)(2,1)S(1)} fusion(bf16[384,512]{1,0:T(8,128)(2,1)S(1)} %shard_map.69, bf16[512,4096]{1,0:T(8,128)(2,1)S(1)} %copy-done.4), kind=kOutput, calls=%fused_computation | convolution fusion | flops 1612185600 | bytes 7733248 | tf_op jit(solution)/shard_map/dot_general | solution.py:187
  77.3 42.1 %all_to_all.5 = bf16[8,48,4096]{2,1,0:T(8,128)(2,1)S(1)} all-to-all(bf16[8,48,4096]{2,1,0:T(8,128)(2,1)S(1)} %bitcast.4), channel_id=1, replica_groups=mesh['ctx'=64,'kvh'=8] {'kvh'}, dimensions={0} | all-to-all | bytes 6291456 | tf_op jit(solution)/shard_map/all_to_all | solution.py:188
  119.4 1.3 %reduce_sum.12 = bf16[48,4096]{1,0:T(8,128)(2,1)} reduce(bf16[8,48,4096]{2,1,0:T(8,128)(2,1)S(1)} %all_to_all.5, bf16[]{:T(256)} %constant.8.clone.1), dimensions={0}, to_apply=%region_0.0 | reduce | flops 1376256 | bytes 3538946 | tf_op jit(solution)/shard_map/reduce_sum | solution.py:189
  (5 shorter events, 0.1 us)
Async XLA Ops:
  0.0 17.8 %collective-permute-start = (bf16[384,256]{1,0:T(8,128)(2,1)}, bf16[384,256]{1,0:T(8,128)(2,1)S(1)}, u32[]{:S(2)}, u32[]{:S(2)}) collective-permute-start(bf16[384,256]{1,0:T(8,128)(2,1)} %rest_0_.1), channel_id=1, source_target_pairs={{0,32},{8,40},{16,48},{24,56},{32,64},{40,72},{48,80},{56,88},{64,... | collective-permute-start | bytes 589832 | tf_op jit(solution)/shard_map/ppermute | solution.py:160
  3.5 21.7 %collective-permute-start.5 = (bf16[384,256]{1,0:T(8,128)(2,1)}, bf16[384,256]{1,0:T(8,128)(2,1)S(1)}, u32[]{:S(2)}, u32[]{:S(2)}) collective-permute-start(bf16[384,256]{1,0:T(8,128)(2,1)} %rest_0_.1), channel_id=1, source_target_pairs={{0,16},{8,24},{16,32},{24,40},{32,48},{40,56},{48,64},{56,72},{64,... | collective-permute-start | bytes 589832 | tf_op jit(solution)/shard_map/ppermute | solution.py:160
  13.5 0.9 copy-start
  14.4 1.0 copy-start.2
  15.4 9.8 %copy-start.3 = (bf16[384,512]{1,0:T(8,128)(2,1)S(1)}, bf16[384,512]{1,0:T(8,128)(2,1)}, u32[]{:S(2)}) copy-start(bf16[384,512]{1,0:T(8,128)(2,1)} %query_ref.11) | copy-start | bytes 1179652
  17.8 11.6 %collective-permute-start.1 = (bf16[384,256]{1,0:T(8,128)(2,1)S(1)}, bf16[384,256]{1,0:T(8,128)(2,1)S(1)}, u32[]{:S(2)}, u32[]{:S(2)}) collective-permute-start(bf16[384,256]{1,0:T(8,128)(2,1)S(1)} %collective-permute-done.rest_1_), channel_id=1, source_target_pairs={{0,32},{8,40},{16,48},{24,56},{32,64},{40,72},{48,80},{56,88},{64,... | collective-permute-start | bytes 589832 | tf_op jit(solution)/shard_map/ppermute | solution.py:160
  22.6 9.2 %collective-permute-start.6 = (bf16[384,256]{1,0:T(8,128)(2,1)S(1)}, bf16[384,256]{1,0:T(8,128)(2,1)S(1)}, u32[]{:S(2)}, u32[]{:S(2)}) collective-permute-start(bf16[384,256]{1,0:T(8,128)(2,1)S(1)} %collective-permute-done.rest_1_), channel_id=1, source_target_pairs={{0,16},{8,24},{16,32},{24,40},{32,48},{40,56},{48,64},{56,72},{64,... | collective-permute-start | bytes 589832 | tf_op jit(solution)/shard_map/ppermute | solution.py:160
  25.2 6.6 %copy-start.1 = (bf16[384,256]{1,0:T(8,128)(2,1)S(1)}, bf16[384,256]{1,0:T(8,128)(2,1)}, u32[]{:S(2)}) copy-start(bf16[384,256]{1,0:T(8,128)(2,1)} %rest_0_.1) | copy-start | bytes 589828
  31.8 20.2 %collective-permute-start.7 = (bf16[1536,256]{1,0:T(8,128)(2,1)S(1)}, bf16[1536,256]{1,0:T(8,128)(2,1)S(1)}, u32[]{:S(2)}, u32[]{:S(2)}) collective-permute-start(bf16[1536,256]{1,0:T(8,128)(2,1)S(1)} %pad_maximum_fusion), channel_id=1, source_target_pairs={{0,8},{8,0},{16,24},{24,16},{32,40},{40,32},{48,56},{56,48},{64,72... | collective-permute-start | bytes 2359304 | tf_op jit(solution)/shard_map/ppermute | solution.py:163
  36.2 8.8 %collective-permute-start.3 = (bf16[384,256]{1,0:T(8,128)(2,1)S(1)}, bf16[384,256]{1,0:T(8,128)(2,1)S(1)}, u32[]{:S(2)}, u32[]{:S(2)}) collective-permute-start(bf16[384,256]{1,0:T(8,128)(2,1)S(1)} %collective-permute-done.1.rest_1_), channel_id=1, source_target_pairs={{0,32},{8,40},{16,48},{24,56},{32,64},{40,72},{48,80},{56,88},{64,... | collective-permute-start | bytes 589832 | tf_op jit(solution)/shard_map/ppermute | solution.py:160
  38.8 13.2 %collective-permute-start.2 = (bf16[384,256]{1,0:T(8,128)(2,1)S(1)}, bf16[384,256]{1,0:T(8,128)(2,1)S(1)}, u32[]{:S(2)}, u32[]{:S(2)}) collective-permute-start(bf16[384,256]{1,0:T(8,128)(2,1)S(1)} %collective-permute-done.1.rest_1_), channel_id=1, source_target_pairs={{0,16},{8,24},{16,32},{24,40},{32,48},{40,56},{48,64},{56,72},{64,... | collective-permute-start | bytes 589832 | tf_op jit(solution)/shard_map/ppermute | solution.py:160
  45.0 17.2 %collective-permute-start.4 = (bf16[384,256]{1,0:T(8,128)(2,1)S(1)}, bf16[384,256]{1,0:T(8,128)(2,1)S(1)}, u32[]{:S(2)}, u32[]{:S(2)}) collective-permute-start(bf16[384,256]{1,0:T(8,128)(2,1)S(1)} %collective-permute-done.3.rest_2_), channel_id=1, source_target_pairs={{0,16},{8,24},{16,32},{24,40},{32,48},{40,56},{48,64},{56,72},{64,... | collective-permute-start | bytes 589832 | tf_op jit(solution)/shard_map/ppermute | solution.py:160
  48.6 13.6 %collective-permute-start.8 = (bf16[384,256]{1,0:T(8,128)(2,1)S(1)}, bf16[384,256]{1,0:T(8,128)(2,1)S(1)}, u32[]{:S(2)}, u32[]{:S(2)}) collective-permute-start(bf16[384,256]{1,0:T(8,128)(2,1)S(1)} %collective-permute-done.3.rest_2_), channel_id=1, source_target_pairs={{0,32},{8,40},{16,48},{24,56},{32,64},{40,72},{48,80},{56,88},{64,... | collective-permute-start | bytes 589832 | tf_op jit(solution)/shard_map/ppermute | solution.py:160
  62.2 6.1 %collective-permute-start.9 = (bf16[1920,256]{1,0:T(8,128)(2,1)S(1)}, bf16[1920,256]{1,0:T(8,128)(2,1)S(1)}, u32[]{:S(2)}, u32[]{:S(2)}) collective-permute-start(bf16[1920,256]{1,0:T(8,128)(2,1)S(1)} %constant_dynamic-update-slice_fusion), channel_id=1, source_target_pairs={{0,8},{8,0},{16,24},{24,16},{32,40},{40,32},{48,56},{56,48},{64,72... | collective-permute-start | bytes 2949128 | tf_op jit(solution)/shard_map/ppermute | solution.py:163
  68.3 7.1 %copy-start.4 = (bf16[512,4096]{1,0:T(8,128)(2,1)S(1)}, bf16[512,4096]{1,0:T(8,128)(2,1)}, u32[]{:S(2)}) copy-start(bf16[512,4096]{1,0:T(8,128)(2,1)} %param.11) | copy-start | bytes 12582916

commit v3 on v2

--- a/solution.py
+++ b/solution.py
@@ -20,7 +20,7 @@
 
 
 def attend_kernel(
-    counts, groups, first, final, index_ref, table_ref, starts_ref, query_ref, *rest
+    counts, groups, first, final, my_ref, doc_ref, index_ref, table_ref, starts_ref, query_ref, *rest
 ):
     pieces, rest = rest[: len(counts)], rest[len(counts) :]
     if not first:
@@ -35,7 +35,7 @@
         copies.append(pltpu.make_async_copy(pieces[i], held.at[pl.ds(at * tok, count * tok)], sems.at[i]))
         copies[-1].start()
         at += count
-    low, high, my = [index_ref[index_ref.shape[0] - 3 + i] for i in range(3)]
+    my, low, high = my_ref[0], doc_ref[0], doc_ref[tok - 1]
     if first:
         acc_ref[...] = jnp.zeros_like(acc_ref)
         max_ref[...] = jnp.full(max_ref.shape, NEG, jnp.float32)
@@ -48,9 +48,9 @@
     def attend_blocks(step, src, count, masked):
         key_scales, value_scales = [], []
         for t in range(count * tok // SBLK):
-            row = index_ref[(src - 2 * (t // (tok // SBLK))) * (tok // SBLK) + t % (tok // SBLK)]
-            key_scales.append(jnp.full((1, SBLK), table_ref[2 * row] * FACTOR, jnp.float32))
-            value_scales.append(jnp.full((SBLK, HD), table_ref[2 * row + 1], jnp.float32))
+            row = index_ref[(src - 4 * (t // (tok // SBLK))) * (tok // SBLK) + t % (tok // SBLK)]
+            key_scales.append(jnp.full((1, SBLK), table_ref[row, 0] * FACTOR, jnp.float32))
+            value_scales.append(jnp.full((SBLK, HD), table_ref[row, 1], jnp.float32))
         scale = jnp.concatenate(key_scales, 1)
         width = count * tok
         kv_rows = pl.ds(pl.multiple_of(step * tok, tok), width)
@@ -88,11 +88,11 @@
 
     at = 0
     for count, mine, back in groups:
-        newest = (my if mine else my ^ 1) - back
+        newest = (my if mine else my ^ 1) - 2 * back
         if count == 1:
             one_block(at, newest)
         else:
-            oldest = newest - 2 * (count - 1)
+            oldest = newest - 4 * (count - 1)
             whole = (oldest >= 0) & (oldest * tok >= high) & (newest < my)
 
             @pl.when(whole)
@@ -102,7 +102,7 @@
             @pl.when(jnp.logical_not(whole))
             def _(at=at, newest=newest, count=count):
                 def one_step(step, _):
-                    one_block(at + step, newest - 2 * step)
+                    one_block(at + step, newest - 4 * step)
                     return 0
 
                 lax.fori_loop(0, count, one_step, 0)
@@ -137,7 +137,7 @@
     return pl.pallas_call(
         functools.partial(attend_kernel, counts, groups, state is None, final),
         out_shape=out_shape,
-        in_specs=[smem] * 2
+        in_specs=[smem] * 4
         + [vmem] * 2
         + [pl.BlockSpec(memory_space=pl.ANY)] * len(pieces)
         + [vmem] * (0 if state is None else 2),
@@ -153,36 +153,32 @@
     ctx_count = lax.axis_size("ctx")
     my = lax.axis_index("ctx").astype(jnp.int32)
     starts = jnp.broadcast_to(doc_start[:, None], (tok, HD))
-    places = jnp.concatenate([scale_index, doc_start[:1], doc_start[-1:], my[None]])
-    common = (places, scale_table.reshape(-1), starts, query)
+    common = (my[None], doc_start, scale_index, scale_table, starts, query)
 
     def shifted(block, distance):
         return lax.ppermute(block, "ctx", [(i, i + distance) for i in range(ctx_count - distance)])
 
-    def swapped(*blocks):
-        return lax.ppermute(jnp.concatenate(blocks), "ctx", [(i, i ^ 1) for i in range(ctx_count)])
+    def swapped(block):
+        return lax.ppermute(block, "ctx", [(i, i ^ 1) for i in range(ctx_count)])
 
     def after(block, *others):
         return lax.optimization_barrier((block, *others))[0]
 
-    even, odd = [keys_values], []
-    odd.append(shifted(even[0], 2))
-    even.append(shifted(even[0], 4))
-    state = attend(common, [even[0]], ((1, True, 0),))
-    odd.append(shifted(even[1], 2))
-    even.append(shifted(even[1], 4))
-    state = attend(common, [odd[0], even[1]], ((2, True, 2),), state)
-    odd.append(shifted(even[2], 2))
-    even.append(shifted(even[2], 4))
-    first_swap = swapped(even[0], odd[0], even[1], after(odd[1], even[2]))
-    state = attend(common, [odd[1], even[2]], ((2, True, 6),), state)
-    odd.append(shifted(even[3], 2))
-    even.append(shifted(even[3], 4))
-    groups = ((1, False, 0), (3, False, 2), (2, True, 10))
-    state = attend(common, [first_swap, odd[2], even[3]], groups, state)
-    second_swap = swapped(even[2], odd[2], even[3], after(odd[3], *state), even[4])
-    state = attend(common, [odd[3], even[4]], ((2, True, 14),), state)
-    attn = attend(common, [second_swap], ((4, False, 8), (1, False, 16)), state, True)
+    from_2 = shifted(keys_values, 4)
+    from_02 = jnp.concatenate([keys_values, from_2])
+    from_46 = shifted(from_02, 8)
+    from_13 = shifted(from_02, 2)
+    from_57 = shifted(from_46, 2)
+    from_8 = shifted(from_46[tok:], 4)
+    other_1302 = swapped(jnp.concatenate([from_13, from_02]))
+    state = attend(common, [keys_values, from_2], ((1, True, 0), (1, True, 2)))
+    state = attend(common, [from_13], ((2, True, 1),), state)
+    other_46 = swapped(after(from_46, *state))
+    groups = ((2, True, 4), (2, False, 1), (1, False, 0), (1, False, 2), (2, False, 4))
+    state = attend(common, [from_46, other_1302, other_46], groups, state)
+    other_578 = swapped(jnp.concatenate([after(from_57, *state), from_8]))
+    state = attend(common, [from_57, from_8], ((2, True, 5), (1, True, 8)), state)
+    attn = attend(common, [other_578], ((2, False, 5), (1, False, 8)), state, True)
     shares = lax.axis_size("kvh")
     partial = jnp.dot(attn, out_weight, preferred_element_type=jnp.float32).astype(jnp.bfloat16)
     pieces = lax.all_to_all(partial.reshape(shares, tok // shares, -1), "kvh", 0, 0)

time: 121 us -> 123 us (1.017)
  other arithmetic: 3.51 us -> 1.42 us
  Pallas kernels: 32.1 us -> 33.5 us
    ppermute x2 -> x3, starting transfers between devices: 6.26 us -> 11 us  [swapped(): return lax.ppermute(block, 'ctx', [(i, i ^ 1) for i in range(ctx_count)])]
    ppermute x8 -> x5, starting transfers between devices: 27.1 us -> 23.4 us  [shifted(): lax.ppermute(block, 'ctx', [(i, i + distance) for i in range(ctx_count -...]
    unnamed x15 -> x12, local copies, waits for them, and re-layouts: 2.76 us -> 4.99 us
    concatenate x2, other arithmetic: 2.19 us -> 0.09 us  [the longest x1 0.05 us: local(): other_1302 = swapped(jnp.concatenate([from_13, from_02]))]
    pallas_call x6 -> x5, Pallas kernels: 32.1 us -> 33.5 us  [attend(): pl.pallas_call(functools.partial(attend_kernel, counts, groups, state is...]
    slice x1, local copies, waits for them, and re-layouts: 1.42 us -> 0.01 us  [local(): from_8 = shifted(from_46[tok:], 4)]
    ppermute x8 -> x5, waiting for transfers between devices: 2.39 us -> 2.62 us  [shifted(): lax.ppermute(block, 'ctx', [(i, i + distance) for i in range(ctx_count -...]
  transfers between devices with their start and end apart: 10 -> 8, of which waited for: 1 -> 1; matrix products, arithmetic and copies ran while one was open for 4% -> 2% of each run, Pallas kernels for 21% -> 24%
where the time goes in v3:
time: 123 us; the launch traced here: 122 us
  blocking collectives  42.6 us (35%)
  starting transfers between devices  34.3 us (28%)
  Pallas kernels  33.5 us (27%)
  local copies, waits for them, and re-layouts  5.81 us (5%)
  waiting for transfers between devices  2.62 us (2%)
  matrix products  1.8 us (1%)
  other arithmetic  1.42 us (1%)
    all_to_all x1, blocking collectives, local(): lax.all_to_all(partial.reshape(shares, tok // shares, -1), 'kvh', 0, 0)  42.6 us
    pallas_call x5, Pallas kernels, attend(): pl.pallas_call(functools.partial(attend_kernel, counts, groups, state is...  33.5 us
    ppermute x5, starting transfers between devices, shifted(): lax.ppermute(block, 'ctx', [(i, i + distance) for i in range(ctx_count -...  23.4 us
    ppermute x3, starting transfers between devices, swapped(): return lax.ppermute(block, 'ctx', [(i, i ^ 1) for i in range(ctx_count)])  11 us
    unnamed x12, local copies, waits for them, and re-layouts  4.99 us
    ppermute x5, waiting for transfers between devices, shifted(): lax.ppermute(block, 'ctx', [(i, i + distance) for i in range(ctx_count -...  2.62 us
  transfers between devices with their start and end apart: 8, of which 1 were waited for; matrix products, arithmetic and copies ran while one was open for 2% of the time, Pallas kernels for 24%

profile of v3, /device:TPU:193, one launch (start us, length us, event | category | flops | bytes accessed | tf_op | source)
XLA Modules:
  0.0 122.4 jit_solution(10907285516205578369)
XLA Ops:
  0.0 3.5 %collective-permute-start = (bf16[384,256]{1,0:T(8,128)(2,1)}, bf16[384,256]{1,0:T(8,128)(2,1)S(1)}, u32[]{:S(2)}, u32[]{:S(2)}) collective-permute-start(bf16[384,256]{1,0:T(8,128)(2,1)} %rest_0_.1), channel_id=1, source_target_pairs={{0,32},{8,40},{16,48},{24,56},{32,64},{40,72},{48,80},{56,88},{64,... | collective-permute-start | bytes 589832 | tf_op jit(solution)/shard_map/ppermute | solution.py:159
  3.5 0.8 copy.11.table_ref
  4.3 0.9 constant_dynamic-update-slice_fusion.1
  5.3 2.6 %collective-permute-done.rest_1_ = bf16[384,256]{1,0:T(8,128)(2,1)S(1)} collective-permute-done((bf16[384,256]{1,0:T(8,128)(2,1)}, bf16[384,256]{1,0:T(8,128)(2,1)S(1)}, u32[]{:S(2)}, u32[]{:S(2)}) %collective-permute-start) | collective-permute-done | bytes 196640 | tf_op jit(solution)/shard_map/ppermute | solution.py:159
  7.9 4.7 %collective-permute-start.3 = (bf16[768,256]{1,0:T(8,128)(2,1)S(1)}, bf16[768,256]{1,0:T(8,128)(2,1)S(1)}, u32[]{:S(2)}, u32[]{:S(2)}) collective-permute-start(bf16[768,256]{1,0:T(8,128)(2,1)S(1)} %constant_dynamic-update-slice_fusion), channel_id=1, source_target_pairs={{0,16},{8,24},{16,32},{24,40},{32,48},{40,56},{48,64},{56,72},{64,... | collective-permute-start | bytes 1179656 | tf_op jit(solution)/shard_map/ppermute | solution.py:159
  12.5 7.3 %collective-permute-start.1 = (bf16[768,256]{1,0:T(8,128)(2,1)S(1)}, bf16[768,256]{1,0:T(8,128)(2,1)S(1)}, u32[]{:S(2)}, u32[]{:S(2)}) collective-permute-start(bf16[768,256]{1,0:T(8,128)(2,1)S(1)} %constant_dynamic-update-slice_fusion), channel_id=1, source_target_pairs={{0,64},{8,72},{16,80},{24,88},{32,96},{40,104},{48,112},{56,120},{... | collective-permute-start | bytes 1179656 | tf_op jit(solution)/shard_map/ppermute | solution.py:159
  19.9 0.8 broadcast_in_dim.10.starts_ref
  20.7 0.0 copy-start
  20.7 0.9 copy-done
  21.6 0.0 copy-start.1
  21.6 0.7 copy-done.1
  22.3 0.0 copy-start.2
  22.3 1.0 copy-done.2
  23.3 0.0 copy-start.3
  23.3 0.7 copy-done.3
  24.0 4.7 %shard_map.64 = (f32[1536,256]{1,0:T(8,128)S(1)}, f32[1536,128]{1,0:T(8,128)S(1)}) custom-call(s32[1]{0:T(128)} %bitcast.my_ref, s32[384]{0:T(512)S(1)} %copy-done.1, s32[192]{0:T(256)S(1)} %copy-done.3, f32[64,2]{1,0:T(8,128)S(1)} %copy.11.table_ref, s32[384,128]{1,0:T(8,128)S(1)} %broadcast_in_dim.10.starts_ref, bf16[384,512]{1,0:T(8,128)(2,1)S(1)} %copy-done.2, ...), custom_call_target="tpu_custom_call" | custom-call | flops 6039797760 | bytes 4194304 | tf_op jit(solution)/shard_map/pallas_call | solution.py:137
  28.7 0.0 collective-permute-done.3.rest_0_
  28.7 0.1 pad_maximum_fusion
  28.7 7.1 %collective-permute-start.4 = (bf16[1536,256]{1,0:T(8,128)(2,1)S(1)}, bf16[1536,256]{1,0:T(8,128)(2,1)S(1)}, u32[]{:S(2)}, u32[]{:S(2)}) collective-permute-start(bf16[1536,256]{1,0:T(8,128)(2,1)S(1)} %pad_maximum_fusion), channel_id=1, source_target_pairs={{0,8},{8,0},{16,24},{24,16},{32,40},{40,32},{48,56},{56,48},{64,72... | collective-permute-start | bytes 2359304 | tf_op jit(solution)/shard_map/ppermute | solution.py:162
  35.9 4.4 %shard_map.65 = (f32[1536,256]{1,0:T(8,128)S(1)}, f32[1536,128]{1,0:T(8,128)S(1)}) custom-call(s32[1]{0:T(128)} %bitcast.my_ref, s32[384]{0:T(512)S(1)} %copy-done.1, s32[192]{0:T(256)S(1)} %copy-done.3, f32[64,2]{1,0:T(8,128)S(1)} %copy.11.table_ref, s32[384,128]{1,0:T(8,128)S(1)} %broadcast_in_dim.10.starts_ref, bf16[384,512]{1,0:T(8,128)(2,1)S(1)} %copy-done.2, ...), custom_call_target="tpu_custom_call" | custom-call | flops 6039797760 | bytes 4194304 | tf_op jit(solution)/shard_map/pallas_call | solution.py:137
  40.3 0.0 collective-permute-done.1.rest_0_
  40.3 1.9 %collective-permute-start.5 = (bf16[768,256]{1,0:T(8,128)(2,1)S(1)}, bf16[768,256]{1,0:T(8,128)(2,1)S(1)}, u32[]{:S(2)}, u32[]{:S(2)}) collective-permute-start(bf16[768,256]{1,0:T(8,128)(2,1)S(1)} %collective-permute-done.1.rest_0_), channel_id=1, source_target_pairs={{0,8},{8,0},{16,24},{24,16},{32,40},{40,32},{48,56},{56,48},{64,72... | collective-permute-start | bytes 1179656 | tf_op jit(solution)/shard_map/ppermute | solution.py:162
  42.2 1.9 %collective-permute-start.6 = (bf16[384,256]{1,0:T(8,128)(2,1)S(1)}, bf16[384,256]{1,0:T(8,128)(2,1)S(1)}, u32[]{:S(2)}, u32[]{:S(2)}) collective-permute-start(bf16[384,256]{1,0:T(8,128)(2,1)S(1)} %slice.4), channel_id=1, source_target_pairs={{0,32},{8,40},{16,48},{24,56},{32,64},{40,72},{48,80},{56,88},{64,... | collective-permute-start | bytes 589832 | tf_op jit(solution)/shard_map/ppermute | solution.py:159
  44.2 5.9 %collective-permute-start.2 = (bf16[768,256]{1,0:T(8,128)(2,1)S(1)}, bf16[768,256]{1,0:T(8,128)(2,1)S(1)}, u32[]{:S(2)}, u32[]{:S(2)}) collective-permute-start(bf16[768,256]{1,0:T(8,128)(2,1)S(1)} %collective-permute-done.1.rest_0_), channel_id=1, source_target_pairs={{0,16},{8,24},{16,32},{24,40},{32,48},{40,56},{48,64},{56,72},{64,... | collective-permute-start | bytes 1179656 | tf_op jit(solution)/shard_map/ppermute | solution.py:159
  50.1 0.0 collective-permute-done.5.rest_2_
  50.1 0.0 collective-permute-done.4.rest_1_
  50.1 13.7 %shard_map.66 = (f32[1536,256]{1,0:T(8,128)S(1)}, f32[1536,128]{1,0:T(8,128)S(1)}) custom-call(s32[1]{0:T(128)} %bitcast.my_ref, s32[384]{0:T(512)S(1)} %copy-done.1, s32[192]{0:T(256)S(1)} %copy-done.3, f32[64,2]{1,0:T(8,128)S(1)} %copy.11.table_ref, s32[384,128]{1,0:T(8,128)S(1)} %broadcast_in_dim.10.starts_ref, bf16[384,512]{1,0:T(8,128)(2,1)S(1)} %copy-done.2, ...), custom_call_target="tpu_custom_call" | custom-call | flops 24159191040 | bytes 4194304 | tf_op jit(solution)/shard_map/pallas_call | solution.py:137
  63.8 0.0 collective-permute-done.2.rest_0_
  63.8 0.0 collective-permute-done.6.rest_1_
  63.9 1.9 %collective-permute-start.7 = (bf16[1152,256]{1,0:T(8,128)(2,1)S(1)}, bf16[1152,256]{1,0:T(8,128)(2,1)S(1)}, u32[]{:S(2)}, u32[]{:S(2)}) collective-permute-start(bf16[1152,256]{1,0:T(8,128)(2,1)S(1)} %pad_maximum_fusion.1), channel_id=1, source_target_pairs={{0,8},{8,0},{16,24},{24,16},{32,40},{40,32},{48,56},{56,48},{64,72... | collective-permute-start | bytes 1769480 | tf_op jit(solution)/shard_map/ppermute | solution.py:162
  65.8 6.4 %shard_map.67 = (f32[1536,256]{1,0:T(8,128)S(1)}, f32[1536,128]{1,0:T(8,128)S(1)}) custom-call(s32[1]{0:T(128)} %bitcast.my_ref, s32[384]{0:T(512)S(1)} %copy-done.1, s32[192]{0:T(256)S(1)} %copy-done.3, f32[64,2]{1,0:T(8,128)S(1)} %copy.11.table_ref, s32[384,128]{1,0:T(8,128)S(1)} %broadcast_in_dim.10.starts_ref, bf16[384,512]{1,0:T(8,128)(2,1)S(1)} %copy-done.2, ...), custom_call_target="tpu_custom_call" | custom-call | flops 9059696640 | bytes 4194304 | tf_op jit(solution)/shard_map/pallas_call | solution.py:137
  72.2 0.0 collective-permute-done.7.rest_0_
  72.2 0.0 copy-start.4
  72.2 4.3 %shard_map.68 = bf16[384,512]{1,0:T(8,128)(2,1)S(1)} custom-call(s32[1]{0:T(128)} %bitcast.my_ref, s32[384]{0:T(512)S(1)} %copy-done.1, s32[192]{0:T(256)S(1)} %copy-done.3, f32[64,2]{1,0:T(8,128)S(1)} %copy.11.table_ref, s32[384,128]{1,0:T(8,128)S(1)} %broadcast_in_dim.10.starts_ref, bf16[384,512]{1,0:T(8,128)(2,1)S(1)} %copy-done.2, ...), custom_call_target="tpu_custom_call" | custom-call | flops 9059696640 | bytes 4194304 | tf_op jit(solution)/shard_map/pallas_call | solution.py:137
  76.6 0.0 copy-done.4
  76.6 1.8 %convolution_convert_fusion = bf16[384,4096]{1,0:T(8,128)(2,1)S(1)} fusion(bf16[384,512]{1,0:T(8,128)(2,1)S(1)} %shard_map.68, bf16[512,4096]{1,0:T(8,128)(2,1)S(1)} %copy-done.4), kind=kOutput, calls=%fused_computation | convolution fusion | flops 1612185600 | bytes 7733248 | tf_op jit(solution)/shard_map/dot_general | solution.py:183
  78.4 42.6 %all_to_all.5 = bf16[8,48,4096]{2,1,0:T(8,128)(2,1)S(1)} all-to-all(bf16[8,48,4096]{2,1,0:T(8,128)(2,1)S(1)} %bitcast.4), channel_id=1, replica_groups=mesh['ctx'=64,'kvh'=8] {'kvh'}, dimensions={0} | all-to-all | bytes 6291456 | tf_op jit(solution)/shard_map/all_to_all | solution.py:184
  121.0 1.3 %reduce_sum.12 = bf16[48,4096]{1,0:T(8,128)(2,1)} reduce(bf16[8,48,4096]{2,1,0:T(8,128)(2,1)S(1)} %all_to_all.5, bf16[]{:T(256)} %constant.8.clone.1), dimensions={0}, to_apply=%region_0.0 | reduce | flops 1376256 | bytes 3538946 | tf_op jit(solution)/shard_map/reduce_sum | solution.py:185
  (3 shorter events, 0.1 us)
Async XLA Ops:
  0.0 7.9 %collective-permute-start = (bf16[384,256]{1,0:T(8,128)(2,1)}, bf16[384,256]{1,0:T(8,128)(2,1)S(1)}, u32[]{:S(2)}, u32[]{:S(2)}) collective-permute-start(bf16[384,256]{1,0:T(8,128)(2,1)} %rest_0_.1), channel_id=1, source_target_pairs={{0,32},{8,40},{16,48},{24,56},{32,64},{40,72},{48,80},{56,88},{64,... | collective-permute-start | bytes 589832 | tf_op jit(solution)/shard_map/ppermute | solution.py:159
  7.9 20.8 %collective-permute-start.3 = (bf16[768,256]{1,0:T(8,128)(2,1)S(1)}, bf16[768,256]{1,0:T(8,128)(2,1)S(1)}, u32[]{:S(2)}, u32[]{:S(2)}) collective-permute-start(bf16[768,256]{1,0:T(8,128)(2,1)S(1)} %constant_dynamic-update-slice_fusion), channel_id=1, source_target_pairs={{0,16},{8,24},{16,32},{24,40},{32,48},{40,56},{48,64},{56,72},{64,... | collective-permute-start | bytes 1179656 | tf_op jit(solution)/shard_map/ppermute | solution.py:159
  12.5 27.7 %collective-permute-start.1 = (bf16[768,256]{1,0:T(8,128)(2,1)S(1)}, bf16[768,256]{1,0:T(8,128)(2,1)S(1)}, u32[]{:S(2)}, u32[]{:S(2)}) collective-permute-start(bf16[768,256]{1,0:T(8,128)(2,1)S(1)} %constant_dynamic-update-slice_fusion), channel_id=1, source_target_pairs={{0,64},{8,72},{16,80},{24,88},{32,96},{40,104},{48,112},{56,120},{... | collective-permute-start | bytes 1179656 | tf_op jit(solution)/shard_map/ppermute | solution.py:159
  20.7 0.9 copy-start
  21.6 0.7 copy-start.1
  22.3 1.0 copy-start.2
  23.3 0.7 copy-start.3
  28.7 21.4 %collective-permute-start.4 = (bf16[1536,256]{1,0:T(8,128)(2,1)S(1)}, bf16[1536,256]{1,0:T(8,128)(2,1)S(1)}, u32[]{:S(2)}, u32[]{:S(2)}) collective-permute-start(bf16[1536,256]{1,0:T(8,128)(2,1)S(1)} %pad_maximum_fusion), channel_id=1, source_target_pairs={{0,8},{8,0},{16,24},{24,16},{32,40},{40,32},{48,56},{56,48},{64,72... | collective-permute-start | bytes 2359304 | tf_op jit(solution)/shard_map/ppermute | solution.py:162
  40.3 9.8 %collective-permute-start.5 = (bf16[768,256]{1,0:T(8,128)(2,1)S(1)}, bf16[768,256]{1,0:T(8,128)(2,1)S(1)}, u32[]{:S(2)}, u32[]{:S(2)}) collective-permute-start(bf16[768,256]{1,0:T(8,128)(2,1)S(1)} %collective-permute-done.1.rest_0_), channel_id=1, source_target_pairs={{0,8},{8,0},{16,24},{24,16},{32,40},{40,32},{48,56},{56,48},{64,72... | collective-permute-start | bytes 1179656 | tf_op jit(solution)/shard_map/ppermute | solution.py:162
  42.2 21.6 %collective-permute-start.6 = (bf16[384,256]{1,0:T(8,128)(2,1)S(1)}, bf16[384,256]{1,0:T(8,128)(2,1)S(1)}, u32[]{:S(2)}, u32[]{:S(2)}) collective-permute-start(bf16[384,256]{1,0:T(8,128)(2,1)S(1)} %slice.4), channel_id=1, source_target_pairs={{0,32},{8,40},{16,48},{24,56},{32,64},{40,72},{48,80},{56,88},{64,... | collective-permute-start | bytes 589832 | tf_op jit(solution)/shard_map/ppermute | solution.py:159
  44.2 19.7 %collective-permute-start.2 = (bf16[768,256]{1,0:T(8,128)(2,1)S(1)}, bf16[768,256]{1,0:T(8,128)(2,1)S(1)}, u32[]{:S(2)}, u32[]{:S(2)}) collective-permute-start(bf16[768,256]{1,0:T(8,128)(2,1)S(1)} %collective-permute-done.1.rest_0_), channel_id=1, source_target_pairs={{0,16},{8,24},{16,32},{24,40},{32,48},{40,56},{48,64},{56,72},{64,... | collective-permute-start | bytes 1179656 | tf_op jit(solution)/shard_map/ppermute | solution.py:159
  63.9 8.3 %collective-permute-start.7 = (bf16[1152,256]{1,0:T(8,128)(2,1)S(1)}, bf16[1152,256]{1,0:T(8,128)(2,1)S(1)}, u32[]{:S(2)}, u32[]{:S(2)}) collective-permute-start(bf16[1152,256]{1,0:T(8,128)(2,1)S(1)} %pad_maximum_fusion.1), channel_id=1, source_target_pairs={{0,8},{8,0},{16,24},{24,16},{32,40},{40,32},{48,56},{56,48},{64,72... | collective-permute-start | bytes 1769480 | tf_op jit(solution)/shard_map/ppermute | solution.py:162
  72.2 4.4 %copy-start.4 = (bf16[512,4096]{1,0:T(8,128)(2,1)S(1)}, bf16[512,4096]{1,0:T(8,128)(2,1)}, u32[]{:S(2)}) copy-start(bf16[512,4096]{1,0:T(8,128)(2,1)} %param.11) | copy-start | bytes 12582916

commit v4 on v3

--- a/solution.py
+++ b/solution.py
@@ -24,10 +24,11 @@
 ):
     pieces, rest = rest[: len(counts)], rest[len(counts) :]
     if not first:
-        (acc_in, max_in), rest = rest[:2], rest[2:]
+        rest = rest[2:]
+    acc_ref, max_ref, *rest = rest
     if final:
-        out_ref, rest = rest[0], rest[1:]
-    acc_ref, max_ref, bias_ref, held, sems = rest
+        out_ref, *rest = rest
+    bias_ref, held, sems = rest
     tok = query_ref.shape[0]
     copies = []
     at = 0
@@ -39,9 +40,6 @@
     if first:
         acc_ref[...] = jnp.zeros_like(acc_ref)
         max_ref[...] = jnp.full(max_ref.shape, NEG, jnp.float32)
-    else:
-        acc_ref[...] = acc_in[...]
-        max_ref[...] = max_in[...]
     for copy in copies:
         copy.wait()
 
@@ -128,11 +126,9 @@
         pltpu.VMEM((sum(counts) * tok, 2 * HD), jnp.bfloat16),
         pltpu.SemaphoreType.DMA((len(counts),)),
     ]
+    out_shape = state_shape
     if final:
-        out_shape, out_specs = jax.ShapeDtypeStruct((tok, GROUPS * HD), jnp.bfloat16), vmem
-        scratch = [pltpu.VMEM(s.shape, s.dtype) for s in state_shape] + scratch
-    else:
-        out_shape, out_specs = state_shape, (vmem, vmem)
+        out_shape += (jax.ShapeDtypeStruct((tok, GROUPS * HD), jnp.bfloat16),)
     flops = sum(counts) * GROUPS * tok * tok * HD * 4
     return pl.pallas_call(
         functools.partial(attend_kernel, counts, groups, state is None, final),
@@ -141,8 +137,9 @@
         + [vmem] * 2
         + [pl.BlockSpec(memory_space=pl.ANY)] * len(pieces)
         + [vmem] * (0 if state is None else 2),
-        out_specs=out_specs,
+        out_specs=(vmem,) * len(out_shape),
         scratch_shapes=scratch,
+        input_output_aliases={} if state is None else {6 + len(pieces): 0, 7 + len(pieces): 1},
         compiler_params=pltpu.CompilerParams(vmem_limit_bytes=40 << 20),
         cost_estimate=pl.CostEstimate(flops=10 * flops, bytes_accessed=4 << 20, transcendentals=0),
     )(*common, *pieces, *(state or ()))
@@ -165,20 +162,20 @@
         return lax.optimization_barrier((block, *others))[0]
 
     from_2 = shifted(keys_values, 4)
+    from_4 = shifted(from_2, 4)
+    from_6 = shifted(from_4, 4)
+    from_8 = shifted(from_6, 4)
     from_02 = jnp.concatenate([keys_values, from_2])
-    from_46 = shifted(from_02, 8)
     from_13 = shifted(from_02, 2)
+    from_46 = jnp.concatenate([from_4, from_6])
     from_57 = shifted(from_46, 2)
-    from_8 = shifted(from_46[tok:], 4)
     other_1302 = swapped(jnp.concatenate([from_13, from_02]))
     state = attend(common, [keys_values, from_2], ((1, True, 0), (1, True, 2)))
-    state = attend(common, [from_13], ((2, True, 1),), state)
-    other_46 = swapped(after(from_46, *state))
-    groups = ((2, True, 4), (2, False, 1), (1, False, 0), (1, False, 2), (2, False, 4))
-    state = attend(common, [from_46, other_1302, other_46], groups, state)
-    other_578 = swapped(jnp.concatenate([after(from_57, *state), from_8]))
+    groups = ((2, True, 1), (2, True, 4), (2, False, 1), (1, False, 0), (1, False, 2))
+    state = attend(common, [from_13, from_46, other_1302], groups, state)
+    other_46857 = swapped(jnp.concatenate([from_46, from_8, after(from_57, *state)]))
     state = attend(common, [from_57, from_8], ((2, True, 5), (1, True, 8)), state)
-    attn = attend(common, [other_578], ((2, False, 5), (1, False, 8)), state, True)
+    _, _, attn = attend(common, [other_46857], ((3, False, 4), (2, False, 5)), state, True)
     shares = lax.axis_size("kvh")
     partial = jnp.dot(attn, out_weight, preferred_element_type=jnp.float32).astype(jnp.bfloat16)
     pieces = lax.all_to_all(partial.reshape(shares, tok // shares, -1), "kvh", 0, 0)

time: 123 us -> 122 us (level)
  the two profiles are of different devices: /device:TPU:193 before, /device:TPU:229 now
where the time goes in v4:
time: 122 us; the launch traced here: 121 us
  blocking collectives  43.2 us (35%)
  Pallas kernels  32 us (26%)
  starting transfers between devices  27.8 us (23%)
  waiting for transfers between devices  12.2 us (10%)
  other arithmetic  3.32 us (3%)
  matrix products  1.8 us (1%)
    all_to_all x1, blocking collectives, local(): lax.all_to_all(partial.reshape(shares, tok // shares, -1), 'kvh', 0, 0)  43.2 us
    pallas_call x4, Pallas kernels, attend(): pl.pallas_call(functools.partial(attend_kernel, counts, groups, state is...  32 us
    ppermute x6, starting transfers between devices, shifted(): lax.ppermute(block, 'ctx', [(i, i + distance) for i in range(ctx_count -...  21.2 us
    ppermute x6, waiting for transfers between devices, shifted(): lax.ppermute(block, 'ctx', [(i, i + distance) for i in range(ctx_count -...  12.2 us
    ppermute x2, starting transfers between devices, swapped(): return lax.ppermute(block, 'ctx', [(i, i ^ 1) for i in range(ctx_count)])  6.58 us
  transfers between devices with their start and end apart: 8, of which 2 were waited for; matrix products, arithmetic and copies ran while one was open for 2% of the time, Pallas kernels for 20%

profile of v4, /device:TPU:229, one launch (start us, length us, event | category | flops | bytes accessed | tf_op | source)
XLA Modules:
  0.0 121.4 jit_solution(11039128983357760296)
XLA Ops:
  0.0 0.0 copy-start
  0.0 0.0 copy-start.1
  0.0 0.0 copy-start.2
  0.0 0.0 copy-start.3
  0.0 4.9 %collective-permute-start = (bf16[384,256]{1,0:T(8,128)(2,1)}, bf16[384,256]{1,0:T(8,128)(2,1)S(1)}, u32[]{:S(2)}, u32[]{:S(2)}) collective-permute-start(bf16[384,256]{1,0:T(8,128)(2,1)} %rest_0_.1), channel_id=1, source_target_pairs={{0,32},{8,40},{16,48},{24,56},{32,64},{40,72},{48,80},{56,88},{64,... | collective-permute-start | bytes 589832 | tf_op jit(solution)/shard_map/ppermute | solution.py:156
  4.9 3.9 %collective-permute-done.rest_1_ = bf16[384,256]{1,0:T(8,128)(2,1)S(1)} collective-permute-done((bf16[384,256]{1,0:T(8,128)(2,1)}, bf16[384,256]{1,0:T(8,128)(2,1)S(1)}, u32[]{:S(2)}, u32[]{:S(2)}) %collective-permute-start) | collective-permute-done | bytes 196640 | tf_op jit(solution)/shard_map/ppermute | solution.py:156
  8.8 1.0 pad_maximum_fusion.2
  9.7 5.2 %collective-permute-start.5 = (bf16[768,256]{1,0:T(8,128)(2,1)S(1)}, bf16[768,256]{1,0:T(8,128)(2,1)S(1)}, u32[]{:S(2)}, u32[]{:S(2)}) collective-permute-start(bf16[768,256]{1,0:T(8,128)(2,1)S(1)} %pad_maximum_fusion.2), channel_id=1, source_target_pairs={{0,16},{8,24},{16,32},{24,40},{32,48},{40,56},{48,64},{56,72},{64,... | collective-permute-start | bytes 1179656 | tf_op jit(solution)/shard_map/ppermute | solution.py:156
  14.9 2.0 %collective-permute-start.1 = (bf16[384,256]{1,0:T(8,128)(2,1)S(1)}, bf16[384,256]{1,0:T(8,128)(2,1)S(1)}, u32[]{:S(2)}, u32[]{:S(2)}) collective-permute-start(bf16[384,256]{1,0:T(8,128)(2,1)S(1)} %collective-permute-done.rest_1_), channel_id=1, source_target_pairs={{0,32},{8,40},{16,48},{24,56},{32,64},{40,72},{48,80},{56,88},{64,... | collective-permute-start | bytes 589832 | tf_op jit(solution)/shard_map/ppermute | solution.py:156
  16.9 0.8 copy.16.table_ref
  17.7 8.3 %collective-permute-done.1 = bf16[384,256]{1,0:T(8,128)(2,1)S(1)} collective-permute-done((bf16[384,256]{1,0:T(8,128)(2,1)S(1)}, bf16[384,256]{1,0:T(8,128)(2,1)S(1)}, u32[]{:S(2)}, u32[]{:S(2)}) %collective-permute-start.1) | collective-permute-done | bytes 196640 | tf_op jit(solution)/shard_map/ppermute | solution.py:156
  26.0 5.3 %collective-permute-start.2 = (bf16[384,256]{1,0:T(8,128)(2,1)S(1)}, bf16[384,256]{1,0:T(8,128)(2,1)S(1)}, u32[]{:S(2)}, u32[]{:S(2)}) collective-permute-start(bf16[384,256]{1,0:T(8,128)(2,1)S(1)} %collective-permute-done.1), channel_id=1, source_target_pairs={{0,32},{8,40},{16,48},{24,56},{32,64},{40,72},{48,80},{56,88},{64,... | collective-permute-start | bytes 589832 | tf_op jit(solution)/shard_map/ppermute | solution.py:156
  31.3 0.0 collective-permute-done.5.rest_0_
  31.3 1.0 pad_maximum_fusion.1
  32.3 4.7 %collective-permute-start.6 = (bf16[1536,256]{1,0:T(8,128)(2,1)S(1)}, bf16[1536,256]{1,0:T(8,128)(2,1)S(1)}, u32[]{:S(2)}, u32[]{:S(2)}) collective-permute-start(bf16[1536,256]{1,0:T(8,128)(2,1)S(1)} %pad_maximum_fusion.1), channel_id=1, source_target_pairs={{0,8},{8,0},{16,24},{24,16},{32,40},{40,32},{48,56},{56,48},{64,72... | collective-permute-start | bytes 2359304 | tf_op jit(solution)/shard_map/ppermute | solution.py:159
  36.9 0.0 copy-done.1
  36.9 0.1 broadcast_in_dim.10.starts_ref
  37.1 0.0 copy-done
  37.1 0.0 copy-done.2
  37.1 0.0 copy-done.3
  37.1 4.7 %shard_map.64 = (f32[1536,256]{1,0:T(8,128)S(1)}, f32[1536,128]{1,0:T(8,128)S(1)}) custom-call(s32[1]{0:T(128)} %bitcast.my_ref, s32[384]{0:T(512)S(1)} %copy-done.1, s32[192]{0:T(256)S(1)} %copy-done.3, f32[64,2]{1,0:T(8,128)S(1)} %copy.16.table_ref, s32[384,128]{1,0:T(8,128)S(1)} %broadcast_in_dim.10.starts_ref, bf16[384,512]{1,0:T(8,128)(2,1)S(1)} %copy-done.2, ...), custom_call_target="tpu_custom_call" | custom-call | flops 6039797760 | bytes 4194304 | tf_op jit(solution)/shard_map/pallas_call | solution.py:133
  41.8 0.0 collective-permute-done.2
  41.9 1.9 %collective-permute-start.4 = (bf16[768,256]{1,0:T(8,128)(2,1)S(1)}, bf16[768,256]{1,0:T(8,128)(2,1)S(1)}, u32[]{:S(2)}, u32[]{:S(2)}) collective-permute-start(bf16[768,256]{1,0:T(8,128)(2,1)S(1)} %constant_dynamic-update-slice_fusion.rest_1_), channel_id=1, source_target_pairs={{0,16},{8,24},{16,32},{24,40},{32,48},{40,56},{48,64},{56,72},{64,... | collective-permute-start | bytes 1179656 | tf_op jit(solution)/shard_map/ppermute | solution.py:156
  43.8 1.9 %collective-permute-start.3 = (bf16[384,256]{1,0:T(8,128)(2,1)S(1)}, bf16[384,256]{1,0:T(8,128)(2,1)S(1)}, u32[]{:S(2)}, u32[]{:S(2)}) collective-permute-start(bf16[384,256]{1,0:T(8,128)(2,1)S(1)} %collective-permute-done.2), channel_id=1, source_target_pairs={{0,32},{8,40},{16,48},{24,56},{32,64},{40,72},{48,80},{56,88},{64,... | collective-permute-start | bytes 589832 | tf_op jit(solution)/shard_map/ppermute | solution.py:156
  45.7 0.0 collective-permute-done.6.rest_2_
  45.7 13.5 %shard_map.65 = (f32[1536,256]{1,0:T(8,128)S(1)}, f32[1536,128]{1,0:T(8,128)S(1)}) custom-call(s32[1]{0:T(128)} %bitcast.my_ref, s32[384]{0:T(512)S(1)} %copy-done.1, s32[192]{0:T(256)S(1)} %copy-done.3, f32[64,2]{1,0:T(8,128)S(1)} %copy.16.table_ref, s32[384,128]{1,0:T(8,128)S(1)} %broadcast_in_dim.10.starts_ref, ...), custom_call_target="tpu_custom_call", output_to_operand_aliasing={{0}: (9, {}), {1}: (10, {})} | custom-call | flops 24159191040 | bytes 4194304 | tf_op jit(solution)/shard_map/pallas_call | solution.py:133
  59.3 0.0 collective-permute-done.4.rest_0_
  59.3 0.0 collective-permute-done.3.rest_1_
  59.3 0.1 pad_maximum_fusion
  59.4 1.9 %collective-permute-start.7 = (bf16[1920,256]{1,0:T(8,128)(2,1)S(1)}, bf16[1920,256]{1,0:T(8,128)(2,1)S(1)}, u32[]{:S(2)}, u32[]{:S(2)}) collective-permute-start(bf16[1920,256]{1,0:T(8,128)(2,1)S(1)} %pad_maximum_fusion), channel_id=1, source_target_pairs={{0,8},{8,0},{16,24},{24,16},{32,40},{40,32},{48,56},{56,48},{64,72... | collective-permute-start | bytes 2949128 | tf_op jit(solution)/shard_map/ppermute | solution.py:159
  61.3 6.0 %shard_map.66 = (f32[1536,256]{1,0:T(8,128)S(1)}, f32[1536,128]{1,0:T(8,128)S(1)}) custom-call(s32[1]{0:T(128)} %bitcast.my_ref, s32[384]{0:T(512)S(1)} %copy-done.1, s32[192]{0:T(256)S(1)} %copy-done.3, f32[64,2]{1,0:T(8,128)S(1)} %copy.16.table_ref, s32[384,128]{1,0:T(8,128)S(1)} %broadcast_in_dim.10.starts_ref, ...), custom_call_target="tpu_custom_call", output_to_operand_aliasing={{0}: (8, {}), {1}: (9, {})} | custom-call | flops 9059696640 | bytes 4194304 | tf_op jit(solution)/shard_map/pallas_call | solution.py:133
  67.3 0.0 collective-permute-done.7.rest_0_
  67.3 0.0 copy-start.4
  67.3 7.7 %shard_map.67 = (f32[1536,256]{1,0:T(8,128)S(1)}, f32[1536,128]{1,0:T(8,128)S(1)}, bf16[384,512]{1,0:T(8,128)(2,1)S(1)}) custom-call(s32[1]{0:T(128)} %bitcast.my_ref, s32[384]{0:T(512)S(1)} %copy-done.1, s32[192]{0:T(256)S(1)} %copy-done.3, f32[64,2]{1,0:T(8,128)S(1)} %copy.16.table_ref, ...), custom_call_target="tpu_custom_call", output_to_operand_aliasing={{0}: (7, {}), {1}: (8, {})} | custom-call | flops 15099494400 | bytes 4194304 | tf_op jit(solution)/shard_map/pallas_call | solution.py:133
  75.0 0.0 copy-done.4
  75.0 1.8 %convolution_convert_fusion = bf16[384,4096]{1,0:T(8,128)(2,1)S(1)} fusion(bf16[384,512]{1,0:T(8,128)(2,1)S(1)} %get-tuple-element.20, bf16[512,4096]{1,0:T(8,128)(2,1)S(1)} %copy-done.4), kind=kOutput, calls=%fused_computation | convolution fusion | flops 1612185600 | bytes 7733248 | tf_op jit(solution)/shard_map/dot_general | solution.py:180
  76.9 43.2 %all_to_all.5 = bf16[8,48,4096]{2,1,0:T(8,128)(2,1)S(1)} all-to-all(bf16[8,48,4096]{2,1,0:T(8,128)(2,1)S(1)} %bitcast.4), channel_id=1, replica_groups=mesh['ctx'=64,'kvh'=8] {'kvh'}, dimensions={0} | all-to-all | bytes 6291456 | tf_op jit(solution)/shard_map/all_to_all | solution.py:181
  120.1 1.3 %reduce_sum.12 = bf16[48,4096]{1,0:T(8,128)(2,1)} reduce(bf16[8,48,4096]{2,1,0:T(8,128)(2,1)S(1)} %all_to_all.5, bf16[]{:T(256)} %constant.8.clone.1), dimensions={0}, to_apply=%region_0.0 | reduce | flops 1376256 | bytes 3538946 | tf_op jit(solution)/shard_map/reduce_sum | solution.py:182
  (2 shorter events, 0.0 us)
Async XLA Ops:
  0.0 37.1 %copy-start = (bf16[384,256]{1,0:T(8,128)(2,1)S(1)}, bf16[384,256]{1,0:T(8,128)(2,1)}, u32[]{:S(2)}) copy-start(bf16[384,256]{1,0:T(8,128)(2,1)} %rest_0_.1) | copy-start | bytes 589828
  0.0 36.9 %copy-start.1 = (s32[384]{0:T(512)S(1)}, s32[384]{0:T(512)}, u32[]{:S(2)}) copy-start(s32[384]{0:T(512)} %doc_ref.7) | copy-start | bytes 4612
  0.0 37.1 %copy-start.2 = (bf16[384,512]{1,0:T(8,128)(2,1)S(1)}, bf16[384,512]{1,0:T(8,128)(2,1)}, u32[]{:S(2)}) copy-start(bf16[384,512]{1,0:T(8,128)(2,1)} %query_ref.7) | copy-start | bytes 1179652
  0.0 37.1 %copy-start.3 = (s32[192]{0:T(256)S(1)}, s32[192]{0:T(256)}, u32[]{:S(2)}) copy-start(s32[192]{0:T(256)} %index_ref.7) | copy-start | bytes 2308
  0.0 8.8 %collective-permute-start = (bf16[384,256]{1,0:T(8,128)(2,1)}, bf16[384,256]{1,0:T(8,128)(2,1)S(1)}, u32[]{:S(2)}, u32[]{:S(2)}) collective-permute-start(bf16[384,256]{1,0:T(8,128)(2,1)} %rest_0_.1), channel_id=1, source_target_pairs={{0,32},{8,40},{16,48},{24,56},{32,64},{40,72},{48,80},{56,88},{64,... | collective-permute-start | bytes 589832 | tf_op jit(solution)/shard_map/ppermute | solution.py:156
  9.7 21.5 %collective-permute-start.5 = (bf16[768,256]{1,0:T(8,128)(2,1)S(1)}, bf16[768,256]{1,0:T(8,128)(2,1)S(1)}, u32[]{:S(2)}, u32[]{:S(2)}) collective-permute-start(bf16[768,256]{1,0:T(8,128)(2,1)S(1)} %pad_maximum_fusion.2), channel_id=1, source_target_pairs={{0,16},{8,24},{16,32},{24,40},{32,48},{40,56},{48,64},{56,72},{64,... | collective-permute-start | bytes 1179656 | tf_op jit(solution)/shard_map/ppermute | solution.py:156
  14.9 11.1 %collective-permute-start.1 = (bf16[384,256]{1,0:T(8,128)(2,1)S(1)}, bf16[384,256]{1,0:T(8,128)(2,1)S(1)}, u32[]{:S(2)}, u32[]{:S(2)}) collective-permute-start(bf16[384,256]{1,0:T(8,128)(2,1)S(1)} %collective-permute-done.rest_1_), channel_id=1, source_target_pairs={{0,32},{8,40},{16,48},{24,56},{32,64},{40,72},{48,80},{56,88},{64,... | collective-permute-start | bytes 589832 | tf_op jit(solution)/shard_map/ppermute | solution.py:156
  26.0 15.9 %collective-permute-start.2 = (bf16[384,256]{1,0:T(8,128)(2,1)S(1)}, bf16[384,256]{1,0:T(8,128)(2,1)S(1)}, u32[]{:S(2)}, u32[]{:S(2)}) collective-permute-start(bf16[384,256]{1,0:T(8,128)(2,1)S(1)} %collective-permute-done.1), channel_id=1, source_target_pairs={{0,32},{8,40},{16,48},{24,56},{32,64},{40,72},{48,80},{56,88},{64,... | collective-permute-start | bytes 589832 | tf_op jit(solution)/shard_map/ppermute | solution.py:156
  32.3 13.5 %collective-permute-start.6 = (bf16[1536,256]{1,0:T(8,128)(2,1)S(1)}, bf16[1536,256]{1,0:T(8,128)(2,1)S(1)}, u32[]{:S(2)}, u32[]{:S(2)}) collective-permute-start(bf16[1536,256]{1,0:T(8,128)(2,1)S(1)} %pad_maximum_fusion.1), channel_id=1, source_target_pairs={{0,8},{8,0},{16,24},{24,16},{32,40},{40,32},{48,56},{56,48},{64,72... | collective-permute-start | bytes 2359304 | tf_op jit(solution)/shard_map/ppermute | solution.py:159
  41.9 17.4 %collective-permute-start.4 = (bf16[768,256]{1,0:T(8,128)(2,1)S(1)}, bf16[768,256]{1,0:T(8,128)(2,1)S(1)}, u32[]{:S(2)}, u32[]{:S(2)}) collective-permute-start(bf16[768,256]{1,0:T(8,128)(2,1)S(1)} %constant_dynamic-update-slice_fusion.rest_1_), channel_id=1, source_target_pairs={{0,16},{8,24},{16,32},{24,40},{32,48},{40,56},{48,64},{56,72},{64,... | collective-permute-start | bytes 1179656 | tf_op jit(solution)/shard_map/ppermute | solution.py:156
  43.8 15.5 %collective-permute-start.3 = (bf16[384,256]{1,0:T(8,128)(2,1)S(1)}, bf16[384,256]{1,0:T(8,128)(2,1)S(1)}, u32[]{:S(2)}, u32[]{:S(2)}) collective-permute-start(bf16[384,256]{1,0:T(8,128)(2,1)S(1)} %collective-permute-done.2), channel_id=1, source_target_pairs={{0,32},{8,40},{16,48},{24,56},{32,64},{40,72},{48,80},{56,88},{64,... | collective-permute-start | bytes 589832 | tf_op jit(solution)/shard_map/ppermute | solution.py:156
  59.4 7.9 %collective-permute-start.7 = (bf16[1920,256]{1,0:T(8,128)(2,1)S(1)}, bf16[1920,256]{1,0:T(8,128)(2,1)S(1)}, u32[]{:S(2)}, u32[]{:S(2)}) collective-permute-start(bf16[1920,256]{1,0:T(8,128)(2,1)S(1)} %pad_maximum_fusion), channel_id=1, source_target_pairs={{0,8},{8,0},{16,24},{24,16},{32,40},{40,32},{48,56},{56,48},{64,72... | collective-permute-start | bytes 2949128 | tf_op jit(solution)/shard_map/ppermute | solution.py:159
  67.3 7.7 %copy-start.4 = (bf16[512,4096]{1,0:T(8,128)(2,1)S(1)}, bf16[512,4096]{1,0:T(8,128)(2,1)}, u32[]{:S(2)}) copy-start(bf16[512,4096]{1,0:T(8,128)(2,1)} %param.11) | copy-start | bytes 12582916

commit v5 on v4

v5 whole, which is shorter than its diff:
```python
import functools
import math

import jax
import jax.numpy as jnp
from jax import lax
from jax.experimental import pallas as pl
from jax.experimental.pallas import tpu as pltpu
from jax.sharding import PartitionSpec as P

H = 32
KVH = 8
HD = 128
SBLK = 128
GROUPS = H // KVH
NEG = -1e30
FACTOR = math.log2(math.e) / math.sqrt(HD)
SAFE = 80.0


def attend_kernel(
    counts, plan, first, final, my_ref, doc_ref, index_ref, table_ref, norm_ref, starts_ref, query_ref, *rest
):
    pieces, rest = rest[: len(counts)], rest[len(counts) :]
    if not first:
        rest = rest[2:]
    acc_ref, max_ref, *rest = rest
    if final:
        out_ref, *rest = rest
    bias_ref, held, src_ref, sems = rest
    tok = query_ref.shape[0]
    parts = tok // SBLK
    flag_row = GROUPS * tok
    blocks = len(plan)
    copies = []
    at = 0
    for i, count in enumerate(counts):
        copies.append(pltpu.make_async_copy(pieces[i], held.at[pl.ds(at * tok, count * tok)], sems.at[i]))
        copies[-1].start()
        at += count
    my, low, high = my_ref[0], doc_ref[0], doc_ref[tok - 1]
    for step, (mine, back, crossed) in enumerate(plan):
        src = (my if mine else my ^ 1) - 2 * back
        if crossed:
            src = src - 2 * (my & 2)
        src_ref[step] = src
    if blocks % 2:
        src_ref[blocks] = -1
        held[pl.ds(blocks * tok, tok), :] = jnp.zeros((tok, 2 * HD), held.dtype)
    if first:
        acc_ref[...] = jnp.zeros_like(acc_ref)
    for copy in copies:
        copy.wait()

    def scale_row(step, t):
        return index_ref[jnp.clip(src_ref[step], 0, my) * parts + t]

    def widest(step, most):
        for t in range(parts):
            rows = pl.ds(pl.multiple_of(step * tok + t * SBLK, SBLK), SBLK)
            key = held[rows, :HD].astype(jnp.float32)
            scale = table_ref[scale_row(step, t), 0] * FACTOR
            most = jnp.maximum(most, jnp.sum(key * key, axis=1, keepdims=True) * (scale * scale))
        return most

    most = lax.fori_loop(0, blocks, widest, jnp.zeros((SBLK, 1), jnp.float32))
    small = jnp.max(most) * norm_ref[0] <= SAFE * SAFE
    if first:
        max_ref[...] = jnp.full(max_ref.shape, jnp.where(small, 0.0, NEG), jnp.float32)
    else:
        small = small & (max_ref[flag_row, 0] > 0.0)
    max_ref[pl.ds(flag_row, 8), :] = jnp.full((8, HD), jnp.where(small, 1.0, 0.0), jnp.float32)

    def attend_pair(step, masked, shifted):
        key_scales, value_scales = [], []
        for t in range(2 * parts):
            row = scale_row(step + t // parts, t % parts)
            key_scales.append(jnp.full((1, SBLK), table_ref[row, 0] * FACTOR, jnp.float32))
            value_scales.append(jnp.full((SBLK, HD), table_ref[row, 1], jnp.float32))
        scale = jnp.concatenate(key_scales, 1)
        kv_rows = pl.ds(pl.multiple_of(step * tok, tok), 2 * tok)
        keys = held[kv_rows, :HD]
        values = held[kv_rows, HD:].astype(jnp.float32) * jnp.concatenate(value_scales, 0)
        values = jnp.concatenate([values.astype(jnp.bfloat16), jnp.ones((2 * tok, HD), jnp.bfloat16)], 1)
        if masked:
            column = lax.broadcasted_iota(jnp.int32, (tok, tok), 1)
            last = my * tok + lax.broadcasted_iota(jnp.int32, (tok, tok), 0)
            starts = jnp.concatenate([starts_ref[...]] * (tok // HD), 1)
            for i in range(2):
                key_pos = src_ref[step + i] * tok + column
                seen = (key_pos >= starts) & (key_pos <= last)
                bias_ref[:, i * tok : (i + 1) * tok] = jnp.where(seen, 0.0, NEG)
        for h in range(GROUPS):
            rows = pl.ds(h * tok, tok)
            scores = lax.dot_general(
                query_ref[:, h * HD : (h + 1) * HD],
                keys,
                (((1,), (1,)), ((), ())),
                preferred_element_type=jnp.float32,
            )
            scores = scores * scale
            if masked:
                scores = scores + bias_ref[...]
            if shifted:
                old_max = max_ref[rows, :]
                new_max = jnp.maximum(old_max, jnp.max(scores, axis=1, keepdims=True))
                carry = jnp.exp2(old_max - new_max)
                max_ref[rows, :] = new_max
                scores = scores - jnp.concatenate([new_max] * (2 * tok // HD), 1)
                acc_ref[rows, :] = acc_ref[rows, :] * jnp.concatenate([carry, carry], 1)
            probs = jnp.exp2(scores).astype(jnp.bfloat16)
            acc_ref[rows, :] += jnp.dot(probs, values, preferred_element_type=jnp.float32)

    def one_pair(pair, _):
        step = 2 * pair
        seen, whole = jnp.bool_(False), jnp.bool_(True)
        for i in range(2):
            src = src_ref[step + i]
            seen = seen | ((src >= 0) & (src * tok + tok - 1 >= low) & (src <= my))
            whole = whole & (src >= 0) & (src * tok >= high) & (src < my)

        @pl.when(seen & small & whole)
        def _():
            attend_pair(step, False, False)

        @pl.when(seen & small & jnp.logical_not(whole))
        def _():
            attend_pair(step, True, False)

        @pl.when(seen & jnp.logical_not(small))
        def _():
            attend_pair(step, True, True)

        return 0

    lax.fori_loop(0, (blocks + 1) // 2, one_pair, 0)
    if final:
        for h in range(GROUPS):
            acc = acc_ref[pl.ds(h * tok, tok), :]
            out_ref[:, h * HD : (h + 1) * HD] = (acc[:, :HD] / acc[:, HD:]).astype(jnp.bfloat16)


def attend(common, pieces, plan, state=None, final=False):
    query = common[-1]
    tok = query.shape[0]
    counts = tuple(piece.shape[0] // tok for piece in pieces)
    blocks = sum(counts)
    assert blocks == len(plan)
    even = blocks + blocks % 2
    vmem, smem = pl.BlockSpec(memory_space=pltpu.VMEM), pl.BlockSpec(memory_space=pltpu.SMEM)
    out_shape = (
        jax.ShapeDtypeStruct((GROUPS * tok, 2 * HD), jnp.float32),
        jax.ShapeDtypeStruct((GROUPS * tok + 8, HD), jnp.float32),
    )
    if final:
        out_shape += (jax.ShapeDtypeStruct((tok, GROUPS * HD), jnp.bfloat16),)
    flops = blocks * GROUPS * tok * tok * HD * 4
    return pl.pallas_call(
        functools.partial(attend_kernel, counts, plan, state is None, final),
        out_shape=out_shape,
        in_specs=[smem] * 5
        + [vmem] * 2
        + [pl.BlockSpec(memory_space=pl.ANY)] * len(pieces)
        + [vmem] * (0 if state is None else 2),
        out_specs=(vmem,) * len(out_shape),
        scratch_shapes=[
            pltpu.VMEM((tok, 2 * tok), jnp.float32),
            pltpu.VMEM((even * tok, 2 * HD), jnp.bfloat16),
            pltpu.SMEM((even,), jnp.int32),
            pltpu.SemaphoreType.DMA((len(counts),)),
        ],
        input_output_aliases={} if state is None else {7 + len(pieces): 0, 8 + len(pieces): 1},
        compiler_params=pltpu.CompilerParams(vmem_limit_bytes=40 << 20),
        cost_estimate=pl.CostEstimate(flops=10 * flops, bytes_accessed=4 << 20, transcendentals=0),
    )(*common, *pieces, *(state or ()))


def local(query, keys_values, doc_start, scale_index, scale_table, out_weight):
    tok = query.shape[0]
    ctx_count = lax.axis_size("ctx")
    my = lax.axis_index("ctx").astype(jnp.int32)
    starts = jnp.broadcast_to(doc_start[:, None], (tok, HD))
    squares = jnp.square(query.astype(jnp.float32)).reshape(tok, GROUPS, HD)
    norm = jnp.max(jnp.sum(squares, axis=2))
    common = (my[None], doc_start, scale_index, scale_table, norm[None], starts, query)

    def shifted(block, distance):
        return lax.ppermute(block, "ctx", [(i, i + distance) for i in range(ctx_count - distance)])

    def swapped(block):
        return lax.ppermute(block, "ctx", [(i, i ^ 1) for i in range(ctx_count)])

    def crossed(block):
        return lax.ppermute(block, "ctx", [(i, i ^ 2) for i in range(ctx_count)])

    def after(block, *others):
        return lax.optimization_barrier((block, *others))[0]

    def own(*back):
        return tuple((True, k, False) for k in back)

    def others(plan):
        return tuple((False, k, cross) for _, k, cross in plan)

    from_2 = shifted(keys_values, 4)
    from_02 = jnp.concatenate([keys_values, from_2])
    cross_02 = crossed(from_02)
    from_4 = shifted(from_2, 4)
    from_6 = shifted(from_4, 4)
    from_46 = jnp.concatenate([from_4, from_6])
    cross_46 = crossed(from_46)
    from_8 = shifted(from_6, 4)
    last = [(i, i + 2) for i in range(ctx_count - 2) if i & 2]
    from_7 = lax.ppermute(from_6, "ctx", last)
    plan_02, plan_46, plan_8 = own(0, 2), own(4, 6), own(8)
    cplan_02, cplan_46, cplan_7 = [tuple((True, k, True) for k in ks) for ks in ((-1, 1), (3, 5), (7,))]

    swap_02 = swapped(jnp.concatenate([from_02, cross_02]))
    state = attend(common, [keys_values, from_2], plan_02)
    plan = cplan_02 + plan_46 + others(plan_02 + cplan_02)
    state = attend(common, [cross_02, from_46, swap_02], plan, state)
    swap_46 = swapped(jnp.concatenate([from_46, from_8, from_7, after(cross_46, *state)]))
    state = attend(common, [cross_46, from_8, from_7], cplan_46 + plan_8 + cplan_7, state)
    plan = others(plan_46 + plan_8 + cplan_7 + cplan_46)
    _, _, attn = attend(common, [swap_46], plan, state, True)
    shares = lax.axis_size("kvh")
    partial = jnp.dot(attn, out_weight, preferred_element_type=jnp.float32).astype(jnp.bfloat16)
    pieces = lax.all_to_all(partial.reshape(shares, tok // shares, -1), "kvh", 0, 0)
    return jnp.sum(pieces.astype(jnp.float32), axis=0).astype(jnp.bfloat16)


def solution(mesh):
    placed = (P("ctx", "kvh"), P("ctx", "kvh"), P("ctx"), P(), P(None, "kvh"), P("kvh", None))
    return jax.shard_map(
        local, mesh=mesh, in_specs=placed, out_specs=P(("ctx", "kvh"), None), check_vma=False
    )
```

time: 122 us -> 126 us (1.033)
  the two profiles are of different devices: /device:TPU:229 before, /device:TPU:224 now
where the time goes in v5:
time: 126 us
  blocking collectives  43.8 us (35%)
  starting transfers between devices  34 us (27%)
  Pallas kernels  30.9 us (25%)
  waiting for transfers between devices  9.59 us (8%)
  other arithmetic  4.56 us (4%)
  matrix products  1.88 us (1%)
    all_to_all x1, blocking collectives, local(): lax.all_to_all(partial.reshape(shares, tok // shares, -1), 'kvh', 0, 0)  43.8 us
    pallas_call x4, Pallas kernels, attend(): pl.pallas_call(functools.partial(attend_kernel, counts, plan, state is No...  30.9 us
    ppermute x4, starting transfers between devices, shifted(): lax.ppermute(block, 'ctx', [(i, i + distance) for i in range(ctx_count -...  18 us
    ppermute x2, starting transfers between devices, crossed(): return lax.ppermute(block, 'ctx', [(i, i ^ 2) for i in range(ctx_count)])  10.6 us
    ppermute x4, waiting for transfers between devices, shifted(): lax.ppermute(block, 'ctx', [(i, i + distance) for i in range(ctx_count -...  5.13 us
    ppermute x1, waiting for transfers between devices, local(): from_7 = lax.ppermute(from_6, 'ctx', last)  4.45 us
    ppermute x2, starting transfers between devices, swapped(): return lax.ppermute(block, 'ctx', [(i, i ^ 1) for i in range(ctx_count)])  4.06 us
  transfers between devices with their start and end apart: 9, of which 4 were waited for; matrix products, arithmetic and copies ran while one was open for 2% of the time, Pallas kernels for 17%

profile of v5, /device:TPU:224, one launch (start us, length us, event | category | flops | bytes accessed | tf_op | source)
XLA Modules:
  0.0 125.7 jit_solution(14493763982649610090)
XLA Ops:
  0.0 5.0 %collective-permute-start = (bf16[384,256]{1,0:T(8,128)(2,1)}, bf16[384,256]{1,0:T(8,128)(2,1)S(1)}, u32[]{:S(2)}, u32[]{:S(2)}) collective-permute-start(bf16[384,256]{1,0:T(8,128)(2,1)} %rest_0_.1), channel_id=1, source_target_pairs={{0,32},{8,40},{16,48},{24,56},{32,64},{40,72},{48,80},{56,88},{64,... | collective-permute-start | bytes 589832 | tf_op jit(solution)/shard_map/ppermute | solution.py:188
  5.0 4.5 %collective-permute-done.rest_1_ = bf16[384,256]{1,0:T(8,128)(2,1)S(1)} collective-permute-done((bf16[384,256]{1,0:T(8,128)(2,1)}, bf16[384,256]{1,0:T(8,128)(2,1)S(1)}, u32[]{:S(2)}, u32[]{:S(2)}) %collective-permute-start) | collective-permute-done | bytes 196640 | tf_op jit(solution)/shard_map/ppermute | solution.py:188
  9.5 1.0 pad_maximum_fusion.1
  10.4 0.0 copy-start.4
  10.5 4.9 %collective-permute-start.6 = (bf16[768,256]{1,0:T(8,128)(2,1)S(1)}, bf16[768,256]{1,0:T(8,128)(2,1)S(1)}, u32[]{:S(2)}, u32[]{:S(2)}) collective-permute-start(bf16[768,256]{1,0:T(8,128)(2,1)S(1)} %pad_maximum_fusion.1), channel_id=1, source_target_pairs={{0,16},{8,24},{16,0},{24,8},{32,48},{40,56},{48,32},{56,40},{64,80... | collective-permute-start | bytes 1179656 | tf_op jit(solution)/shard_map/ppermute | solution.py:194
  15.4 5.5 %collective-permute-start.1 = (bf16[384,256]{1,0:T(8,128)(2,1)S(1)}, bf16[384,256]{1,0:T(8,128)(2,1)S(1)}, u32[]{:S(2)}, u32[]{:S(2)}) collective-permute-start(bf16[384,256]{1,0:T(8,128)(2,1)S(1)} %collective-permute-done.rest_1_), channel_id=1, source_target_pairs={{0,32},{8,40},{16,48},{24,56},{32,64},{40,72},{48,80},{56,88},{64,... | collective-permute-start | bytes 589832 | tf_op jit(solution)/shard_map/ppermute | solution.py:188
  20.9 1.1 convert_multiply_fusion
  22.0 0.0 copy-start
  22.0 0.3 reshape.7
  22.3 0.0 copy-done.4
  22.3 0.0 copy-start.2
  22.3 0.0 copy-start.1
  22.3 0.0 copy-start.3
  22.3 0.1 copy.25.table_ref
  22.4 0.5 reduce_sum.21
  22.9 0.7 reduce_max.9
  23.6 0.5 collective-permute-done.1
  24.1 5.6 %collective-permute-start.2 = (bf16[384,256]{1,0:T(8,128)(2,1)S(1)}, bf16[384,256]{1,0:T(8,128)(2,1)S(1)}, u32[]{:S(2)}, u32[]{:S(2)}) collective-permute-start(bf16[384,256]{1,0:T(8,128)(2,1)S(1)} %collective-permute-done.1), channel_id=1, source_target_pairs={{0,32},{8,40},{16,48},{24,56},{32,64},{40,72},{48,80},{56,88},{64,... | collective-permute-start | bytes 589832 | tf_op jit(solution)/shard_map/ppermute | solution.py:188
  29.7 0.0 collective-permute-done.6.rest_0_
  29.7 0.0 copy-done
  29.7 0.1 pad_maximum_fusion
  29.7 1.9 %collective-permute-start.7 = (bf16[1536,256]{1,0:T(8,128)(2,1)S(1)}, bf16[1536,256]{1,0:T(8,128)(2,1)S(1)}, u32[]{:S(2)}, u32[]{:S(2)}) collective-permute-start(bf16[1536,256]{1,0:T(8,128)(2,1)S(1)} %pad_maximum_fusion), channel_id=1, source_target_pairs={{0,8},{8,0},{16,24},{24,16},{32,40},{40,32},{48,56},{56,48},{64,72... | collective-permute-start | bytes 2359304 | tf_op jit(solution)/shard_map/ppermute | solution.py:191
  31.7 0.0 copy-done.2
  31.7 0.1 broadcast_in_dim.14.starts_ref
  31.8 0.0 copy-done.1
  31.8 0.0 copy-done.3
  31.8 4.8 %shard_map.64 = (f32[1536,256]{1,0:T(8,128)S(1)}, f32[1544,128]{1,0:T(8,128)S(1)}) custom-call(s32[1]{0:T(128)} %bitcast.my_ref, s32[384]{0:T(512)S(1)} %copy-done.2, s32[192]{0:T(256)S(1)} %copy-done.3, f32[64,2]{1,0:T(8,128)S(1)} %copy.25.table_ref, f32[1]{0:T(128)} %bitcast.1.norm_ref, s32[384,128]{1,0:T(8,128)S(1)} %broadcast_in_dim.14.starts_ref, ...), custom_call_target="tpu_custom_call" | custom-call | flops 6039797760 | bytes 4194304 | tf_op jit(solution)/shard_map/pallas_call | solution.py:158
  36.6 0.0 collective-permute-done.2
  36.6 1.9 %collective-permute-start.3 = (bf16[384,256]{1,0:T(8,128)(2,1)S(1)}, bf16[384,256]{1,0:T(8,128)(2,1)S(1)}, u32[]{:S(2)}, u32[]{:S(2)}) collective-permute-start(bf16[384,256]{1,0:T(8,128)(2,1)S(1)} %collective-permute-done.2), channel_id=1, source_target_pairs={{0,32},{8,40},{16,48},{24,56},{32,64},{40,72},{48,80},{56,88},{64,... | collective-permute-start | bytes 589832 | tf_op jit(solution)/shard_map/ppermute | solution.py:188
  38.6 1.3 %collective-permute-start.4 = (bf16[384,256]{1,0:T(8,128)(2,1)S(1)}, bf16[384,256]{1,0:T(8,128)(2,1)S(1)}, u32[]{:S(2)}, u32[]{:S(2)}) collective-permute-start(bf16[384,256]{1,0:T(8,128)(2,1)S(1)} %collective-permute-done.2), channel_id=1, source_target_pairs={{16,32},{24,40},{48,64},{56,72},{80,96},{88,104},{112,128},{120,13... | collective-permute-start | bytes 589832 | tf_op jit(solution)/shard_map/ppermute | solution.py:214
  39.9 5.7 %collective-permute-start.5 = (bf16[768,256]{1,0:T(8,128)(2,1)S(1)}, bf16[768,256]{1,0:T(8,128)(2,1)S(1)}, u32[]{:S(2)}, u32[]{:S(2)}) collective-permute-start(bf16[768,256]{1,0:T(8,128)(2,1)S(1)} %get-tuple-element.21.rest_1_), channel_id=1, source_target_pairs={{0,16},{8,24},{16,0},{24,8},{32,48},{40,56},{48,32},{56,40},{64,80... | collective-permute-start | bytes 1179656 | tf_op jit(solution)/shard_map/ppermute | solution.py:194
  45.6 0.2 collective-permute-done.3.rest_1_
  45.8 4.4 %collective-permute-done.4.rest_2_ = bf16[384,256]{1,0:T(8,128)(2,1)S(1)} collective-permute-done((bf16[384,256]{1,0:T(8,128)(2,1)S(1)}, bf16[384,256]{1,0:T(8,128)(2,1)S(1)}, u32[]{:S(2)}, u32[]{:S(2)}) %collective-permute-start.4) | collective-permute-done | bytes 196640 | tf_op jit(solution)/shard_map/ppermute | solution.py:214
  50.3 0.0 collective-permute-done.7.rest_2_
  50.3 11.6 %shard_map.65 = (f32[1536,256]{1,0:T(8,128)S(1)}, f32[1544,128]{1,0:T(8,128)S(1)}) custom-call(s32[1]{0:T(128)} %bitcast.my_ref, s32[384]{0:T(512)S(1)} %copy-done.2, s32[192]{0:T(256)S(1)} %copy-done.3, f32[64,2]{1,0:T(8,128)S(1)} %copy.25.table_ref, f32[1]{0:T(128)} %bitcast.1.norm_ref, ...), custom_call_target="tpu_custom_call", output_to_operand_aliasing={{0}: (10, {}), {1}: (11, {})} | custom-call | flops 24159191040 | bytes 4194304 | tf_op jit(solution)/shard_map/pallas_call | solution.py:158
  62.0 0.0 collective-permute-done.5.rest_0_
  62.0 2.1 %collective-permute-start.8 = (bf16[2304,256]{1,0:T(8,128)(2,1)S(1)}, bf16[2304,256]{1,0:T(8,128)(2,1)S(1)}, u32[]{:S(2)}, u32[]{:S(2)}) collective-permute-start(bf16[2304,256]{1,0:T(8,128)(2,1)S(1)} %constant_dynamic-update-slice_fusion.2), channel_id=1, source_target_pairs={{0,8},{8,0},{16,24},{24,16},{32,40},{40,32},{48,56},{56,48},{64,72... | collective-permute-start | bytes 3538952 | tf_op jit(solution)/shard_map/ppermute | solution.py:191
  64.2 5.2 %shard_map.66 = (f32[1536,256]{1,0:T(8,128)S(1)}, f32[1544,128]{1,0:T(8,128)S(1)}) custom-call(s32[1]{0:T(128)} %bitcast.my_ref, s32[384]{0:T(512)S(1)} %copy-done.2, s32[192]{0:T(256)S(1)} %copy-done.3, f32[64,2]{1,0:T(8,128)S(1)} %copy.25.table_ref, f32[1]{0:T(128)} %bitcast.1.norm_ref, ...), custom_call_target="tpu_custom_call", output_to_operand_aliasing={{0}: (10, {}), {1}: (11, {})} | custom-call | flops 12079595520 | bytes 4194304 | tf_op jit(solution)/shard_map/pallas_call | solution.py:158
  69.3 0.0 collective-permute-done.8.rest_0_
  69.3 0.0 copy-start.5
  69.3 9.3 %shard_map.67 = (f32[1536,256]{1,0:T(8,128)S(1)}, f32[1544,128]{1,0:T(8,128)S(1)}, bf16[384,512]{1,0:T(8,128)(2,1)S(1)}) custom-call(s32[1]{0:T(128)} %bitcast.my_ref, s32[384]{0:T(512)S(1)} %copy-done.2, s32[192]{0:T(256)S(1)} %copy-done.3, f32[64,2]{1,0:T(8,128)S(1)} %copy.25.table_ref, ...), custom_call_target="tpu_custom_call", output_to_operand_aliasing={{0}: (8, {}), {1}: (9, {})} | custom-call | flops 18119393280 | bytes 4194304 | tf_op jit(solution)/shard_map/pallas_call | solution.py:158
  78.7 0.0 copy-done.5
  78.7 1.9 %convolution_convert_fusion = bf16[384,4096]{1,0:T(8,128)(2,1)S(1)} fusion(bf16[384,512]{1,0:T(8,128)(2,1)S(1)} %get-tuple-element.20, bf16[512,4096]{1,0:T(8,128)(2,1)S(1)} %copy-done.5), kind=kOutput, calls=%fused_computation | convolution fusion | flops 1612185600 | bytes 7733248 | tf_op jit(solution)/shard_map/dot_general | solution.py:227
  80.6 43.8 %all_to_all.5 = bf16[8,48,4096]{2,1,0:T(8,128)(2,1)S(1)} all-to-all(bf16[8,48,4096]{2,1,0:T(8,128)(2,1)S(1)} %bitcast.5), channel_id=1, replica_groups=mesh['ctx'=64,'kvh'=8] {'kvh'}, dimensions={0} | all-to-all | bytes 6291456 | tf_op jit(solution)/shard_map/all_to_all | solution.py:228
  124.4 1.3 %reduce_sum.22 = bf16[48,4096]{1,0:T(8,128)(2,1)} reduce(bf16[8,48,4096]{2,1,0:T(8,128)(2,1)S(1)} %all_to_all.5, bf16[]{:T(256)} %constant.11.clone.1), dimensions={0}, to_apply=%region_2.0 | reduce | flops 1376256 | bytes 3538946 | tf_op jit(solution)/shard_map/reduce_sum | solution.py:229
  (5 shorter events, 0.1 us)
Async XLA Ops:
  0.0 9.5 %collective-permute-start = (bf16[384,256]{1,0:T(8,128)(2,1)}, bf16[384,256]{1,0:T(8,128)(2,1)S(1)}, u32[]{:S(2)}, u32[]{:S(2)}) collective-permute-start(bf16[384,256]{1,0:T(8,128)(2,1)} %rest_0_.1), channel_id=1, source_target_pairs={{0,32},{8,40},{16,48},{24,56},{32,64},{40,72},{48,80},{56,88},{64,... | collective-permute-start | bytes 589832 | tf_op jit(solution)/shard_map/ppermute | solution.py:188
  10.4 11.8 %copy-start.4 = (f32[64,2]{0,1:T(2,128)S(1)}, f32[64,2]{0,1:T(2,128)}, u32[]{:S(2)}) copy-start(f32[64,2]{0,1:T(2,128)} %param.10) | copy-start | bytes 1540
  10.5 19.2 %collective-permute-start.6 = (bf16[768,256]{1,0:T(8,128)(2,1)S(1)}, bf16[768,256]{1,0:T(8,128)(2,1)S(1)}, u32[]{:S(2)}, u32[]{:S(2)}) collective-permute-start(bf16[768,256]{1,0:T(8,128)(2,1)S(1)} %pad_maximum_fusion.1), channel_id=1, source_target_pairs={{0,16},{8,24},{16,0},{24,8},{32,48},{40,56},{48,32},{56,40},{64,80... | collective-permute-start | bytes 1179656 | tf_op jit(solution)/shard_map/ppermute | solution.py:194
  15.4 8.7 %collective-permute-start.1 = (bf16[384,256]{1,0:T(8,128)(2,1)S(1)}, bf16[384,256]{1,0:T(8,128)(2,1)S(1)}, u32[]{:S(2)}, u32[]{:S(2)}) collective-permute-start(bf16[384,256]{1,0:T(8,128)(2,1)S(1)} %collective-permute-done.rest_1_), channel_id=1, source_target_pairs={{0,32},{8,40},{16,48},{24,56},{32,64},{40,72},{48,80},{56,88},{64,... | collective-permute-start | bytes 589832 | tf_op jit(solution)/shard_map/ppermute | solution.py:188
  22.0 7.7 %copy-start = (bf16[384,256]{1,0:T(8,128)(2,1)S(1)}, bf16[384,256]{1,0:T(8,128)(2,1)}, u32[]{:S(2)}) copy-start(bf16[384,256]{1,0:T(8,128)(2,1)} %rest_0_.1) | copy-start | bytes 589828
  22.3 9.4 %copy-start.2 = (s32[384]{0:T(512)S(1)}, s32[384]{0:T(512)}, u32[]{:S(2)}) copy-start(s32[384]{0:T(512)} %doc_ref.7) | copy-start | bytes 4612
  22.3 9.5 %copy-start.1 = (bf16[384,512]{1,0:T(8,128)(2,1)S(1)}, bf16[384,512]{1,0:T(8,128)(2,1)}, u32[]{:S(2)}) copy-start(bf16[384,512]{1,0:T(8,128)(2,1)} %query_ref.7) | copy-start | bytes 1179652
  22.3 9.5 %copy-start.3 = (s32[192]{0:T(256)S(1)}, s32[192]{0:T(256)}, u32[]{:S(2)}) copy-start(s32[192]{0:T(256)} %index_ref.7) | copy-start | bytes 2308
  24.1 12.6 %collective-permute-start.2 = (bf16[384,256]{1,0:T(8,128)(2,1)S(1)}, bf16[384,256]{1,0:T(8,128)(2,1)S(1)}, u32[]{:S(2)}, u32[]{:S(2)}) collective-permute-start(bf16[384,256]{1,0:T(8,128)(2,1)S(1)} %collective-permute-done.1), channel_id=1, source_target_pairs={{0,32},{8,40},{16,48},{24,56},{32,64},{40,72},{48,80},{56,88},{64,... | collective-permute-start | bytes 589832 | tf_op jit(solution)/shard_map/ppermute | solution.py:188
  29.7 20.6 %collective-permute-start.7 = (bf16[1536,256]{1,0:T(8,128)(2,1)S(1)}, bf16[1536,256]{1,0:T(8,128)(2,1)S(1)}, u32[]{:S(2)}, u32[]{:S(2)}) collective-permute-start(bf16[1536,256]{1,0:T(8,128)(2,1)S(1)} %pad_maximum_fusion), channel_id=1, source_target_pairs={{0,8},{8,0},{16,24},{24,16},{32,40},{40,32},{48,56},{56,48},{64,72... | collective-permute-start | bytes 2359304 | tf_op jit(solution)/shard_map/ppermute | solution.py:191
  36.6 9.2 %collective-permute-start.3 = (bf16[384,256]{1,0:T(8,128)(2,1)S(1)}, bf16[384,256]{1,0:T(8,128)(2,1)S(1)}, u32[]{:S(2)}, u32[]{:S(2)}) collective-permute-start(bf16[384,256]{1,0:T(8,128)(2,1)S(1)} %collective-permute-done.2), channel_id=1, source_target_pairs={{0,32},{8,40},{16,48},{24,56},{32,64},{40,72},{48,80},{56,88},{64,... | collective-permute-start | bytes 589832 | tf_op jit(solution)/shard_map/ppermute | solution.py:188
  38.6 11.7 %collective-permute-start.4 = (bf16[384,256]{1,0:T(8,128)(2,1)S(1)}, bf16[384,256]{1,0:T(8,128)(2,1)S(1)}, u32[]{:S(2)}, u32[]{:S(2)}) collective-permute-start(bf16[384,256]{1,0:T(8,128)(2,1)S(1)} %collective-permute-done.2), channel_id=1, source_target_pairs={{16,32},{24,40},{48,64},{56,72},{80,96},{88,104},{112,128},{120,13... | collective-permute-start | bytes 589832 | tf_op jit(solution)/shard_map/ppermute | solution.py:214
  39.9 22.0 %collective-permute-start.5 = (bf16[768,256]{1,0:T(8,128)(2,1)S(1)}, bf16[768,256]{1,0:T(8,128)(2,1)S(1)}, u32[]{:S(2)}, u32[]{:S(2)}) collective-permute-start(bf16[768,256]{1,0:T(8,128)(2,1)S(1)} %get-tuple-element.21.rest_1_), channel_id=1, source_target_pairs={{0,16},{8,24},{16,0},{24,8},{32,48},{40,56},{48,32},{56,40},{64,80... | collective-permute-start | bytes 1179656 | tf_op jit(solution)/shard_map/ppermute | solution.py:194
  62.0 7.3 %collective-permute-start.8 = (bf16[2304,256]{1,0:T(8,128)(2,1)S(1)}, bf16[2304,256]{1,0:T(8,128)(2,1)S(1)}, u32[]{:S(2)}, u32[]{:S(2)}) collective-permute-start(bf16[2304,256]{1,0:T(8,128)(2,1)S(1)} %constant_dynamic-update-slice_fusion.2), channel_id=1, source_target_pairs={{0,8},{8,0},{16,24},{24,16},{32,40},{40,32},{48,56},{56,48},{64,72... | collective-permute-start | bytes 3538952 | tf_op jit(solution)/shard_map/ppermute | solution.py:191
  69.3 9.4 %copy-start.5 = (bf16[512,4096]{1,0:T(8,128)(2,1)S(1)}, bf16[512,4096]{1,0:T(8,128)(2,1)}, u32[]{:S(2)}) copy-start(bf16[512,4096]{1,0:T(8,128)(2,1)} %param.11) | copy-start | bytes 12582916

commit v6 on v5

--- a/solution.py
+++ b/solution.py
@@ -55,15 +55,17 @@
     def scale_row(step, t):
         return index_ref[jnp.clip(src_ref[step], 0, my) * parts + t]
 
+    ones = jnp.ones((HD, HD), jnp.bfloat16)
+
     def widest(step, most):
+        key = held[pl.ds(pl.multiple_of(step * tok, tok), tok), :HD]
+        squares = jnp.dot(key * key, ones, preferred_element_type=jnp.float32)
         for t in range(parts):
-            rows = pl.ds(pl.multiple_of(step * tok + t * SBLK, SBLK), SBLK)
-            key = held[rows, :HD].astype(jnp.float32)
-            scale = table_ref[scale_row(step, t), 0] * FACTOR
-            most = jnp.maximum(most, jnp.sum(key * key, axis=1, keepdims=True) * (scale * scale))
+            scale = table_ref[0, scale_row(step, t)] * FACTOR
+            most = jnp.maximum(most, squares[t * SBLK : (t + 1) * SBLK] * (scale * scale))
         return most
 
-    most = lax.fori_loop(0, blocks, widest, jnp.zeros((SBLK, 1), jnp.float32))
+    most = lax.fori_loop(0, blocks, widest, jnp.zeros((SBLK, HD), jnp.float32))
     small = jnp.max(most) * norm_ref[0] <= SAFE * SAFE
     if first:
         max_ref[...] = jnp.full(max_ref.shape, jnp.where(small, 0.0, NEG), jnp.float32)
@@ -75,8 +77,8 @@
         key_scales, value_scales = [], []
         for t in range(2 * parts):
             row = scale_row(step + t // parts, t % parts)
-            key_scales.append(jnp.full((1, SBLK), table_ref[row, 0] * FACTOR, jnp.float32))
-            value_scales.append(jnp.full((SBLK, HD), table_ref[row, 1], jnp.float32))
+            key_scales.append(jnp.full((1, SBLK), table_ref[0, row] * FACTOR, jnp.float32))
+            value_scales.append(jnp.full((SBLK, HD), table_ref[1, row], jnp.float32))
         scale = jnp.concatenate(key_scales, 1)
         kv_rows = pl.ds(pl.multiple_of(step * tok, tok), 2 * tok)
         keys = held[kv_rows, :HD]
@@ -182,7 +184,7 @@
     starts = jnp.broadcast_to(doc_start[:, None], (tok, HD))
     squares = jnp.square(query.astype(jnp.float32)).reshape(tok, GROUPS, HD)
     norm = jnp.max(jnp.sum(squares, axis=2))
-    common = (my[None], doc_start, scale_index, scale_table, norm[None], starts, query)
+    common = (my[None], doc_start, scale_index, scale_table.T, norm[None], starts, query)
 
     def shifted(block, distance):
         return lax.ppermute(block, "ctx", [(i, i + distance) for i in range(ctx_count - distance)])
@@ -203,22 +205,22 @@
         return tuple((False, k, cross) for _, k, cross in plan)
 
     from_2 = shifted(keys_values, 4)
-    from_02 = jnp.concatenate([keys_values, from_2])
+    from_02 = jnp.concatenate([keys_values, after(from_2, norm, starts)])
+    from_46 = shifted(from_02, 8)
     cross_02 = crossed(from_02)
-    from_4 = shifted(from_2, 4)
-    from_6 = shifted(from_4, 4)
-    from_46 = jnp.concatenate([from_4, from_6])
+    last = [(i, i + 2) for i in range(ctx_count - 2) if i & 2]
+    plan_02, plan_46, plan_8 = own(0, 2), own(4, 6), own(8)
+    cplan_02, cplan_46, cplan_7 = [tuple((True, k, True) for k in ks) for ks in ((-1, 1), (3, 5), (7,))]
+
+    swap_02 = swapped(jnp.concatenate([from_02, cross_02]))
+    state = attend(common, [from_02, cross_02], plan_02 + cplan_02)
+    from_46 = after(from_46, *state)
+    from_6 = from_46[tok:]
     cross_46 = crossed(from_46)
     from_8 = shifted(from_6, 4)
-    last = [(i, i + 2) for i in range(ctx_count - 2) if i & 2]
     from_7 = lax.ppermute(from_6, "ctx", last)
-    plan_02, plan_46, plan_8 = own(0, 2), own(4, 6), own(8)
-    cplan_02, cplan_46, cplan_7 = [tuple((True, k, True) for k in ks) for ks in ((-1, 1), (3, 5), (7,))]
-
-    swap_02 = swapped(jnp.concatenate([from_02, cross_02]))
-    state = attend(common, [keys_values, from_2], plan_02)
-    plan = cplan_02 + plan_46 + others(plan_02 + cplan_02)
-    state = attend(common, [cross_02, from_46, swap_02], plan, state)
+    plan = plan_46 + others(plan_02 + cplan_02)
+    state = attend(common, [from_46, swap_02], plan, state)
     swap_46 = swapped(jnp.concatenate([from_46, from_8, from_7, after(cross_46, *state)]))
     state = attend(common, [cross_46, from_8, from_7], cplan_46 + plan_8 + cplan_7, state)
     plan = others(plan_46 + plan_8 + cplan_7 + cplan_46)

time: 126 us -> 120 us (0.952)
  the two profiles are of different devices: /device:TPU:224 before, /device:TPU:68 now
where the time goes in v6:
time: 120 us; the launch traced here: 119 us
  blocking collectives  44.6 us (37%)
  starting transfers between devices  31.9 us (27%)
  Pallas kernels  27.5 us (23%)
  waiting for transfers between devices  9.11 us (8%)
  other arithmetic  3.72 us (3%)
  matrix products  1.8 us (2%)
    all_to_all x1, blocking collectives, local(): lax.all_to_all(partial.reshape(shares, tok // shares, -1), 'kvh', 0, 0)  44.6 us
    pallas_call x4, Pallas kernels, attend(): pl.pallas_call(functools.partial(attend_kernel, counts, plan, state is No...  27.5 us
    ppermute x3, starting transfers between devices, shifted(): lax.ppermute(block, 'ctx', [(i, i + distance) for i in range(ctx_count -...  13.3 us
    ppermute x2, starting transfers between devices, crossed(): return lax.ppermute(block, 'ctx', [(i, i ^ 2) for i in range(ctx_count)])  7.33 us
    ppermute x1, starting transfers between devices, local(): from_7 = lax.ppermute(from_6, 'ctx', last)  7.18 us
    ppermute x3, waiting for transfers between devices, shifted(): lax.ppermute(block, 'ctx', [(i, i + distance) for i in range(ctx_count -...  5.76 us
    ppermute x2, starting transfers between devices, swapped(): return lax.ppermute(block, 'ctx', [(i, i ^ 1) for i in range(ctx_count)])  4.06 us
    ppermute x2, waiting for transfers between devices, crossed(): return lax.ppermute(block, 'ctx', [(i, i ^ 2) for i in range(ctx_count)])  3.35 us
  transfers between devices with their start and end apart: 8, of which 3 were waited for; matrix products, arithmetic and copies ran while one was open for 2% of the time, Pallas kernels for 17%

profile of v6, /device:TPU:68, one launch (start us, length us, event | category | flops | bytes accessed | tf_op | source)
XLA Modules:
  0.0 119.5 jit_solution(12372491450729587027)
XLA Ops:
  0.0 3.8 %collective-permute-start = (bf16[384,256]{1,0:T(8,128)(2,1)}, bf16[384,256]{1,0:T(8,128)(2,1)S(1)}, u32[]{:S(2)}, u32[]{:S(2)}) collective-permute-start(bf16[384,256]{1,0:T(8,128)(2,1)} %param.7), channel_id=1, source_target_pairs={{0,32},{8,40},{16,48},{24,56},{32,64},{40,72},{48,80},{56,88},{64,... | collective-permute-start | bytes 589832 | tf_op jit(solution)/shard_map/ppermute | solution.py:190
  3.8 1.1 convert_multiply_fusion
  4.9 0.0 copy-start.4
  4.9 0.0 copy-start.1
  4.9 0.3 reshape.7
  5.2 0.5 reduce_sum.21
  5.7 0.0 copy-start
  5.7 0.0 copy-start.2
  5.7 0.0 copy-start.3
  5.7 0.7 reduce_max.9
  6.4 0.0 copy-done.4
  6.5 2.3 %collective-permute-done = bf16[384,256]{1,0:T(8,128)(2,1)S(1)} collective-permute-done((bf16[384,256]{1,0:T(8,128)(2,1)}, bf16[384,256]{1,0:T(8,128)(2,1)S(1)}, u32[]{:S(2)}, u32[]{:S(2)}) %collective-permute-start) | collective-permute-done | bytes 196640 | tf_op jit(solution)/shard_map/ppermute | solution.py:190
  8.7 0.0 copy-done.1
  8.7 0.1 broadcast_in_dim.14.starts_ref
  8.9 2.4 %collective-permute-start.2 = (bf16[768,256]{1,0:T(8,128)(2,1)S(1)}, bf16[768,256]{1,0:T(8,128)(2,1)S(1)}, u32[]{:S(2)}, u32[]{:S(2)}) collective-permute-start(bf16[768,256]{1,0:T(8,128)(2,1)S(1)} %constant_dynamic-update-slice_fusion.rest_0_), channel_id=1, source_target_pairs={{0,16},{8,24},{16,0},{24,8},{32,48},{40,56},{48,32},{56,40},{64,80... | collective-permute-start | bytes 1179656 | tf_op jit(solution)/shard_map/ppermute | solution.py:196
  11.3 7.6 %collective-permute-start.1 = (bf16[768,256]{1,0:T(8,128)(2,1)S(1)}, bf16[768,256]{1,0:T(8,128)(2,1)S(1)}, u32[]{:S(2)}, u32[]{:S(2)}) collective-permute-start(bf16[768,256]{1,0:T(8,128)(2,1)S(1)} %constant_dynamic-update-slice_fusion.rest_0_), channel_id=1, source_target_pairs={{0,64},{8,72},{16,80},{24,88},{32,96},{40,104},{48,112},{56,120},{... | collective-permute-start | bytes 1179656 | tf_op jit(solution)/shard_map/ppermute | solution.py:190
  18.9 3.3 %collective-permute-done.2.rest_1_ = bf16[768,256]{1,0:T(8,128)(2,1)S(1)} collective-permute-done((bf16[768,256]{1,0:T(8,128)(2,1)S(1)}, bf16[768,256]{1,0:T(8,128)(2,1)S(1)}, u32[]{:S(2)}, u32[]{:S(2)}) %collective-permute-start.2) | collective-permute-done | bytes 393248 | tf_op jit(solution)/shard_map/ppermute | solution.py:196
  22.3 0.1 pad_maximum_fusion.1
  22.3 1.9 %collective-permute-start.6 = (bf16[1536,256]{1,0:T(8,128)(2,1)S(1)}, bf16[1536,256]{1,0:T(8,128)(2,1)S(1)}, u32[]{:S(2)}, u32[]{:S(2)}) collective-permute-start(bf16[1536,256]{1,0:T(8,128)(2,1)S(1)} %pad_maximum_fusion.1), channel_id=1, source_target_pairs={{0,8},{8,0},{16,24},{24,16},{32,40},{40,32},{48,56},{56,48},{64,72... | collective-permute-start | bytes 2359304 | tf_op jit(solution)/shard_map/ppermute | solution.py:193
  24.2 0.0 copy-done
  24.3 0.0 copy-done.2
  24.3 0.0 copy-done.3
  24.3 6.7 %shard_map.64 = (f32[1536,256]{1,0:T(8,128)S(1)}, f32[1544,128]{1,0:T(8,128)S(1)}) custom-call(s32[1]{0:T(128)} %bitcast.my_ref, s32[384]{0:T(512)S(1)} %copy-done.1, s32[192]{0:T(256)S(1)} %copy-done.2, f32[2,64]{1,0:T(2,128)S(1)} %bitcast.6, f32[1]{0:T(128)} %bitcast.2.norm_ref, s32[384,128]{1,0:T(8,128)S(1)} %broadcast_in_dim.14.starts_ref, ...), custom_call_target="tpu_custom_call" | custom-call | flops 12079595520 | bytes 4194304 | tf_op jit(solution)/shard_map/pallas_call | solution.py:160
  31.0 3.5 %collective-permute-done.1.rest_0_ = bf16[768,256]{1,0:T(8,128)(2,1)S(1)} collective-permute-done((bf16[768,256]{1,0:T(8,128)(2,1)S(1)}, bf16[768,256]{1,0:T(8,128)(2,1)S(1)}, u32[]{:S(2)}, u32[]{:S(2)}) %collective-permute-start.1) | collective-permute-done | bytes 393248 | tf_op jit(solution)/shard_map/ppermute | solution.py:190
  34.5 4.9 %collective-permute-start.5 = (bf16[768,256]{1,0:T(8,128)(2,1)S(1)}, bf16[768,256]{1,0:T(8,128)(2,1)S(1)}, u32[]{:S(2)}, u32[]{:S(2)}) collective-permute-start(bf16[768,256]{1,0:T(8,128)(2,1)S(1)} %collective-permute-done.1.rest_0_), channel_id=1, source_target_pairs={{0,16},{8,24},{16,0},{24,8},{32,48},{40,56},{48,32},{56,40},{64,80... | collective-permute-start | bytes 1179656 | tf_op jit(solution)/shard_map/ppermute | solution.py:196
  39.4 1.9 %collective-permute-start.3 = (bf16[384,256]{1,0:T(8,128)(2,1)S(1)}, bf16[384,256]{1,0:T(8,128)(2,1)S(1)}, u32[]{:S(2)}, u32[]{:S(2)}) collective-permute-start(bf16[384,256]{1,0:T(8,128)(2,1)S(1)} %slice.3), channel_id=1, source_target_pairs={{0,32},{8,40},{16,48},{24,56},{32,64},{40,72},{48,80},{56,88},{64,... | collective-permute-start | bytes 589832 | tf_op jit(solution)/shard_map/ppermute | solution.py:190
  41.4 7.2 %collective-permute-start.4 = (bf16[384,256]{1,0:T(8,128)(2,1)S(1)}, bf16[384,256]{1,0:T(8,128)(2,1)S(1)}, u32[]{:S(2)}, u32[]{:S(2)}) collective-permute-start(bf16[384,256]{1,0:T(8,128)(2,1)S(1)} %slice.3), channel_id=1, source_target_pairs={{16,32},{24,40},{48,64},{56,72},{80,96},{88,104},{112,128},{120,13... | collective-permute-start | bytes 589832 | tf_op jit(solution)/shard_map/ppermute | solution.py:221
  48.6 0.0 collective-permute-done.6.rest_1_
  48.6 8.9 %shard_map.65 = (f32[1536,256]{1,0:T(8,128)S(1)}, f32[1544,128]{1,0:T(8,128)S(1)}) custom-call(s32[1]{0:T(128)} %bitcast.my_ref, s32[384]{0:T(512)S(1)} %copy-done.1, s32[192]{0:T(256)S(1)} %copy-done.2, f32[2,64]{1,0:T(2,128)S(1)} %bitcast.7, f32[1]{0:T(128)} %bitcast.2.norm_ref, ...), custom_call_target="tpu_custom_call", output_to_operand_aliasing={{0}: (9, {}), {1}: (10, {})} | custom-call | flops 18119393280 | bytes 4194304 | tf_op jit(solution)/shard_map/pallas_call | solution.py:160
  57.4 0.0 collective-permute-done.5.rest_0_
  57.4 0.0 collective-permute-done.3.rest_1_
  57.5 0.0 collective-permute-done.4.rest_2_
  57.5 0.1 pad_maximum_fusion
  57.6 2.1 %collective-permute-start.7 = (bf16[2304,256]{1,0:T(8,128)(2,1)S(1)}, bf16[2304,256]{1,0:T(8,128)(2,1)S(1)}, u32[]{:S(2)}, u32[]{:S(2)}) collective-permute-start(bf16[2304,256]{1,0:T(8,128)(2,1)S(1)} %pad_maximum_fusion), channel_id=1, source_target_pairs={{0,8},{8,0},{16,24},{24,16},{32,40},{40,32},{48,56},{56,48},{64,72... | collective-permute-start | bytes 3538952 | tf_op jit(solution)/shard_map/ppermute | solution.py:193
  59.7 4.9 %shard_map.66 = (f32[1536,256]{1,0:T(8,128)S(1)}, f32[1544,128]{1,0:T(8,128)S(1)}) custom-call(s32[1]{0:T(128)} %bitcast.my_ref, s32[384]{0:T(512)S(1)} %copy-done.1, s32[192]{0:T(256)S(1)} %copy-done.2, f32[2,64]{1,0:T(2,128)S(1)} %bitcast.8, f32[1]{0:T(128)} %bitcast.2.norm_ref, ...), custom_call_target="tpu_custom_call", output_to_operand_aliasing={{0}: (10, {}), {1}: (11, {})} | custom-call | flops 12079595520 | bytes 4194304 | tf_op jit(solution)/shard_map/pallas_call | solution.py:160
  64.6 0.0 collective-permute-done.7.rest_0_
  64.6 0.0 copy-start.5
  64.6 7.1 %shard_map.67 = (f32[1536,256]{1,0:T(8,128)S(1)}, f32[1544,128]{1,0:T(8,128)S(1)}, bf16[384,512]{1,0:T(8,128)(2,1)S(1)}) custom-call(s32[1]{0:T(128)} %bitcast.my_ref, s32[384]{0:T(512)S(1)} %copy-done.1, s32[192]{0:T(256)S(1)} %copy-done.2, f32[2,64]{1,0:T(2,128)S(1)} %bitcast.9, f32[1]{0:T(128)} %bitcast.2.norm_ref, ...), custom_call_target="tpu_custom_call", output_to_operand_aliasing={{0}: (8, {}), {1}: (9, {})} | custom-call | flops 18119393280 | bytes 4194304 | tf_op jit(solution)/shard_map/pallas_call | solution.py:160
  71.7 0.0 copy-done.5
  71.7 1.8 %convolution_convert_fusion = bf16[384,4096]{1,0:T(8,128)(2,1)S(1)} fusion(bf16[384,512]{1,0:T(8,128)(2,1)S(1)} %get-tuple-element.24, bf16[512,4096]{1,0:T(8,128)(2,1)S(1)} %copy-done.5), kind=kOutput, calls=%fused_computation | convolution fusion | flops 1612185600 | bytes 7733248 | tf_op jit(solution)/shard_map/dot_general | solution.py:229
  73.5 44.6 %all_to_all.5 = bf16[8,48,4096]{2,1,0:T(8,128)(2,1)S(1)} all-to-all(bf16[8,48,4096]{2,1,0:T(8,128)(2,1)S(1)} %bitcast.10), channel_id=1, replica_groups=mesh['ctx'=64,'kvh'=8] {'kvh'}, dimensions={0} | all-to-all | bytes 6291456 | tf_op jit(solution)/shard_map/all_to_all | solution.py:230
  118.1 1.3 %reduce_sum.22 = bf16[48,4096]{1,0:T(8,128)(2,1)} reduce(bf16[8,48,4096]{2,1,0:T(8,128)(2,1)S(1)} %all_to_all.5, bf16[]{:T(256)} %constant.11.clone.1), dimensions={0}, to_apply=%region_2.0 | reduce | flops 1376256 | bytes 3538946 | tf_op jit(solution)/shard_map/reduce_sum | solution.py:231
  (3 shorter events, 0.0 us)
Async XLA Ops:
  0.0 8.7 %collective-permute-start = (bf16[384,256]{1,0:T(8,128)(2,1)}, bf16[384,256]{1,0:T(8,128)(2,1)S(1)}, u32[]{:S(2)}, u32[]{:S(2)}) collective-permute-start(bf16[384,256]{1,0:T(8,128)(2,1)} %param.7), channel_id=1, source_target_pairs={{0,32},{8,40},{16,48},{24,56},{32,64},{40,72},{48,80},{56,88},{64,... | collective-permute-start | bytes 589832 | tf_op jit(solution)/shard_map/ppermute | solution.py:190
  4.9 1.5 %copy-start.4 = (bf16[384,256]{1,0:T(8,128)(2,1)S(1)}, bf16[384,256]{1,0:T(8,128)(2,1)}, u32[]{:S(2)}) copy-start(bf16[384,256]{1,0:T(8,128)(2,1)} %param.7) | copy-start | bytes 589828
  4.9 3.8 %copy-start.1 = (s32[384]{0:T(512)S(1)}, s32[384]{0:T(512)}, u32[]{:S(2)}) copy-start(s32[384]{0:T(512)} %doc_ref.7) | copy-start | bytes 4612
  5.7 18.5 %copy-start = (bf16[384,512]{1,0:T(8,128)(2,1)S(1)}, bf16[384,512]{1,0:T(8,128)(2,1)}, u32[]{:S(2)}) copy-start(bf16[384,512]{1,0:T(8,128)(2,1)} %query_ref.7) | copy-start | bytes 1179652
  5.7 18.5 %copy-start.2 = (s32[192]{0:T(256)S(1)}, s32[192]{0:T(256)}, u32[]{:S(2)}) copy-start(s32[192]{0:T(256)} %index_ref.7) | copy-start | bytes 2308
  5.7 18.5 %copy-start.3 = (f32[64,2]{0,1:T(2,128)S(1)}, f32[64,2]{0,1:T(2,128)}, u32[]{:S(2)}) copy-start(f32[64,2]{0,1:T(2,128)} %param.10) | copy-start | bytes 1540
  8.9 13.4 %collective-permute-start.2 = (bf16[768,256]{1,0:T(8,128)(2,1)S(1)}, bf16[768,256]{1,0:T(8,128)(2,1)S(1)}, u32[]{:S(2)}, u32[]{:S(2)}) collective-permute-start(bf16[768,256]{1,0:T(8,128)(2,1)S(1)} %constant_dynamic-update-slice_fusion.rest_0_), channel_id=1, source_target_pairs={{0,16},{8,24},{16,0},{24,8},{32,48},{40,56},{48,32},{56,40},{64,80... | collective-permute-start | bytes 1179656 | tf_op jit(solution)/shard_map/ppermute | solution.py:196
  11.3 23.2 %collective-permute-start.1 = (bf16[768,256]{1,0:T(8,128)(2,1)S(1)}, bf16[768,256]{1,0:T(8,128)(2,1)S(1)}, u32[]{:S(2)}, u32[]{:S(2)}) collective-permute-start(bf16[768,256]{1,0:T(8,128)(2,1)S(1)} %constant_dynamic-update-slice_fusion.rest_0_), channel_id=1, source_target_pairs={{0,64},{8,72},{16,80},{24,88},{32,96},{40,104},{48,112},{56,120},{... | collective-permute-start | bytes 1179656 | tf_op jit(solution)/shard_map/ppermute | solution.py:190
  22.3 26.2 %collective-permute-start.6 = (bf16[1536,256]{1,0:T(8,128)(2,1)S(1)}, bf16[1536,256]{1,0:T(8,128)(2,1)S(1)}, u32[]{:S(2)}, u32[]{:S(2)}) collective-permute-start(bf16[1536,256]{1,0:T(8,128)(2,1)S(1)} %pad_maximum_fusion.1), channel_id=1, source_target_pairs={{0,8},{8,0},{16,24},{24,16},{32,40},{40,32},{48,56},{56,48},{64,72... | collective-permute-start | bytes 2359304 | tf_op jit(solution)/shard_map/ppermute | solution.py:193
  34.5 23.0 %collective-permute-start.5 = (bf16[768,256]{1,0:T(8,128)(2,1)S(1)}, bf16[768,256]{1,0:T(8,128)(2,1)S(1)}, u32[]{:S(2)}, u32[]{:S(2)}) collective-permute-start(bf16[768,256]{1,0:T(8,128)(2,1)S(1)} %collective-permute-done.1.rest_0_), channel_id=1, source_target_pairs={{0,16},{8,24},{16,0},{24,8},{32,48},{40,56},{48,32},{56,40},{64,80... | collective-permute-start | bytes 1179656 | tf_op jit(solution)/shard_map/ppermute | solution.py:196
  39.4 18.0 %collective-permute-start.3 = (bf16[384,256]{1,0:T(8,128)(2,1)S(1)}, bf16[384,256]{1,0:T(8,128)(2,1)S(1)}, u32[]{:S(2)}, u32[]{:S(2)}) collective-permute-start(bf16[384,256]{1,0:T(8,128)(2,1)S(1)} %slice.3), channel_id=1, source_target_pairs={{0,32},{8,40},{16,48},{24,56},{32,64},{40,72},{48,80},{56,88},{64,... | collective-permute-start | bytes 589832 | tf_op jit(solution)/shard_map/ppermute | solution.py:190
  41.4 16.1 %collective-permute-start.4 = (bf16[384,256]{1,0:T(8,128)(2,1)S(1)}, bf16[384,256]{1,0:T(8,128)(2,1)S(1)}, u32[]{:S(2)}, u32[]{:S(2)}) collective-permute-start(bf16[384,256]{1,0:T(8,128)(2,1)S(1)} %slice.3), channel_id=1, source_target_pairs={{16,32},{24,40},{48,64},{56,72},{80,96},{88,104},{112,128},{120,13... | collective-permute-start | bytes 589832 | tf_op jit(solution)/shard_map/ppermute | solution.py:221
  57.6 7.0 %collective-permute-start.7 = (bf16[2304,256]{1,0:T(8,128)(2,1)S(1)}, bf16[2304,256]{1,0:T(8,128)(2,1)S(1)}, u32[]{:S(2)}, u32[]{:S(2)}) collective-permute-start(bf16[2304,256]{1,0:T(8,128)(2,1)S(1)} %pad_maximum_fusion), channel_id=1, source_target_pairs={{0,8},{8,0},{16,24},{24,16},{32,40},{40,32},{48,56},{56,48},{64,72... | collective-permute-start | bytes 3538952 | tf_op jit(solution)/shard_map/ppermute | solution.py:193
  64.6 7.1 %copy-start.5 = (bf16[512,4096]{1,0:T(8,128)(2,1)S(1)}, bf16[512,4096]{1,0:T(8,128)(2,1)}, u32[]{:S(2)}) copy-start(bf16[512,4096]{1,0:T(8,128)(2,1)} %param.11) | copy-start | bytes 12582916

commit v7 on v6

--- a/solution.py
+++ b/solution.py
@@ -204,6 +204,13 @@
     def others(plan):
         return tuple((False, k, cross) for _, k, cross in plan)
 
+    half = out_weight.shape[1] // 2
+    side = (lax.axis_index("kvh") // 2) % 2
+    pairs = [(k, k ^ 2) for k in range(lax.axis_size("kvh"))]
+    own_weight = lax.dynamic_slice_in_dim(out_weight, side * half, half, 1)
+    sent_weight = lax.dynamic_slice_in_dim(out_weight, (1 - side) * half, half, 1)
+    pair_weight = lax.ppermute(sent_weight, "kvh", pairs)
+
     from_2 = shifted(keys_values, 4)
     from_02 = jnp.concatenate([keys_values, after(from_2, norm, starts)])
     from_46 = shifted(from_02, 8)
@@ -216,19 +223,24 @@
     state = attend(common, [from_02, cross_02], plan_02 + cplan_02)
     from_46 = after(from_46, *state)
     from_6 = from_46[tok:]
-    cross_46 = crossed(from_46)
+    cross_46 = crossed(after(from_46, swap_02))
     from_8 = shifted(from_6, 4)
     from_7 = lax.ppermute(from_6, "ctx", last)
     plan = plan_46 + others(plan_02 + cplan_02)
-    state = attend(common, [from_46, swap_02], plan, state)
+    state = attend(common, [from_46, after(swap_02, pair_weight)], plan, state)
     swap_46 = swapped(jnp.concatenate([from_46, from_8, from_7, after(cross_46, *state)]))
     state = attend(common, [cross_46, from_8, from_7], cplan_46 + plan_8 + cplan_7, state)
     plan = others(plan_46 + plan_8 + cplan_7 + cplan_46)
     _, _, attn = attend(common, [swap_46], plan, state, True)
     shares = lax.axis_size("kvh")
-    partial = jnp.dot(attn, out_weight, preferred_element_type=jnp.float32).astype(jnp.bfloat16)
-    pieces = lax.all_to_all(partial.reshape(shares, tok // shares, -1), "kvh", 0, 0)
-    return jnp.sum(pieces.astype(jnp.float32), axis=0).astype(jnp.bfloat16)
+    pair_attn = lax.ppermute(attn, "kvh", pairs)
+    partial = jnp.dot(attn, own_weight, preferred_element_type=jnp.float32)
+    partial = partial + jnp.dot(pair_attn, pair_weight, preferred_element_type=jnp.float32)
+    partial = partial.astype(jnp.bfloat16).reshape(shares, tok // shares, half)
+    pieces = lax.all_to_all(partial, "kvh", 0, 0)
+    pieces = pieces.astype(jnp.float32).reshape(shares // 4, 2, 2, tok // shares, half)
+    summed = jnp.sum(pieces, axis=(0, 2)).astype(jnp.bfloat16)
+    return jnp.concatenate([summed[0], summed[1]], axis=1)
 
 
 def solution(mesh):

time: 120 us -> 124 us (1.033)
  the two profiles are of different devices: /device:TPU:68 before, /device:TPU:64 now
where the time goes in v7:
time: 124 us; the launch traced here: 123 us
  starting transfers between devices  40.4 us (33%)
  Pallas kernels  26.7 us (22%)
  blocking collectives  25.4 us (20%)
  waiting for transfers between devices  20.5 us (17%)
  local copies, waits for them, and re-layouts  3.69 us (3%)
  matrix products  3.62 us (3%)
  other arithmetic  2.47 us (2%)
    pallas_call x4, Pallas kernels, attend(): pl.pallas_call(functools.partial(attend_kernel, counts, plan, state is No...  26.7 us
    all_to_all x1, blocking collectives, local(): pieces = lax.all_to_all(partial, 'kvh', 0, 0)  25.4 us
    ppermute x2, starting transfers between devices, crossed(): return lax.ppermute(block, 'ctx', [(i, i ^ 2) for i in range(ctx_count)])  15.8 us
    ppermute x3, starting transfers between devices, shifted(): lax.ppermute(block, 'ctx', [(i, i + distance) for i in range(ctx_count -...  13.3 us
    ppermute x1, waiting for transfers between devices, local(): pair_attn = lax.ppermute(attn, 'kvh', pairs)  11 us
    ppermute x3, waiting for transfers between devices, shifted(): lax.ppermute(block, 'ctx', [(i, i + distance) for i in range(ctx_count -...  8.85 us
    ppermute x2, starting transfers between devices, swapped(): return lax.ppermute(block, 'ctx', [(i, i ^ 1) for i in range(ctx_count)])  4.06 us
    ppermute x1, starting transfers between devices, local(): pair_weight = lax.ppermute(sent_weight, 'kvh', pairs)  3.61 us
  transfers between devices with their start and end apart: 10, of which 4 were waited for; matrix products, arithmetic and copies ran while one was open for 1% of the time, Pallas kernels for 16%

profile of v7, /device:TPU:64, one launch (start us, length us, event | category | flops | bytes accessed | tf_op | source)
XLA Modules:
  0.0 123.1 jit_solution(7620397875935540434)
XLA Ops:
  0.0 0.0 copy-start.5
  0.0 0.0 copy-start
  0.0 3.2 %constant_dynamic-slice_fusion = bf16[512,2048]{1,0:T(8,128)(2,1)} fusion(bf16[512,4096]{1,0:T(8,128)(2,1)} %param.11, s32[]{:T(128)S(6)} %select_n.19), kind=kLoop, calls=%fused_computation.11 | loop fusion | bytes 4194308 | tf_op jit(solution)/shard_map/dynamic_slice | solution.py:211
  3.2 3.6 %collective-permute-start.7 = (bf16[512,2048]{1,0:T(8,128)(2,1)}, bf16[512,2048]{1,0:T(8,128)(2,1)}, u32[]{:S(2)}, u32[]{:S(2)}) collective-permute-start(bf16[512,2048]{1,0:T(8,128)(2,1)} %constant_dynamic-slice_fusion), channel_id=1, source_target_pairs={{0,2},{1,3},{2,0},{3,1},{4,6},{5,7},{6,4},{7,5},{8,10},{9,11},{10,... | collective-permute-start | bytes 6291464 | tf_op jit(solution)/shard_map/ppermute | solution.py:212
  6.8 0.0 copy-done.5
  6.8 3.8 %collective-permute-start = (bf16[384,256]{1,0:T(8,128)(2,1)S(1)}, bf16[384,256]{1,0:T(8,128)(2,1)S(1)}, u32[]{:S(2)}, u32[]{:S(2)}) collective-permute-start(bf16[384,256]{1,0:T(8,128)(2,1)S(1)} %copy-done.5), channel_id=1, source_target_pairs={{0,32},{8,40},{16,48},{24,56},{32,64},{40,72},{48,80},{56,88},{64,... | collective-permute-start | bytes 589832 | tf_op jit(solution)/shard_map/ppermute | solution.py:190
  10.7 0.0 copy-done
  10.7 0.1 convert_multiply_fusion
  10.8 0.3 reshape.13
  11.1 0.0 copy-start.2
  11.1 0.0 copy-start.3
  11.1 0.5 reduce_sum.18
  11.6 0.7 reduce_max.9
  12.3 2.8 %collective-permute-done = bf16[384,256]{1,0:T(8,128)(2,1)S(1)} collective-permute-done((bf16[384,256]{1,0:T(8,128)(2,1)S(1)}, bf16[384,256]{1,0:T(8,128)(2,1)S(1)}, u32[]{:S(2)}, u32[]{:S(2)}) %collective-permute-start) | collective-permute-done | bytes 196640 | tf_op jit(solution)/shard_map/ppermute | solution.py:190
  15.1 0.0 copy-done.1
  15.1 0.1 broadcast_in_dim.14.starts_ref
  15.2 4.9 %collective-permute-start.2 = (bf16[768,256]{1,0:T(8,128)(2,1)S(1)}, bf16[768,256]{1,0:T(8,128)(2,1)S(1)}, u32[]{:S(2)}, u32[]{:S(2)}) collective-permute-start(bf16[768,256]{1,0:T(8,128)(2,1)S(1)} %constant_dynamic-update-slice_fusion.rest_0_), channel_id=1, source_target_pairs={{0,16},{8,24},{16,0},{24,8},{32,48},{40,56},{48,32},{56,40},{64,80... | collective-permute-start | bytes 1179656 | tf_op jit(solution)/shard_map/ppermute | solution.py:196
  20.2 7.6 %collective-permute-start.1 = (bf16[768,256]{1,0:T(8,128)(2,1)S(1)}, bf16[768,256]{1,0:T(8,128)(2,1)S(1)}, u32[]{:S(2)}, u32[]{:S(2)}) collective-permute-start(bf16[768,256]{1,0:T(8,128)(2,1)S(1)} %constant_dynamic-update-slice_fusion.rest_0_), channel_id=1, source_target_pairs={{0,64},{8,72},{16,80},{24,88},{32,96},{40,104},{48,112},{56,120},{... | collective-permute-start | bytes 1179656 | tf_op jit(solution)/shard_map/ppermute | solution.py:190
  27.8 0.6 collective-permute-done.2.rest_1_
  28.4 0.1 pad_maximum_fusion.1
  28.5 1.9 %collective-permute-start.5 = (bf16[1536,256]{1,0:T(8,128)(2,1)S(1)}, bf16[1536,256]{1,0:T(8,128)(2,1)S(1)}, u32[]{:S(2)}, u32[]{:S(2)}) collective-permute-start(bf16[1536,256]{1,0:T(8,128)(2,1)S(1)} %pad_maximum_fusion.1), channel_id=1, source_target_pairs={{0,8},{8,0},{16,24},{24,16},{32,40},{40,32},{48,56},{56,48},{64,72... | collective-permute-start | bytes 2359304 | tf_op jit(solution)/shard_map/ppermute | solution.py:193
  30.4 0.0 copy-done.2
  30.4 0.0 copy-done.3
  30.4 6.6 %shard_map.64 = (f32[1536,256]{1,0:T(8,128)S(1)}, f32[1544,128]{1,0:T(8,128)S(1)}) custom-call(s32[1]{0:T(128)} %bitcast.my_ref, s32[384]{0:T(512)S(1)} %copy-done.1, s32[192]{0:T(256)S(1)} %copy-done.2, f32[2,64]{1,0:T(2,128)S(1)} %bitcast.12, f32[1]{0:T(128)} %bitcast.2.norm_ref, s32[384,128]{1,0:T(8,128)S(1)} %broadcast_in_dim.14.starts_ref, ...), custom_call_target="tpu_custom_call" | custom-call | flops 12079595520 | bytes 4194304 | tf_op jit(solution)/shard_map/pallas_call | solution.py:160
  37.0 6.1 %collective-permute-done.1.rest_0_ = bf16[768,256]{1,0:T(8,128)(2,1)S(1)} collective-permute-done((bf16[768,256]{1,0:T(8,128)(2,1)S(1)}, bf16[768,256]{1,0:T(8,128)(2,1)S(1)}, u32[]{:S(2)}, u32[]{:S(2)}) %collective-permute-start.1) | collective-permute-done | bytes 393248 | tf_op jit(solution)/shard_map/ppermute | solution.py:190
  43.1 1.9 %collective-permute-start.3 = (bf16[384,256]{1,0:T(8,128)(2,1)S(1)}, bf16[384,256]{1,0:T(8,128)(2,1)S(1)}, u32[]{:S(2)}, u32[]{:S(2)}) collective-permute-start(bf16[384,256]{1,0:T(8,128)(2,1)S(1)} %slice.9), channel_id=1, source_target_pairs={{0,32},{8,40},{16,48},{24,56},{32,64},{40,72},{48,80},{56,88},{64,... | collective-permute-start | bytes 589832 | tf_op jit(solution)/shard_map/ppermute | solution.py:190
  45.0 1.3 %collective-permute-start.4 = (bf16[384,256]{1,0:T(8,128)(2,1)S(1)}, bf16[384,256]{1,0:T(8,128)(2,1)S(1)}, u32[]{:S(2)}, u32[]{:S(2)}) collective-permute-start(bf16[384,256]{1,0:T(8,128)(2,1)S(1)} %slice.9), channel_id=1, source_target_pairs={{16,32},{24,40},{48,64},{56,72},{80,96},{88,104},{112,128},{120,13... | collective-permute-start | bytes 589832 | tf_op jit(solution)/shard_map/ppermute | solution.py:228
  46.3 0.0 collective-permute-done.5.rest_1_
  46.3 10.8 %collective-permute-start.6 = (bf16[768,256]{1,0:T(8,128)(2,1)S(1)}, bf16[768,256]{1,0:T(8,128)(2,1)S(1)}, u32[]{:S(2)}, u32[]{:S(2)}) collective-permute-start(bf16[768,256]{1,0:T(8,128)(2,1)S(1)} %collective-permute-done.1.rest_0_), channel_id=1, source_target_pairs={{0,16},{8,24},{16,0},{24,8},{32,48},{40,56},{48,32},{56,40},{64,80... | collective-permute-start | bytes 1179656 | tf_op jit(solution)/shard_map/ppermute | solution.py:196
  57.1 0.0 collective-permute-done.7
  57.1 8.6 %shard_map.65 = (f32[1536,256]{1,0:T(8,128)S(1)}, f32[1544,128]{1,0:T(8,128)S(1)}) custom-call(s32[1]{0:T(128)} %bitcast.my_ref, s32[384]{0:T(512)S(1)} %copy-done.1, s32[192]{0:T(256)S(1)} %copy-done.2, f32[2,64]{1,0:T(2,128)S(1)} %bitcast.13, f32[1]{0:T(128)} %bitcast.2.norm_ref, ...), custom_call_target="tpu_custom_call", output_to_operand_aliasing={{0}: (9, {}), {1}: (10, {})} | custom-call | flops 18119393280 | bytes 4194304 | tf_op jit(solution)/shard_map/pallas_call | solution.py:160
  65.7 0.0 collective-permute-done.6.rest_0_
  65.7 0.0 collective-permute-done.3.rest_1_
  65.8 0.0 collective-permute-done.4.rest_2_
  65.8 0.1 pad_maximum_fusion
  65.9 2.1 %collective-permute-start.8 = (bf16[2304,256]{1,0:T(8,128)(2,1)S(1)}, bf16[2304,256]{1,0:T(8,128)(2,1)S(1)}, u32[]{:S(2)}, u32[]{:S(2)}) collective-permute-start(bf16[2304,256]{1,0:T(8,128)(2,1)S(1)} %pad_maximum_fusion), channel_id=1, source_target_pairs={{0,8},{8,0},{16,24},{24,16},{32,40},{40,32},{48,56},{56,48},{64,72... | collective-permute-start | bytes 3538952 | tf_op jit(solution)/shard_map/ppermute | solution.py:193
  68.0 4.8 %shard_map.66 = (f32[1536,256]{1,0:T(8,128)S(1)}, f32[1544,128]{1,0:T(8,128)S(1)}) custom-call(s32[1]{0:T(128)} %bitcast.my_ref, s32[384]{0:T(512)S(1)} %copy-done.1, s32[192]{0:T(256)S(1)} %copy-done.2, f32[2,64]{1,0:T(2,128)S(1)} %bitcast.14, f32[1]{0:T(128)} %bitcast.2.norm_ref, ...), custom_call_target="tpu_custom_call", output_to_operand_aliasing={{0}: (10, {}), {1}: (11, {})} | custom-call | flops 12079595520 | bytes 4194304 | tf_op jit(solution)/shard_map/pallas_call | solution.py:160
  72.8 0.0 collective-permute-done.8.rest_0_
  72.8 6.7 %shard_map.67 = (f32[1536,256]{1,0:T(8,128)S(1)}, f32[1544,128]{1,0:T(8,128)S(1)}, bf16[384,512]{1,0:T(8,128)(2,1)S(1)}) custom-call(s32[1]{0:T(128)} %bitcast.my_ref, s32[384]{0:T(512)S(1)} %copy-done.1, s32[192]{0:T(256)S(1)} %copy-done.2, f32[2,64]{1,0:T(2,128)S(1)} %bitcast.15, f32[1]{0:T(128)} %bitcast.2.norm_ref, ...), custom_call_target="tpu_custom_call", output_to_operand_aliasing={{0}: (8, {}), {1}: (9, {})} | custom-call | flops 18119393280 | bytes 4194304 | tf_op jit(solution)/shard_map/pallas_call | solution.py:160
  79.6 2.4 %collective-permute-start.9 = (bf16[384,512]{1,0:T(8,128)(2,1)S(1)}, bf16[384,512]{1,0:T(8,128)(2,1)S(1)}, u32[]{:S(2)}, u32[]{:S(2)}) collective-permute-start(bf16[384,512]{1,0:T(8,128)(2,1)S(1)} %get-tuple-element.28), channel_id=1, source_target_pairs={{0,2},{1,3},{2,0},{3,1},{4,6},{5,7},{6,4},{7,5},{8,10},{9,11},{10,... | collective-permute-start | bytes 1179656 | tf_op jit(solution)/shard_map/ppermute | solution.py:236
  81.9 0.0 copy-start.4
  82.0 11.0 %collective-permute-done.9 = bf16[384,512]{1,0:T(8,128)(2,1)S(1)} collective-permute-done((bf16[384,512]{1,0:T(8,128)(2,1)S(1)}, bf16[384,512]{1,0:T(8,128)(2,1)S(1)}, u32[]{:S(2)}, u32[]{:S(2)}) %collective-permute-start.9) | collective-permute-done | bytes 393248 | tf_op jit(solution)/shard_map/ppermute | solution.py:236
  93.0 2.6 %fusion.2 = f32[384,2048]{1,0:T(8,128)S(1)} fusion(bf16[384,512]{1,0:T(8,128)(2,1)S(1)} %collective-permute-done.9, bf16[512,2048]{1,0:T(8,128)(2,1)} %collective-permute-done.7), kind=kOutput, calls=%fused_computation.12 | convolution fusion | flops 805306368 | bytes 5636096 | tf_op jit(solution)/shard_map/dot_general | solution.py:238
  95.6 0.0 copy-done.4
  95.6 1.1 add_convert_fusion
  96.6 25.4 %all_to_all.5 = bf16[8,48,2048]{2,1,0:T(8,128)(2,1)S(1)} all-to-all(bf16[8,48,2048]{2,1,0:T(8,128)(2,1)S(1)} %bitcast.16), channel_id=1, replica_groups=mesh['ctx'=64,'kvh'=8] {'kvh'}, dimensions={0} | all-to-all | bytes 3145728 | tf_op jit(solution)/shard_map/all_to_all | solution.py:240
  122.1 0.3 reduce
  122.4 0.8 pad_maximum_fusion.2
  (5 shorter events, 0.1 us)
Async XLA Ops:
  0.0 6.8 %copy-start.5 = (bf16[384,256]{1,0:T(8,128)(2,1)S(1)}, bf16[384,256]{1,0:T(8,128)(2,1)}, u32[]{:S(2)}) copy-start(bf16[384,256]{1,0:T(8,128)(2,1)} %param.7) | copy-start | bytes 589828
  0.0 10.7 %copy-start = (bf16[384,512]{1,0:T(8,128)(2,1)S(1)}, bf16[384,512]{1,0:T(8,128)(2,1)}, u32[]{:S(2)}) copy-start(bf16[384,512]{1,0:T(8,128)(2,1)} %query_ref.7) | copy-start | bytes 1179652
  3.2 11.9 %copy-start.1 = (s32[384]{0:T(512)S(1)}, s32[384]{0:T(512)}, u32[]{:S(2)}) copy-start(s32[384]{0:T(512)} %doc_ref.7) | copy-start | bytes 4612
  3.2 53.9 %collective-permute-start.7 = (bf16[512,2048]{1,0:T(8,128)(2,1)}, bf16[512,2048]{1,0:T(8,128)(2,1)}, u32[]{:S(2)}, u32[]{:S(2)}) collective-permute-start(bf16[512,2048]{1,0:T(8,128)(2,1)} %constant_dynamic-slice_fusion), channel_id=1, source_target_pairs={{0,2},{1,3},{2,0},{3,1},{4,6},{5,7},{6,4},{7,5},{8,10},{9,11},{10,... | collective-permute-start | bytes 6291464 | tf_op jit(solution)/shard_map/ppermute | solution.py:212
  6.8 8.3 %collective-permute-start = (bf16[384,256]{1,0:T(8,128)(2,1)S(1)}, bf16[384,256]{1,0:T(8,128)(2,1)S(1)}, u32[]{:S(2)}, u32[]{:S(2)}) collective-permute-start(bf16[384,256]{1,0:T(8,128)(2,1)S(1)} %copy-done.5), channel_id=1, source_target_pairs={{0,32},{8,40},{16,48},{24,56},{32,64},{40,72},{48,80},{56,88},{64,... | collective-permute-start | bytes 589832 | tf_op jit(solution)/shard_map/ppermute | solution.py:190
  11.1 19.3 %copy-start.2 = (s32[192]{0:T(256)S(1)}, s32[192]{0:T(256)}, u32[]{:S(2)}) copy-start(s32[192]{0:T(256)} %index_ref.7) | copy-start | bytes 2308
  11.1 19.3 %copy-start.3 = (f32[64,2]{0,1:T(2,128)S(1)}, f32[64,2]{0,1:T(2,128)}, u32[]{:S(2)}) copy-start(f32[64,2]{0,1:T(2,128)} %param.10) | copy-start | bytes 1540
  15.2 13.2 %collective-permute-start.2 = (bf16[768,256]{1,0:T(8,128)(2,1)S(1)}, bf16[768,256]{1,0:T(8,128)(2,1)S(1)}, u32[]{:S(2)}, u32[]{:S(2)}) collective-permute-start(bf16[768,256]{1,0:T(8,128)(2,1)S(1)} %constant_dynamic-update-slice_fusion.rest_0_), channel_id=1, source_target_pairs={{0,16},{8,24},{16,0},{24,8},{32,48},{40,56},{48,32},{56,40},{64,80... | collective-permute-start | bytes 1179656 | tf_op jit(solution)/shard_map/ppermute | solution.py:196
  20.2 22.9 %collective-permute-start.1 = (bf16[768,256]{1,0:T(8,128)(2,1)S(1)}, bf16[768,256]{1,0:T(8,128)(2,1)S(1)}, u32[]{:S(2)}, u32[]{:S(2)}) collective-permute-start(bf16[768,256]{1,0:T(8,128)(2,1)S(1)} %constant_dynamic-update-slice_fusion.rest_0_), channel_id=1, source_target_pairs={{0,64},{8,72},{16,80},{24,88},{32,96},{40,104},{48,112},{56,120},{... | collective-permute-start | bytes 1179656 | tf_op jit(solution)/shard_map/ppermute | solution.py:190
  28.5 17.8 %collective-permute-start.5 = (bf16[1536,256]{1,0:T(8,128)(2,1)S(1)}, bf16[1536,256]{1,0:T(8,128)(2,1)S(1)}, u32[]{:S(2)}, u32[]{:S(2)}) collective-permute-start(bf16[1536,256]{1,0:T(8,128)(2,1)S(1)} %pad_maximum_fusion.1), channel_id=1, source_target_pairs={{0,8},{8,0},{16,24},{24,16},{32,40},{40,32},{48,56},{56,48},{64,72... | collective-permute-start | bytes 2359304 | tf_op jit(solution)/shard_map/ppermute | solution.py:193
  43.1 22.7 %collective-permute-start.3 = (bf16[384,256]{1,0:T(8,128)(2,1)S(1)}, bf16[384,256]{1,0:T(8,128)(2,1)S(1)}, u32[]{:S(2)}, u32[]{:S(2)}) collective-permute-start(bf16[384,256]{1,0:T(8,128)(2,1)S(1)} %slice.9), channel_id=1, source_target_pairs={{0,32},{8,40},{16,48},{24,56},{32,64},{40,72},{48,80},{56,88},{64,... | collective-permute-start | bytes 589832 | tf_op jit(solution)/shard_map/ppermute | solution.py:190
  45.0 20.8 %collective-permute-start.4 = (bf16[384,256]{1,0:T(8,128)(2,1)S(1)}, bf16[384,256]{1,0:T(8,128)(2,1)S(1)}, u32[]{:S(2)}, u32[]{:S(2)}) collective-permute-start(bf16[384,256]{1,0:T(8,128)(2,1)S(1)} %slice.9), channel_id=1, source_target_pairs={{16,32},{24,40},{48,64},{56,72},{80,96},{88,104},{112,128},{120,13... | collective-permute-start | bytes 589832 | tf_op jit(solution)/shard_map/ppermute | solution.py:228
  46.3 19.4 %collective-permute-start.6 = (bf16[768,256]{1,0:T(8,128)(2,1)S(1)}, bf16[768,256]{1,0:T(8,128)(2,1)S(1)}, u32[]{:S(2)}, u32[]{:S(2)}) collective-permute-start(bf16[768,256]{1,0:T(8,128)(2,1)S(1)} %collective-permute-done.1.rest_0_), channel_id=1, source_target_pairs={{0,16},{8,24},{16,0},{24,8},{32,48},{40,56},{48,32},{56,40},{64,80... | collective-permute-start | bytes 1179656 | tf_op jit(solution)/shard_map/ppermute | solution.py:196
  65.9 7.0 %collective-permute-start.8 = (bf16[2304,256]{1,0:T(8,128)(2,1)S(1)}, bf16[2304,256]{1,0:T(8,128)(2,1)S(1)}, u32[]{:S(2)}, u32[]{:S(2)}) collective-permute-start(bf16[2304,256]{1,0:T(8,128)(2,1)S(1)} %pad_maximum_fusion), channel_id=1, source_target_pairs={{0,8},{8,0},{16,24},{24,16},{32,40},{40,32},{48,56},{56,48},{64,72... | collective-permute-start | bytes 3538952 | tf_op jit(solution)/shard_map/ppermute | solution.py:193
  79.6 13.4 %collective-permute-start.9 = (bf16[384,512]{1,0:T(8,128)(2,1)S(1)}, bf16[384,512]{1,0:T(8,128)(2,1)S(1)}, u32[]{:S(2)}, u32[]{:S(2)}) collective-permute-start(bf16[384,512]{1,0:T(8,128)(2,1)S(1)} %get-tuple-element.28), channel_id=1, source_target_pairs={{0,2},{1,3},{2,0},{3,1},{4,6},{5,7},{6,4},{7,5},{8,10},{9,11},{10,... | collective-permute-start | bytes 1179656 | tf_op jit(solution)/shard_map/ppermute | solution.py:236
  81.9 13.6 %copy-start.4 = (bf16[512,4096]{1,0:T(8,128)(2,1)S(1)}, bf16[512,4096]{1,0:T(8,128)(2,1)}, u32[]{:S(2)}) copy-start(bf16[512,4096]{1,0:T(8,128)(2,1)} %param.11) | copy-start | bytes 12582916

commit v8 on v6

--- a/solution.py
+++ b/solution.py
@@ -27,16 +27,14 @@
     acc_ref, max_ref, *rest = rest
     if final:
         out_ref, *rest = rest
-    bias_ref, held, src_ref, sems = rest
+    bias_ref, held, src_ref = rest
     tok = query_ref.shape[0]
     parts = tok // SBLK
     flag_row = GROUPS * tok
     blocks = len(plan)
-    copies = []
     at = 0
-    for i, count in enumerate(counts):
-        copies.append(pltpu.make_async_copy(pieces[i], held.at[pl.ds(at * tok, count * tok)], sems.at[i]))
-        copies[-1].start()
+    for piece, count in zip(pieces, counts):
+        held[pl.ds(at * tok, count * tok), :] = piece[...]
         at += count
     my, low, high = my_ref[0], doc_ref[0], doc_ref[tok - 1]
     for step, (mine, back, crossed) in enumerate(plan):
@@ -49,23 +47,19 @@
         held[pl.ds(blocks * tok, tok), :] = jnp.zeros((tok, 2 * HD), held.dtype)
     if first:
         acc_ref[...] = jnp.zeros_like(acc_ref)
-    for copy in copies:
-        copy.wait()
 
     def scale_row(step, t):
         return index_ref[jnp.clip(src_ref[step], 0, my) * parts + t]
 
     ones = jnp.ones((HD, HD), jnp.bfloat16)
 
-    def widest(step, most):
-        key = held[pl.ds(pl.multiple_of(step * tok, tok), tok), :HD]
+    most = jnp.zeros((SBLK, HD), jnp.float32)
+    for step in range(blocks):
+        key = held[pl.ds(step * tok, tok), :HD]
         squares = jnp.dot(key * key, ones, preferred_element_type=jnp.float32)
         for t in range(parts):
             scale = table_ref[0, scale_row(step, t)] * FACTOR
             most = jnp.maximum(most, squares[t * SBLK : (t + 1) * SBLK] * (scale * scale))
-        return most
-
-    most = lax.fori_loop(0, blocks, widest, jnp.zeros((SBLK, HD), jnp.float32))
     small = jnp.max(most) * norm_ref[0] <= SAFE * SAFE
     if first:
         max_ref[...] = jnp.full(max_ref.shape, jnp.where(small, 0.0, NEG), jnp.float32)
@@ -161,15 +155,13 @@
         functools.partial(attend_kernel, counts, plan, state is None, final),
         out_shape=out_shape,
         in_specs=[smem] * 5
-        + [vmem] * 2
-        + [pl.BlockSpec(memory_space=pl.ANY)] * len(pieces)
+        + [vmem] * (2 + len(pieces))
         + [vmem] * (0 if state is None else 2),
         out_specs=(vmem,) * len(out_shape),
         scratch_shapes=[
             pltpu.VMEM((tok, 2 * tok), jnp.float32),
             pltpu.VMEM((even * tok, 2 * HD), jnp.bfloat16),
             pltpu.SMEM((even,), jnp.int32),
-            pltpu.SemaphoreType.DMA((len(counts),)),
         ],
         input_output_aliases={} if state is None else {7 + len(pieces): 0, 8 + len(pieces): 1},
         compiler_params=pltpu.CompilerParams(vmem_limit_bytes=40 << 20),
@@ -216,7 +208,7 @@
     state = attend(common, [from_02, cross_02], plan_02 + cplan_02)
     from_46 = after(from_46, *state)
     from_6 = from_46[tok:]
-    cross_46 = crossed(from_46)
+    cross_46 = crossed(after(from_46, swap_02))
     from_8 = shifted(from_6, 4)
     from_7 = lax.ppermute(from_6, "ctx", last)
     plan = plan_46 + others(plan_02 + cplan_02)

time: 120 us -> 118 us (0.983)
  the two profiles are of different devices: /device:TPU:68 before, /device:TPU:96 now
where the time goes in v8:
time: 118 us
  blocking collectives  43.1 us (37%)
  starting transfers between devices  34.2 us (29%)
  Pallas kernels  24.4 us (21%)
  waiting for transfers between devices  9.95 us (8%)
  other arithmetic  3.71 us (3%)
  matrix products  1.8 us (2%)
    all_to_all x1, blocking collectives, local(): lax.all_to_all(partial.reshape(shares, tok // shares, -1), 'kvh', 0, 0)  43.1 us
    pallas_call x4, Pallas kernels, attend(): pl.pallas_call(functools.partial(attend_kernel, counts, plan, state is No...  24.4 us
    ppermute x3, starting transfers between devices, shifted(): lax.ppermute(block, 'ctx', [(i, i + distance) for i in range(ctx_count -...  18.4 us
    ppermute x2, starting transfers between devices, crossed(): return lax.ppermute(block, 'ctx', [(i, i ^ 2) for i in range(ctx_count)])  10.6 us
    ppermute x3, waiting for transfers between devices, shifted(): lax.ppermute(block, 'ctx', [(i, i + distance) for i in range(ctx_count -...  5.19 us
    ppermute x2, waiting for transfers between devices, crossed(): return lax.ppermute(block, 'ctx', [(i, i ^ 2) for i in range(ctx_count)])  4.75 us
    ppermute x2, starting transfers between devices, swapped(): return lax.ppermute(block, 'ctx', [(i, i ^ 1) for i in range(ctx_count)])  3.84 us
  transfers between devices with their start and end apart: 8, of which 4 were waited for; matrix products, arithmetic and copies ran while one was open for 2% of the time, Pallas kernels for 15%

profile of v8, /device:TPU:96, one launch (start us, length us, event | category | flops | bytes accessed | tf_op | source)
XLA Modules:
  0.0 117.9 jit_solution(17027458358357689221)
XLA Ops:
  0.0 5.0 %collective-permute-start = (bf16[384,256]{1,0:T(8,128)(2,1)}, bf16[384,256]{1,0:T(8,128)(2,1)S(1)}, u32[]{:S(2)}, u32[]{:S(2)}) collective-permute-start(bf16[384,256]{1,0:T(8,128)(2,1)} %param.7), channel_id=1, source_target_pairs={{0,32},{8,40},{16,48},{24,56},{32,64},{40,72},{48,80},{56,88},{64,... | collective-permute-start | bytes 589832 | tf_op jit(solution)/shard_map/ppermute | solution.py:182
  5.0 1.1 convert_multiply_fusion
  6.1 0.0 copy-start.4
  6.1 0.0 copy-start.1
  6.1 0.3 reshape.7
  6.4 0.5 reduce_sum.21
  6.9 0.0 copy-start
  6.9 0.0 copy-start.2
  6.9 0.0 copy-start.3
  6.9 0.7 reduce_max.9
  7.7 0.0 copy-done.4
  7.7 1.8 %collective-permute-done = bf16[384,256]{1,0:T(8,128)(2,1)S(1)} collective-permute-done((bf16[384,256]{1,0:T(8,128)(2,1)}, bf16[384,256]{1,0:T(8,128)(2,1)S(1)}, u32[]{:S(2)}, u32[]{:S(2)}) %collective-permute-start) | collective-permute-done | bytes 196640 | tf_op jit(solution)/shard_map/ppermute | solution.py:182
  9.5 0.0 copy-done.1
  9.5 0.1 broadcast_in_dim.14.starts_ref
  9.6 4.9 %collective-permute-start.2 = (bf16[768,256]{1,0:T(8,128)(2,1)S(1)}, bf16[768,256]{1,0:T(8,128)(2,1)S(1)}, u32[]{:S(2)}, u32[]{:S(2)}) collective-permute-start(bf16[768,256]{1,0:T(8,128)(2,1)S(1)} %constant_dynamic-update-slice_fusion.rest_0_), channel_id=1, source_target_pairs={{0,16},{8,24},{16,0},{24,8},{32,48},{40,56},{48,32},{56,40},{64,80... | collective-permute-start | bytes 1179656 | tf_op jit(solution)/shard_map/ppermute | solution.py:188
  14.6 5.6 %collective-permute-start.1 = (bf16[768,256]{1,0:T(8,128)(2,1)S(1)}, bf16[768,256]{1,0:T(8,128)(2,1)S(1)}, u32[]{:S(2)}, u32[]{:S(2)}) collective-permute-start(bf16[768,256]{1,0:T(8,128)(2,1)S(1)} %constant_dynamic-update-slice_fusion.rest_0_), channel_id=1, source_target_pairs={{0,64},{8,72},{16,80},{24,88},{32,96},{40,104},{48,112},{56,120},{... | collective-permute-start | bytes 1179656 | tf_op jit(solution)/shard_map/ppermute | solution.py:182
  20.2 2.8 %collective-permute-done.2.rest_1_ = bf16[768,256]{1,0:T(8,128)(2,1)S(1)} collective-permute-done((bf16[768,256]{1,0:T(8,128)(2,1)S(1)}, bf16[768,256]{1,0:T(8,128)(2,1)S(1)}, u32[]{:S(2)}, u32[]{:S(2)}) %collective-permute-start.2) | collective-permute-done | bytes 393248 | tf_op jit(solution)/shard_map/ppermute | solution.py:188
  23.0 0.1 pad_maximum_fusion.1
  23.1 1.9 %collective-permute-start.5 = (bf16[1536,256]{1,0:T(8,128)(2,1)S(1)}, bf16[1536,256]{1,0:T(8,128)(2,1)S(1)}, u32[]{:S(2)}, u32[]{:S(2)}) collective-permute-start(bf16[1536,256]{1,0:T(8,128)(2,1)S(1)} %pad_maximum_fusion.1), channel_id=1, source_target_pairs={{0,8},{8,0},{16,24},{24,16},{32,40},{40,32},{48,56},{56,48},{64,72... | collective-permute-start | bytes 2359304 | tf_op jit(solution)/shard_map/ppermute | solution.py:185
  25.0 0.0 copy-done
  25.0 0.0 copy-done.2
  25.0 0.0 copy-done.3
  25.0 6.0 %shard_map.64 = (f32[1536,256]{1,0:T(8,128)S(1)}, f32[1544,128]{1,0:T(8,128)S(1)}) custom-call(s32[1]{0:T(128)} %bitcast.my_ref, s32[384]{0:T(512)S(1)} %copy-done.1, s32[192]{0:T(256)S(1)} %copy-done.2, f32[2,64]{1,0:T(2,128)S(1)} %bitcast.6, f32[1]{0:T(128)} %bitcast.2.norm_ref, s32[384,128]{1,0:T(8,128)S(1)} %broadcast_in_dim.14.starts_ref, ...), custom_call_target="tpu_custom_call" | custom-call | flops 12079595520 | bytes 4194304 | tf_op jit(solution)/shard_map/pallas_call | solution.py:154
  31.0 3.4 %collective-permute-done.1.rest_0_ = bf16[768,256]{1,0:T(8,128)(2,1)S(1)} collective-permute-done((bf16[768,256]{1,0:T(8,128)(2,1)S(1)}, bf16[768,256]{1,0:T(8,128)(2,1)S(1)}, u32[]{:S(2)}, u32[]{:S(2)}) %collective-permute-start.1) | collective-permute-done | bytes 393248 | tf_op jit(solution)/shard_map/ppermute | solution.py:182
  34.4 7.8 %collective-permute-start.3 = (bf16[384,256]{1,0:T(8,128)(2,1)S(1)}, bf16[384,256]{1,0:T(8,128)(2,1)S(1)}, u32[]{:S(2)}, u32[]{:S(2)}) collective-permute-start(bf16[384,256]{1,0:T(8,128)(2,1)S(1)} %slice.3), channel_id=1, source_target_pairs={{0,32},{8,40},{16,48},{24,56},{32,64},{40,72},{48,80},{56,88},{64,... | collective-permute-start | bytes 589832 | tf_op jit(solution)/shard_map/ppermute | solution.py:182
  42.2 1.3 %collective-permute-start.4 = (bf16[384,256]{1,0:T(8,128)(2,1)S(1)}, bf16[384,256]{1,0:T(8,128)(2,1)S(1)}, u32[]{:S(2)}, u32[]{:S(2)}) collective-permute-start(bf16[384,256]{1,0:T(8,128)(2,1)S(1)} %slice.3), channel_id=1, source_target_pairs={{16,32},{24,40},{48,64},{56,72},{80,96},{88,104},{112,128},{120,13... | collective-permute-start | bytes 589832 | tf_op jit(solution)/shard_map/ppermute | solution.py:213
  43.5 0.0 collective-permute-done.5.rest_1_
  43.5 5.7 %collective-permute-start.6 = (bf16[768,256]{1,0:T(8,128)(2,1)S(1)}, bf16[768,256]{1,0:T(8,128)(2,1)S(1)}, u32[]{:S(2)}, u32[]{:S(2)}) collective-permute-start(bf16[768,256]{1,0:T(8,128)(2,1)S(1)} %collective-permute-done.1.rest_0_), channel_id=1, source_target_pairs={{0,16},{8,24},{16,0},{24,8},{32,48},{40,56},{48,32},{56,40},{64,80... | collective-permute-start | bytes 1179656 | tf_op jit(solution)/shard_map/ppermute | solution.py:188
  49.2 8.1 %shard_map.65 = (f32[1536,256]{1,0:T(8,128)S(1)}, f32[1544,128]{1,0:T(8,128)S(1)}) custom-call(s32[1]{0:T(128)} %bitcast.my_ref, s32[384]{0:T(512)S(1)} %copy-done.1, s32[192]{0:T(256)S(1)} %copy-done.2, f32[2,64]{1,0:T(2,128)S(1)} %bitcast.7, f32[1]{0:T(128)} %bitcast.2.norm_ref, ...), custom_call_target="tpu_custom_call", output_to_operand_aliasing={{0}: (9, {}), {1}: (10, {})} | custom-call | flops 18119393280 | bytes 4194304 | tf_op jit(solution)/shard_map/pallas_call | solution.py:154
  57.3 2.0 %collective-permute-done.6.rest_0_ = bf16[768,256]{1,0:T(8,128)(2,1)S(1)} collective-permute-done((bf16[768,256]{1,0:T(8,128)(2,1)S(1)}, bf16[768,256]{1,0:T(8,128)(2,1)S(1)}, u32[]{:S(2)}, u32[]{:S(2)}) %collective-permute-start.6) | collective-permute-done | bytes 393248 | tf_op jit(solution)/shard_map/ppermute | solution.py:188
  59.2 0.0 collective-permute-done.3.rest_1_
  59.2 0.0 collective-permute-done.4.rest_2_
  59.2 0.1 pad_maximum_fusion
  59.3 1.9 %collective-permute-start.7 = (bf16[2304,256]{1,0:T(8,128)(2,1)S(1)}, bf16[2304,256]{1,0:T(8,128)(2,1)S(1)}, u32[]{:S(2)}, u32[]{:S(2)}) collective-permute-start(bf16[2304,256]{1,0:T(8,128)(2,1)S(1)} %pad_maximum_fusion), channel_id=1, source_target_pairs={{0,8},{8,0},{16,24},{24,16},{32,40},{40,32},{48,56},{56,48},{64,72... | collective-permute-start | bytes 3538952 | tf_op jit(solution)/shard_map/ppermute | solution.py:185
  61.2 4.0 %shard_map.66 = (f32[1536,256]{1,0:T(8,128)S(1)}, f32[1544,128]{1,0:T(8,128)S(1)}) custom-call(s32[1]{0:T(128)} %bitcast.my_ref, s32[384]{0:T(512)S(1)} %copy-done.1, s32[192]{0:T(256)S(1)} %copy-done.2, f32[2,64]{1,0:T(2,128)S(1)} %bitcast.8, f32[1]{0:T(128)} %bitcast.2.norm_ref, ...), custom_call_target="tpu_custom_call", output_to_operand_aliasing={{0}: (10, {}), {1}: (11, {})} | custom-call | flops 12079595520 | bytes 4194304 | tf_op jit(solution)/shard_map/pallas_call | solution.py:154
  65.3 0.0 collective-permute-done.7.rest_0_
  65.3 0.0 copy-start.5
  65.3 6.3 %shard_map.67 = (f32[1536,256]{1,0:T(8,128)S(1)}, f32[1544,128]{1,0:T(8,128)S(1)}, bf16[384,512]{1,0:T(8,128)(2,1)S(1)}) custom-call(s32[1]{0:T(128)} %bitcast.my_ref, s32[384]{0:T(512)S(1)} %copy-done.1, s32[192]{0:T(256)S(1)} %copy-done.2, f32[2,64]{1,0:T(2,128)S(1)} %bitcast.9, f32[1]{0:T(128)} %bitcast.2.norm_ref, ...), custom_call_target="tpu_custom_call", output_to_operand_aliasing={{0}: (8, {}), {1}: (9, {})} | custom-call | flops 18119393280 | bytes 4194304 | tf_op jit(solution)/shard_map/pallas_call | solution.py:154
  71.6 0.0 copy-done.5
  71.6 1.8 %convolution_convert_fusion = bf16[384,4096]{1,0:T(8,128)(2,1)S(1)} fusion(bf16[384,512]{1,0:T(8,128)(2,1)S(1)} %get-tuple-element.26, bf16[512,4096]{1,0:T(8,128)(2,1)S(1)} %copy-done.5), kind=kOutput, calls=%fused_computation | convolution fusion | flops 1612185600 | bytes 7733248 | tf_op jit(solution)/shard_map/dot_general | solution.py:221
  73.4 43.1 %all_to_all.5 = bf16[8,48,4096]{2,1,0:T(8,128)(2,1)S(1)} all-to-all(bf16[8,48,4096]{2,1,0:T(8,128)(2,1)S(1)} %bitcast.10), channel_id=1, replica_groups=mesh['ctx'=64,'kvh'=8] {'kvh'}, dimensions={0} | all-to-all | bytes 6291456 | tf_op jit(solution)/shard_map/all_to_all | solution.py:222
  116.5 1.3 %reduce_sum.22 = bf16[48,4096]{1,0:T(8,128)(2,1)} reduce(bf16[8,48,4096]{2,1,0:T(8,128)(2,1)S(1)} %all_to_all.5, bf16[]{:T(256)} %constant.11.clone.1), dimensions={0}, to_apply=%region_2.0 | reduce | flops 1376256 | bytes 3538946 | tf_op jit(solution)/shard_map/reduce_sum | solution.py:223
  (3 shorter events, 0.0 us)
Async XLA Ops:
  0.0 9.5 %collective-permute-start = (bf16[384,256]{1,0:T(8,128)(2,1)}, bf16[384,256]{1,0:T(8,128)(2,1)S(1)}, u32[]{:S(2)}, u32[]{:S(2)}) collective-permute-start(bf16[384,256]{1,0:T(8,128)(2,1)} %param.7), channel_id=1, source_target_pairs={{0,32},{8,40},{16,48},{24,56},{32,64},{40,72},{48,80},{56,88},{64,... | collective-permute-start | bytes 589832 | tf_op jit(solution)/shard_map/ppermute | solution.py:182
  6.1 1.5 %copy-start.4 = (bf16[384,256]{1,0:T(8,128)(2,1)S(1)}, bf16[384,256]{1,0:T(8,128)(2,1)}, u32[]{:S(2)}) copy-start(bf16[384,256]{1,0:T(8,128)(2,1)} %param.7) | copy-start | bytes 589828
  6.1 3.4 %copy-start.1 = (s32[384]{0:T(512)S(1)}, s32[384]{0:T(512)}, u32[]{:S(2)}) copy-start(s32[384]{0:T(512)} %doc_ref.7) | copy-start | bytes 4612
  6.9 18.1 %copy-start = (bf16[384,512]{1,0:T(8,128)(2,1)S(1)}, bf16[384,512]{1,0:T(8,128)(2,1)}, u32[]{:S(2)}) copy-start(bf16[384,512]{1,0:T(8,128)(2,1)} %query_ref.7) | copy-start | bytes 1179652
  6.9 18.1 %copy-start.2 = (s32[192]{0:T(256)S(1)}, s32[192]{0:T(256)}, u32[]{:S(2)}) copy-start(s32[192]{0:T(256)} %index_ref.7) | copy-start | bytes 2308
  6.9 18.1 %copy-start.3 = (f32[64,2]{0,1:T(2,128)S(1)}, f32[64,2]{0,1:T(2,128)}, u32[]{:S(2)}) copy-start(f32[64,2]{0,1:T(2,128)} %param.10) | copy-start | bytes 1540
  9.6 13.4 %collective-permute-start.2 = (bf16[768,256]{1,0:T(8,128)(2,1)S(1)}, bf16[768,256]{1,0:T(8,128)(2,1)S(1)}, u32[]{:S(2)}, u32[]{:S(2)}) collective-permute-start(bf16[768,256]{1,0:T(8,128)(2,1)S(1)} %constant_dynamic-update-slice_fusion.rest_0_), channel_id=1, source_target_pairs={{0,16},{8,24},{16,0},{24,8},{32,48},{40,56},{48,32},{56,40},{64,80... | collective-permute-start | bytes 1179656 | tf_op jit(solution)/shard_map/ppermute | solution.py:188
  14.6 19.8 %collective-permute-start.1 = (bf16[768,256]{1,0:T(8,128)(2,1)S(1)}, bf16[768,256]{1,0:T(8,128)(2,1)S(1)}, u32[]{:S(2)}, u32[]{:S(2)}) collective-permute-start(bf16[768,256]{1,0:T(8,128)(2,1)S(1)} %constant_dynamic-update-slice_fusion.rest_0_), channel_id=1, source_target_pairs={{0,64},{8,72},{16,80},{24,88},{32,96},{40,104},{48,112},{56,120},{... | collective-permute-start | bytes 1179656 | tf_op jit(solution)/shard_map/ppermute | solution.py:182
  23.1 20.4 %collective-permute-start.5 = (bf16[1536,256]{1,0:T(8,128)(2,1)S(1)}, bf16[1536,256]{1,0:T(8,128)(2,1)S(1)}, u32[]{:S(2)}, u32[]{:S(2)}) collective-permute-start(bf16[1536,256]{1,0:T(8,128)(2,1)S(1)} %pad_maximum_fusion.1), channel_id=1, source_target_pairs={{0,8},{8,0},{16,24},{24,16},{32,40},{40,32},{48,56},{56,48},{64,72... | collective-permute-start | bytes 2359304 | tf_op jit(solution)/shard_map/ppermute | solution.py:185
  34.4 24.8 %collective-permute-start.3 = (bf16[384,256]{1,0:T(8,128)(2,1)S(1)}, bf16[384,256]{1,0:T(8,128)(2,1)S(1)}, u32[]{:S(2)}, u32[]{:S(2)}) collective-permute-start(bf16[384,256]{1,0:T(8,128)(2,1)S(1)} %slice.3), channel_id=1, source_target_pairs={{0,32},{8,40},{16,48},{24,56},{32,64},{40,72},{48,80},{56,88},{64,... | collective-permute-start | bytes 589832 | tf_op jit(solution)/shard_map/ppermute | solution.py:182
  42.2 17.1 %collective-permute-start.4 = (bf16[384,256]{1,0:T(8,128)(2,1)S(1)}, bf16[384,256]{1,0:T(8,128)(2,1)S(1)}, u32[]{:S(2)}, u32[]{:S(2)}) collective-permute-start(bf16[384,256]{1,0:T(8,128)(2,1)S(1)} %slice.3), channel_id=1, source_target_pairs={{16,32},{24,40},{48,64},{56,72},{80,96},{88,104},{112,128},{120,13... | collective-permute-start | bytes 589832 | tf_op jit(solution)/shard_map/ppermute | solution.py:213
  43.5 15.7 %collective-permute-start.6 = (bf16[768,256]{1,0:T(8,128)(2,1)S(1)}, bf16[768,256]{1,0:T(8,128)(2,1)S(1)}, u32[]{:S(2)}, u32[]{:S(2)}) collective-permute-start(bf16[768,256]{1,0:T(8,128)(2,1)S(1)} %collective-permute-done.1.rest_0_), channel_id=1, source_target_pairs={{0,16},{8,24},{16,0},{24,8},{32,48},{40,56},{48,32},{56,40},{64,80... | collective-permute-start | bytes 1179656 | tf_op jit(solution)/shard_map/ppermute | solution.py:188
  59.3 6.0 %collective-permute-start.7 = (bf16[2304,256]{1,0:T(8,128)(2,1)S(1)}, bf16[2304,256]{1,0:T(8,128)(2,1)S(1)}, u32[]{:S(2)}, u32[]{:S(2)}) collective-permute-start(bf16[2304,256]{1,0:T(8,128)(2,1)S(1)} %pad_maximum_fusion), channel_id=1, source_target_pairs={{0,8},{8,0},{16,24},{24,16},{32,40},{40,32},{48,56},{56,48},{64,72... | collective-permute-start | bytes 3538952 | tf_op jit(solution)/shard_map/ppermute | solution.py:185
  65.3 6.3 %copy-start.5 = (bf16[512,4096]{1,0:T(8,128)(2,1)S(1)}, bf16[512,4096]{1,0:T(8,128)(2,1)}, u32[]{:S(2)}) copy-start(bf16[512,4096]{1,0:T(8,128)(2,1)} %param.11) | copy-start | bytes 12582916

commit v9 on v8

--- a/solution.py
+++ b/solution.py
@@ -206,13 +206,13 @@
 
     swap_02 = swapped(jnp.concatenate([from_02, cross_02]))
     state = attend(common, [from_02, cross_02], plan_02 + cplan_02)
+    state = attend(common, [swap_02], others(plan_02 + cplan_02), state)
     from_46 = after(from_46, *state)
     from_6 = from_46[tok:]
-    cross_46 = crossed(after(from_46, swap_02))
+    cross_46 = crossed(from_46)
     from_8 = shifted(from_6, 4)
     from_7 = lax.ppermute(from_6, "ctx", last)
-    plan = plan_46 + others(plan_02 + cplan_02)
-    state = attend(common, [from_46, swap_02], plan, state)
+    state = attend(common, [from_46], plan_46, state)
     swap_46 = swapped(jnp.concatenate([from_46, from_8, from_7, after(cross_46, *state)]))
     state = attend(common, [cross_46, from_8, from_7], cplan_46 + plan_8 + cplan_7, state)
     plan = others(plan_46 + plan_8 + cplan_7 + cplan_46)

time: 118 us -> 118 us (level); the launches traced: 118 us -> 116 us
  starting transfers between devices: 34.2 us -> 29.9 us
  Pallas kernels: 24.4 us -> 26 us
    ppermute x1, waiting for transfers between devices: 0.01 us -> 4.52 us  [local(): from_7 = lax.ppermute(from_6, 'ctx', last)]
    ppermute x3, starting transfers between devices: 18.4 us -> 14.1 us  [shifted(): lax.ppermute(block, 'ctx', [(i, i + distance) for i in range(ctx_count -...]
    ppermute x3, waiting for transfers between devices: 5.19 us -> 1.85 us  [shifted(): lax.ppermute(block, 'ctx', [(i, i + distance) for i in range(ctx_count -...]
    pallas_call x4 -> x5, Pallas kernels: 24.4 us -> 26 us  [attend(): pl.pallas_call(functools.partial(attend_kernel, counts, plan, state is No...]
  transfers between devices with their start and end apart: 8 -> 8, of which waited for: 4 -> 4; matrix products, arithmetic and copies ran while one was open for 2% -> 2% of each run, Pallas kernels for 15% -> 17%
where the time goes in v9:
time: 118 us; the launch traced here: 116 us
  blocking collectives  43.2 us (37%)
  starting transfers between devices  29.9 us (25%)
  Pallas kernels  26 us (22%)
  waiting for transfers between devices  10.5 us (9%)
  other arithmetic  3.69 us (3%)
  matrix products  1.8 us (2%)
    all_to_all x1, blocking collectives, local(): lax.all_to_all(partial.reshape(shares, tok // shares, -1), 'kvh', 0, 0)  43.2 us
    pallas_call x5, Pallas kernels, attend(): pl.pallas_call(functools.partial(attend_kernel, counts, plan, state is No...  26 us
    ppermute x3, starting transfers between devices, shifted(): lax.ppermute(block, 'ctx', [(i, i + distance) for i in range(ctx_count -...  14.1 us
    ppermute x2, starting transfers between devices, crossed(): return lax.ppermute(block, 'ctx', [(i, i ^ 2) for i in range(ctx_count)])  9.86 us
    ppermute x2, starting transfers between devices, swapped(): return lax.ppermute(block, 'ctx', [(i, i ^ 1) for i in range(ctx_count)])  4.68 us
    ppermute x1, waiting for transfers between devices, local(): from_7 = lax.ppermute(from_6, 'ctx', last)  4.52 us
    ppermute x2, waiting for transfers between devices, crossed(): return lax.ppermute(block, 'ctx', [(i, i ^ 2) for i in range(ctx_count)])  4.14 us
  transfers between devices with their start and end apart: 8, of which 4 were waited for; matrix products, arithmetic and copies ran while one was open for 2% of the time, Pallas kernels for 17%

profile of v9, /device:TPU:96, one launch (start us, length us, event | category | flops | bytes accessed | tf_op | source)
XLA Modules:
  0.0 115.8 jit_solution(16419023168314296006)
XLA Ops:
  0.0 5.0 %collective-permute-start = (bf16[384,256]{1,0:T(8,128)(2,1)}, bf16[384,256]{1,0:T(8,128)(2,1)S(1)}, u32[]{:S(2)}, u32[]{:S(2)}) collective-permute-start(bf16[384,256]{1,0:T(8,128)(2,1)} %param.7), channel_id=1, source_target_pairs={{0,32},{8,40},{16,48},{24,56},{32,64},{40,72},{48,80},{56,88},{64,... | collective-permute-start | bytes 589832 | tf_op jit(solution)/shard_map/ppermute | solution.py:182
  5.0 1.1 convert_multiply_fusion
  6.1 0.0 copy-start.4
  6.1 0.0 copy-start.1
  6.1 0.3 reshape.7
  6.4 0.5 reduce_sum.21
  6.9 0.0 copy-start
  6.9 0.0 copy-start.2
  6.9 0.0 copy-start.3
  6.9 0.7 reduce_max.9
  7.6 0.0 copy-done.4
  7.6 1.8 %collective-permute-done = bf16[384,256]{1,0:T(8,128)(2,1)S(1)} collective-permute-done((bf16[384,256]{1,0:T(8,128)(2,1)}, bf16[384,256]{1,0:T(8,128)(2,1)S(1)}, u32[]{:S(2)}, u32[]{:S(2)}) %collective-permute-start) | collective-permute-done | bytes 196640 | tf_op jit(solution)/shard_map/ppermute | solution.py:182
  9.5 0.0 copy-done.1
  9.5 0.1 broadcast_in_dim.14.starts_ref
  9.6 4.9 %collective-permute-start.2 = (bf16[768,256]{1,0:T(8,128)(2,1)S(1)}, bf16[768,256]{1,0:T(8,128)(2,1)S(1)}, u32[]{:S(2)}, u32[]{:S(2)}) collective-permute-start(bf16[768,256]{1,0:T(8,128)(2,1)S(1)} %constant_dynamic-update-slice_fusion.rest_0_), channel_id=1, source_target_pairs={{0,16},{8,24},{16,0},{24,8},{32,48},{40,56},{48,32},{56,40},{64,80... | collective-permute-start | bytes 1179656 | tf_op jit(solution)/shard_map/ppermute | solution.py:188
  14.6 5.6 %collective-permute-start.1 = (bf16[768,256]{1,0:T(8,128)(2,1)S(1)}, bf16[768,256]{1,0:T(8,128)(2,1)S(1)}, u32[]{:S(2)}, u32[]{:S(2)}) collective-permute-start(bf16[768,256]{1,0:T(8,128)(2,1)S(1)} %constant_dynamic-update-slice_fusion.rest_0_), channel_id=1, source_target_pairs={{0,64},{8,72},{16,80},{24,88},{32,96},{40,104},{48,112},{56,120},{... | collective-permute-start | bytes 1179656 | tf_op jit(solution)/shard_map/ppermute | solution.py:182
  20.2 2.8 %collective-permute-done.2.rest_1_ = bf16[768,256]{1,0:T(8,128)(2,1)S(1)} collective-permute-done((bf16[768,256]{1,0:T(8,128)(2,1)S(1)}, bf16[768,256]{1,0:T(8,128)(2,1)S(1)}, u32[]{:S(2)}, u32[]{:S(2)}) %collective-permute-start.2) | collective-permute-done | bytes 393248 | tf_op jit(solution)/shard_map/ppermute | solution.py:188
  23.0 0.1 pad_maximum_fusion.1
  23.1 1.9 %collective-permute-start.3 = (bf16[1536,256]{1,0:T(8,128)(2,1)S(1)}, bf16[1536,256]{1,0:T(8,128)(2,1)S(1)}, u32[]{:S(2)}, u32[]{:S(2)}) collective-permute-start(bf16[1536,256]{1,0:T(8,128)(2,1)S(1)} %pad_maximum_fusion.1), channel_id=1, source_target_pairs={{0,8},{8,0},{16,24},{24,16},{32,40},{40,32},{48,56},{56,48},{64,72... | collective-permute-start | bytes 2359304 | tf_op jit(solution)/shard_map/ppermute | solution.py:185
  25.0 0.0 copy-done
  25.0 0.0 copy-done.2
  25.0 0.0 copy-done.3
  25.0 6.0 %shard_map.64 = (f32[1536,256]{1,0:T(8,128)S(1)}, f32[1544,128]{1,0:T(8,128)S(1)}) custom-call(s32[1]{0:T(128)} %bitcast.my_ref, s32[384]{0:T(512)S(1)} %copy-done.1, s32[192]{0:T(256)S(1)} %copy-done.2, f32[2,64]{1,0:T(2,128)S(1)} %bitcast.6, f32[1]{0:T(128)} %bitcast.2.norm_ref, s32[384,128]{1,0:T(8,128)S(1)} %broadcast_in_dim.14.starts_ref, ...), custom_call_target="tpu_custom_call" | custom-call | flops 12079595520 | bytes 4194304 | tf_op jit(solution)/shard_map/pallas_call | solution.py:154
  31.1 0.0 collective-permute-done.3.rest_0_
  31.1 5.9 %shard_map.65 = (f32[1536,256]{1,0:T(8,128)S(1)}, f32[1544,128]{1,0:T(8,128)S(1)}) custom-call(s32[1]{0:T(128)} %bitcast.my_ref, s32[384]{0:T(512)S(1)} %copy-done.1, s32[192]{0:T(256)S(1)} %copy-done.2, f32[2,64]{1,0:T(2,128)S(1)} %bitcast.7, f32[1]{0:T(128)} %bitcast.2.norm_ref, ...), custom_call_target="tpu_custom_call", output_to_operand_aliasing={{0}: (8, {}), {1}: (9, {})} | custom-call | flops 12079595520 | bytes 4194304 | tf_op jit(solution)/shard_map/pallas_call | solution.py:154
  37.0 0.0 collective-permute-done.1.rest_0_
  37.0 4.9 %collective-permute-start.6 = (bf16[768,256]{1,0:T(8,128)(2,1)S(1)}, bf16[768,256]{1,0:T(8,128)(2,1)S(1)}, u32[]{:S(2)}, u32[]{:S(2)}) collective-permute-start(bf16[768,256]{1,0:T(8,128)(2,1)S(1)} %collective-permute-done.1.rest_0_), channel_id=1, source_target_pairs={{0,16},{8,24},{16,0},{24,8},{32,48},{40,56},{48,32},{56,40},{64,80... | collective-permute-start | bytes 1179656 | tf_op jit(solution)/shard_map/ppermute | solution.py:188
  42.0 3.4 %collective-permute-start.4 = (bf16[384,256]{1,0:T(8,128)(2,1)S(1)}, bf16[384,256]{1,0:T(8,128)(2,1)S(1)}, u32[]{:S(2)}, u32[]{:S(2)}) collective-permute-start(bf16[384,256]{1,0:T(8,128)(2,1)S(1)} %slice.3), channel_id=1, source_target_pairs={{0,32},{8,40},{16,48},{24,56},{32,64},{40,72},{48,80},{56,88},{64,... | collective-permute-start | bytes 589832 | tf_op jit(solution)/shard_map/ppermute | solution.py:182
  45.4 1.3 %collective-permute-start.5 = (bf16[384,256]{1,0:T(8,128)(2,1)S(1)}, bf16[384,256]{1,0:T(8,128)(2,1)S(1)}, u32[]{:S(2)}, u32[]{:S(2)}) collective-permute-start(bf16[384,256]{1,0:T(8,128)(2,1)S(1)} %slice.3), channel_id=1, source_target_pairs={{16,32},{24,40},{48,64},{56,72},{80,96},{88,104},{112,128},{120,13... | collective-permute-start | bytes 589832 | tf_op jit(solution)/shard_map/ppermute | solution.py:214
  46.7 3.9 %shard_map.66 = (f32[1536,256]{1,0:T(8,128)S(1)}, f32[1544,128]{1,0:T(8,128)S(1)}) custom-call(s32[1]{0:T(128)} %bitcast.my_ref, s32[384]{0:T(512)S(1)} %copy-done.1, s32[192]{0:T(256)S(1)} %copy-done.2, f32[2,64]{1,0:T(2,128)S(1)} %bitcast.8, f32[1]{0:T(128)} %bitcast.2.norm_ref, ...), custom_call_target="tpu_custom_call", output_to_operand_aliasing={{0}: (8, {}), {1}: (9, {})} | custom-call | flops 6039797760 | bytes 4194304 | tf_op jit(solution)/shard_map/pallas_call | solution.py:154
  50.6 1.3 %collective-permute-done.6.rest_0_ = bf16[768,256]{1,0:T(8,128)(2,1)S(1)} collective-permute-done((bf16[768,256]{1,0:T(8,128)(2,1)S(1)}, bf16[768,256]{1,0:T(8,128)(2,1)S(1)}, u32[]{:S(2)}, u32[]{:S(2)}) %collective-permute-start.6) | collective-permute-done | bytes 393248 | tf_op jit(solution)/shard_map/ppermute | solution.py:188
  51.9 0.0 collective-permute-done.4.rest_1_
  51.9 4.5 %collective-permute-done.5.rest_2_ = bf16[384,256]{1,0:T(8,128)(2,1)S(1)} collective-permute-done((bf16[384,256]{1,0:T(8,128)(2,1)S(1)}, bf16[384,256]{1,0:T(8,128)(2,1)S(1)}, u32[]{:S(2)}, u32[]{:S(2)}) %collective-permute-start.5) | collective-permute-done | bytes 196640 | tf_op jit(solution)/shard_map/ppermute | solution.py:214
  56.4 0.1 pad_maximum_fusion
  56.5 2.8 %collective-permute-start.7 = (bf16[2304,256]{1,0:T(8,128)(2,1)S(1)}, bf16[2304,256]{1,0:T(8,128)(2,1)S(1)}, u32[]{:S(2)}, u32[]{:S(2)}) collective-permute-start(bf16[2304,256]{1,0:T(8,128)(2,1)S(1)} %pad_maximum_fusion), channel_id=1, source_target_pairs={{0,8},{8,0},{16,24},{24,16},{32,40},{40,32},{48,56},{56,48},{64,72... | collective-permute-start | bytes 3538952 | tf_op jit(solution)/shard_map/ppermute | solution.py:185
  59.3 3.8 %shard_map.67 = (f32[1536,256]{1,0:T(8,128)S(1)}, f32[1544,128]{1,0:T(8,128)S(1)}) custom-call(s32[1]{0:T(128)} %bitcast.my_ref, s32[384]{0:T(512)S(1)} %copy-done.1, s32[192]{0:T(256)S(1)} %copy-done.2, f32[2,64]{1,0:T(2,128)S(1)} %bitcast.9, f32[1]{0:T(128)} %bitcast.2.norm_ref, ...), custom_call_target="tpu_custom_call", output_to_operand_aliasing={{0}: (10, {}), {1}: (11, {})} | custom-call | flops 12079595520 | bytes 4194304 | tf_op jit(solution)/shard_map/pallas_call | solution.py:154
  63.1 0.0 collective-permute-done.7.rest_0_
  63.1 0.0 copy-start.5
  63.2 6.3 %shard_map.68 = (f32[1536,256]{1,0:T(8,128)S(1)}, f32[1544,128]{1,0:T(8,128)S(1)}, bf16[384,512]{1,0:T(8,128)(2,1)S(1)}) custom-call(s32[1]{0:T(128)} %bitcast.my_ref, s32[384]{0:T(512)S(1)} %copy-done.1, s32[192]{0:T(256)S(1)} %copy-done.2, f32[2,64]{1,0:T(2,128)S(1)} %bitcast.10, f32[1]{0:T(128)} %bitcast.2.norm_ref, ...), custom_call_target="tpu_custom_call", output_to_operand_aliasing={{0}: (8, {}), {1}: (9, {})} | custom-call | flops 18119393280 | bytes 4194304 | tf_op jit(solution)/shard_map/pallas_call | solution.py:154
  69.5 0.0 copy-done.5
  69.5 1.8 %convolution_convert_fusion = bf16[384,4096]{1,0:T(8,128)(2,1)S(1)} fusion(bf16[384,512]{1,0:T(8,128)(2,1)S(1)} %get-tuple-element.28, bf16[512,4096]{1,0:T(8,128)(2,1)S(1)} %copy-done.5), kind=kOutput, calls=%fused_computation | convolution fusion | flops 1612185600 | bytes 7733248 | tf_op jit(solution)/shard_map/dot_general | solution.py:221
  71.3 43.2 %all_to_all.5 = bf16[8,48,4096]{2,1,0:T(8,128)(2,1)S(1)} all-to-all(bf16[8,48,4096]{2,1,0:T(8,128)(2,1)S(1)} %bitcast.11), channel_id=1, replica_groups=mesh['ctx'=64,'kvh'=8] {'kvh'}, dimensions={0} | all-to-all | bytes 6291456 | tf_op jit(solution)/shard_map/all_to_all | solution.py:222
  114.5 1.3 %reduce_sum.22 = bf16[48,4096]{1,0:T(8,128)(2,1)} reduce(bf16[8,48,4096]{2,1,0:T(8,128)(2,1)S(1)} %all_to_all.5, bf16[]{:T(256)} %constant.11.clone.1), dimensions={0}, to_apply=%region_2.0 | reduce | flops 1376256 | bytes 3538946 | tf_op jit(solution)/shard_map/reduce_sum | solution.py:223
  (3 shorter events, 0.0 us)
Async XLA Ops:
  0.0 9.5 %collective-permute-start = (bf16[384,256]{1,0:T(8,128)(2,1)}, bf16[384,256]{1,0:T(8,128)(2,1)S(1)}, u32[]{:S(2)}, u32[]{:S(2)}) collective-permute-start(bf16[384,256]{1,0:T(8,128)(2,1)} %param.7), channel_id=1, source_target_pairs={{0,32},{8,40},{16,48},{24,56},{32,64},{40,72},{48,80},{56,88},{64,... | collective-permute-start | bytes 589832 | tf_op jit(solution)/shard_map/ppermute | solution.py:182
  6.1 1.5 %copy-start.4 = (bf16[384,256]{1,0:T(8,128)(2,1)S(1)}, bf16[384,256]{1,0:T(8,128)(2,1)}, u32[]{:S(2)}) copy-start(bf16[384,256]{1,0:T(8,128)(2,1)} %param.7) | copy-start | bytes 589828
  6.1 3.4 %copy-start.1 = (s32[384]{0:T(512)S(1)}, s32[384]{0:T(512)}, u32[]{:S(2)}) copy-start(s32[384]{0:T(512)} %doc_ref.9) | copy-start | bytes 4612
  6.9 18.1 %copy-start = (bf16[384,512]{1,0:T(8,128)(2,1)S(1)}, bf16[384,512]{1,0:T(8,128)(2,1)}, u32[]{:S(2)}) copy-start(bf16[384,512]{1,0:T(8,128)(2,1)} %query_ref.9) | copy-start | bytes 1179652
  6.9 18.1 %copy-start.2 = (s32[192]{0:T(256)S(1)}, s32[192]{0:T(256)}, u32[]{:S(2)}) copy-start(s32[192]{0:T(256)} %index_ref.9) | copy-start | bytes 2308
  6.9 18.1 %copy-start.3 = (f32[64,2]{0,1:T(2,128)S(1)}, f32[64,2]{0,1:T(2,128)}, u32[]{:S(2)}) copy-start(f32[64,2]{0,1:T(2,128)} %param.10) | copy-start | bytes 1540
  9.6 13.4 %collective-permute-start.2 = (bf16[768,256]{1,0:T(8,128)(2,1)S(1)}, bf16[768,256]{1,0:T(8,128)(2,1)S(1)}, u32[]{:S(2)}, u32[]{:S(2)}) collective-permute-start(bf16[768,256]{1,0:T(8,128)(2,1)S(1)} %constant_dynamic-update-slice_fusion.rest_0_), channel_id=1, source_target_pairs={{0,16},{8,24},{16,0},{24,8},{32,48},{40,56},{48,32},{56,40},{64,80... | collective-permute-start | bytes 1179656 | tf_op jit(solution)/shard_map/ppermute | solution.py:188
  14.6 22.4 %collective-permute-start.1 = (bf16[768,256]{1,0:T(8,128)(2,1)S(1)}, bf16[768,256]{1,0:T(8,128)(2,1)S(1)}, u32[]{:S(2)}, u32[]{:S(2)}) collective-permute-start(bf16[768,256]{1,0:T(8,128)(2,1)S(1)} %constant_dynamic-update-slice_fusion.rest_0_), channel_id=1, source_target_pairs={{0,64},{8,72},{16,80},{24,88},{32,96},{40,104},{48,112},{56,120},{... | collective-permute-start | bytes 1179656 | tf_op jit(solution)/shard_map/ppermute | solution.py:182
  23.1 8.0 %collective-permute-start.3 = (bf16[1536,256]{1,0:T(8,128)(2,1)S(1)}, bf16[1536,256]{1,0:T(8,128)(2,1)S(1)}, u32[]{:S(2)}, u32[]{:S(2)}) collective-permute-start(bf16[1536,256]{1,0:T(8,128)(2,1)S(1)} %pad_maximum_fusion.1), channel_id=1, source_target_pairs={{0,8},{8,0},{16,24},{24,16},{32,40},{40,32},{48,56},{56,48},{64,72... | collective-permute-start | bytes 2359304 | tf_op jit(solution)/shard_map/ppermute | solution.py:185
  37.0 14.9 %collective-permute-start.6 = (bf16[768,256]{1,0:T(8,128)(2,1)S(1)}, bf16[768,256]{1,0:T(8,128)(2,1)S(1)}, u32[]{:S(2)}, u32[]{:S(2)}) collective-permute-start(bf16[768,256]{1,0:T(8,128)(2,1)S(1)} %collective-permute-done.1.rest_0_), channel_id=1, source_target_pairs={{0,16},{8,24},{16,0},{24,8},{32,48},{40,56},{48,32},{56,40},{64,80... | collective-permute-start | bytes 1179656 | tf_op jit(solution)/shard_map/ppermute | solution.py:188
  42.0 10.0 %collective-permute-start.4 = (bf16[384,256]{1,0:T(8,128)(2,1)S(1)}, bf16[384,256]{1,0:T(8,128)(2,1)S(1)}, u32[]{:S(2)}, u32[]{:S(2)}) collective-permute-start(bf16[384,256]{1,0:T(8,128)(2,1)S(1)} %slice.3), channel_id=1, source_target_pairs={{0,32},{8,40},{16,48},{24,56},{32,64},{40,72},{48,80},{56,88},{64,... | collective-permute-start | bytes 589832 | tf_op jit(solution)/shard_map/ppermute | solution.py:182
  45.4 11.0 %collective-permute-start.5 = (bf16[384,256]{1,0:T(8,128)(2,1)S(1)}, bf16[384,256]{1,0:T(8,128)(2,1)S(1)}, u32[]{:S(2)}, u32[]{:S(2)}) collective-permute-start(bf16[384,256]{1,0:T(8,128)(2,1)S(1)} %slice.3), channel_id=1, source_target_pairs={{16,32},{24,40},{48,64},{56,72},{80,96},{88,104},{112,128},{120,13... | collective-permute-start | bytes 589832 | tf_op jit(solution)/shard_map/ppermute | solution.py:214
  56.5 6.6 %collective-permute-start.7 = (bf16[2304,256]{1,0:T(8,128)(2,1)S(1)}, bf16[2304,256]{1,0:T(8,128)(2,1)S(1)}, u32[]{:S(2)}, u32[]{:S(2)}) collective-permute-start(bf16[2304,256]{1,0:T(8,128)(2,1)S(1)} %pad_maximum_fusion), channel_id=1, source_target_pairs={{0,8},{8,0},{16,24},{24,16},{32,40},{40,32},{48,56},{56,48},{64,72... | collective-permute-start | bytes 3538952 | tf_op jit(solution)/shard_map/ppermute | solution.py:185
  63.1 6.3 %copy-start.5 = (bf16[512,4096]{1,0:T(8,128)(2,1)S(1)}, bf16[512,4096]{1,0:T(8,128)(2,1)}, u32[]{:S(2)}) copy-start(bf16[512,4096]{1,0:T(8,128)(2,1)} %param.11) | copy-start | bytes 12582916

commit v10 on v9

--- a/solution.py
+++ b/solution.py
@@ -197,26 +197,30 @@
         return tuple((False, k, cross) for _, k, cross in plan)
 
     from_2 = shifted(keys_values, 4)
-    from_02 = jnp.concatenate([keys_values, after(from_2, norm, starts)])
-    from_46 = shifted(from_02, 8)
-    cross_02 = crossed(from_02)
+    cross_0 = crossed(keys_values)
+    from_4 = shifted(keys_values, 8)
+    from_2 = after(from_2, norm, starts)
+    from_6 = shifted(from_2, 8)
+    from_24 = jnp.concatenate([from_2, from_4])
+    cross_24 = crossed(from_24)
     last = [(i, i + 2) for i in range(ctx_count - 2) if i & 2]
-    plan_02, plan_46, plan_8 = own(0, 2), own(4, 6), own(8)
-    cplan_02, cplan_46, cplan_7 = [tuple((True, k, True) for k in ks) for ks in ((-1, 1), (3, 5), (7,))]
-
-    swap_02 = swapped(jnp.concatenate([from_02, cross_02]))
-    state = attend(common, [from_02, cross_02], plan_02 + cplan_02)
-    state = attend(common, [swap_02], others(plan_02 + cplan_02), state)
-    from_46 = after(from_46, *state)
-    from_6 = from_46[tok:]
-    cross_46 = crossed(from_46)
+
+    def cross(*back):
+        return tuple((True, k, True) for k in back)
+
+    state = attend(common, [keys_values, from_2, cross_0], own(0, 2) + cross(-1))
+    from_6 = after(from_6, *state)
+    swap_024 = swapped(jnp.concatenate([keys_values, from_24, after(cross_0, from_6)]))
+    cross_6 = crossed(from_6)
     from_8 = shifted(from_6, 4)
     from_7 = lax.ppermute(from_6, "ctx", last)
-    state = attend(common, [from_46], plan_46, state)
-    swap_46 = swapped(jnp.concatenate([from_46, from_8, from_7, after(cross_46, *state)]))
-    state = attend(common, [cross_46, from_8, from_7], cplan_46 + plan_8 + cplan_7, state)
-    plan = others(plan_46 + plan_8 + cplan_7 + cplan_46)
-    _, _, attn = attend(common, [swap_46], plan, state, True)
+    plan = own(4, 6) + others(own(0, 2, 4) + cross(-1))
+    state = attend(common, [from_4, from_6, swap_024], plan, state)
+    swap_6 = swapped(jnp.concatenate([cross_24, from_6, from_8, from_7, after(cross_6, *state)]))
+    plan = cross(1, 3, 5) + own(8) + cross(7)
+    state = attend(common, [cross_24, cross_6, from_8, from_7], plan, state)
+    plan = others(cross(1, 3) + own(6, 8) + cross(7, 5))
+    _, _, attn = attend(common, [swap_6], plan, state, True)
     shares = lax.axis_size("kvh")
     partial = jnp.dot(attn, out_weight, preferred_element_type=jnp.float32).astype(jnp.bfloat16)
     pieces = lax.all_to_all(partial.reshape(shares, tok // shares, -1), "kvh", 0, 0)

time: 118 us -> 129 us (1.093)
  the two profiles are of different devices: /device:TPU:96 before, /device:TPU:224 now
where the time goes in v10:
time: 129 us
  blocking collectives  43.1 us (33%)
  starting transfers between devices  36 us (28%)
  Pallas kernels  28.8 us (22%)
  waiting for transfers between devices  14.6 us (11%)
  other arithmetic  3.68 us (3%)
  matrix products  1.8 us (1%)
    all_to_all x1, blocking collectives, local(): lax.all_to_all(partial.reshape(shares, tok // shares, -1), 'kvh', 0, 0)  43.1 us
    pallas_call x4, Pallas kernels, attend(): pl.pallas_call(functools.partial(attend_kernel, counts, plan, state is No...  28.8 us
    ppermute x4, starting transfers between devices, shifted(): lax.ppermute(block, 'ctx', [(i, i + distance) for i in range(ctx_count -...  16.3 us
    ppermute x3, starting transfers between devices, crossed(): return lax.ppermute(block, 'ctx', [(i, i ^ 2) for i in range(ctx_count)])  14.4 us
    ppermute x4, waiting for transfers between devices, shifted(): lax.ppermute(block, 'ctx', [(i, i + distance) for i in range(ctx_count -...  8.08 us
    ppermute x1, waiting for transfers between devices, local(): from_7 = lax.ppermute(from_6, 'ctx', last)  6.5 us
    ppermute x2, starting transfers between devices, swapped(): return lax.ppermute(block, 'ctx', [(i, i ^ 1) for i in range(ctx_count)])  3.84 us
  transfers between devices with their start and end apart: 10, of which 3 were waited for; matrix products, arithmetic and copies ran while one was open for 2% of the time, Pallas kernels for 16%

profile of v10, /device:TPU:224, one launch (start us, length us, event | category | flops | bytes accessed | tf_op | source)
XLA Modules:
  0.0 128.8 jit_solution(9443510448652576260)
XLA Ops:
  0.0 5.0 %collective-permute-start = (bf16[384,256]{1,0:T(8,128)(2,1)}, bf16[384,256]{1,0:T(8,128)(2,1)S(1)}, u32[]{:S(2)}, u32[]{:S(2)}) collective-permute-start(bf16[384,256]{1,0:T(8,128)(2,1)} %rest_0_.1), channel_id=1, source_target_pairs={{0,32},{8,40},{16,48},{24,56},{32,64},{40,72},{48,80},{56,88},{64,... | collective-permute-start | bytes 589832 | tf_op jit(solution)/shard_map/ppermute | solution.py:182
  5.0 4.9 %collective-permute-start.4 = (bf16[384,256]{1,0:T(8,128)(2,1)}, bf16[384,256]{1,0:T(8,128)(2,1)S(1)}, u32[]{:S(2)}, u32[]{:S(2)}) collective-permute-start(bf16[384,256]{1,0:T(8,128)(2,1)} %rest_0_.1), channel_id=1, source_target_pairs={{0,16},{8,24},{16,0},{24,8},{32,48},{40,56},{48,32},{56,40},{64,80... | collective-permute-start | bytes 589832 | tf_op jit(solution)/shard_map/ppermute | solution.py:188
  10.0 3.4 %collective-permute-start.1 = (bf16[384,256]{1,0:T(8,128)(2,1)}, bf16[384,256]{1,0:T(8,128)(2,1)S(1)}, u32[]{:S(2)}, u32[]{:S(2)}) collective-permute-start(bf16[384,256]{1,0:T(8,128)(2,1)} %rest_0_.1), channel_id=1, source_target_pairs={{0,64},{8,72},{16,80},{24,88},{32,96},{40,104},{48,112},{56,120},{... | collective-permute-start | bytes 589832 | tf_op jit(solution)/shard_map/ppermute | solution.py:182
  13.4 1.1 convert_multiply_fusion
  14.5 0.0 copy-start.2
  14.5 0.0 copy-start
  14.5 0.0 copy-start.1
  14.5 0.0 copy-start.3
  14.5 0.0 copy-start.4
  14.5 0.3 reshape.7
  14.8 0.5 reduce_sum.21
  15.3 0.7 reduce_max.9
  16.0 0.0 collective-permute-done.rest_1_
  16.0 0.0 copy-done.2
  16.0 0.1 broadcast_in_dim.14.starts_ref
  16.1 3.4 %collective-permute-start.3 = (bf16[384,256]{1,0:T(8,128)(2,1)S(1)}, bf16[384,256]{1,0:T(8,128)(2,1)S(1)}, u32[]{:S(2)}, u32[]{:S(2)}) collective-permute-start(bf16[384,256]{1,0:T(8,128)(2,1)S(1)} %collective-permute-done.rest_1_), channel_id=1, source_target_pairs={{0,64},{8,72},{16,80},{24,88},{32,96},{40,104},{48,112},{56,120},{... | collective-permute-start | bytes 589832 | tf_op jit(solution)/shard_map/ppermute | solution.py:182
  19.5 5.1 %collective-permute-done.1.rest_0_ = bf16[384,256]{1,0:T(8,128)(2,1)S(1)} collective-permute-done((bf16[384,256]{1,0:T(8,128)(2,1)}, bf16[384,256]{1,0:T(8,128)(2,1)S(1)}, u32[]{:S(2)}, u32[]{:S(2)}) %collective-permute-start.1) | collective-permute-done | bytes 196640 | tf_op jit(solution)/shard_map/ppermute | solution.py:182
  24.6 2.4 %collective-permute-start.2 = (bf16[768,256]{1,0:T(8,128)(2,1)S(1)}, bf16[768,256]{1,0:T(8,128)(2,1)S(1)}, u32[]{:S(2)}, u32[]{:S(2)}) collective-permute-start(bf16[768,256]{1,0:T(8,128)(2,1)S(1)} %pad_maximum_fusion.1), channel_id=1, source_target_pairs={{0,16},{8,24},{16,0},{24,8},{32,48},{40,56},{48,32},{56,40},{64,80... | collective-permute-start | bytes 1179656 | tf_op jit(solution)/shard_map/ppermute | solution.py:188
  27.1 0.0 collective-permute-done.4.rest_2_
  27.1 0.0 copy-done
  27.1 0.0 copy-done.1
  27.1 0.0 copy-done.3
  27.1 0.0 copy-done.4
  27.1 3.9 %shard_map.64 = (f32[1536,256]{1,0:T(8,128)S(1)}, f32[1544,128]{1,0:T(8,128)S(1)}) custom-call(s32[1]{0:T(128)} %bitcast.my_ref, s32[384]{0:T(512)S(1)} %copy-done.2, s32[192]{0:T(256)S(1)} %copy-done.3, f32[2,64]{1,0:T(2,128)S(1)} %bitcast.6, f32[1]{0:T(128)} %bitcast.2.norm_ref, s32[384,128]{1,0:T(8,128)S(1)} %broadcast_in_dim.14.starts_ref, ...), custom_call_target="tpu_custom_call" | custom-call | flops 9059696640 | bytes 4194304 | tf_op jit(solution)/shard_map/pallas_call | solution.py:154
  31.0 0.0 collective-permute-done.3.rest_1_
  31.1 0.1 pad_maximum_fusion
  31.1 1.9 %collective-permute-start.8 = (bf16[1536,256]{1,0:T(8,128)(2,1)S(1)}, bf16[1536,256]{1,0:T(8,128)(2,1)S(1)}, u32[]{:S(2)}, u32[]{:S(2)}) collective-permute-start(bf16[1536,256]{1,0:T(8,128)(2,1)S(1)} %pad_maximum_fusion), channel_id=1, source_target_pairs={{0,8},{8,0},{16,24},{24,16},{32,40},{40,32},{48,56},{56,48},{64,72... | collective-permute-start | bytes 2359304 | tf_op jit(solution)/shard_map/ppermute | solution.py:185
  33.0 7.0 %collective-permute-start.7 = (bf16[384,256]{1,0:T(8,128)(2,1)S(1)}, bf16[384,256]{1,0:T(8,128)(2,1)S(1)}, u32[]{:S(2)}, u32[]{:S(2)}) collective-permute-start(bf16[384,256]{1,0:T(8,128)(2,1)S(1)} %collective-permute-done.3.rest_1_), channel_id=1, source_target_pairs={{0,16},{8,24},{16,0},{24,8},{32,48},{40,56},{48,32},{56,40},{64,80... | collective-permute-start | bytes 589832 | tf_op jit(solution)/shard_map/ppermute | solution.py:188
  40.1 4.5 %collective-permute-start.5 = (bf16[384,256]{1,0:T(8,128)(2,1)S(1)}, bf16[384,256]{1,0:T(8,128)(2,1)S(1)}, u32[]{:S(2)}, u32[]{:S(2)}) collective-permute-start(bf16[384,256]{1,0:T(8,128)(2,1)S(1)} %collective-permute-done.3.rest_1_), channel_id=1, source_target_pairs={{0,32},{8,40},{16,48},{24,56},{32,64},{40,72},{48,80},{56,88},{64,... | collective-permute-start | bytes 589832 | tf_op jit(solution)/shard_map/ppermute | solution.py:182
  44.6 1.5 %collective-permute-start.6 = (bf16[384,256]{1,0:T(8,128)(2,1)S(1)}, bf16[384,256]{1,0:T(8,128)(2,1)S(1)}, u32[]{:S(2)}, u32[]{:S(2)}) collective-permute-start(bf16[384,256]{1,0:T(8,128)(2,1)S(1)} %collective-permute-done.3.rest_1_), channel_id=1, source_target_pairs={{16,32},{24,40},{48,64},{56,72},{80,96},{88,104},{112,128},{120,13... | collective-permute-start | bytes 589832 | tf_op jit(solution)/shard_map/ppermute | solution.py:216
  46.1 0.0 collective-permute-done.2.rest_0_
  46.1 3.0 %collective-permute-done.5.rest_2_ = bf16[384,256]{1,0:T(8,128)(2,1)S(1)} collective-permute-done((bf16[384,256]{1,0:T(8,128)(2,1)S(1)}, bf16[384,256]{1,0:T(8,128)(2,1)S(1)}, u32[]{:S(2)}, u32[]{:S(2)}) %collective-permute-start.5) | collective-permute-done | bytes 196640 | tf_op jit(solution)/shard_map/ppermute | solution.py:182
  49.1 6.5 %collective-permute-done.6.rest_3_ = bf16[384,256]{1,0:T(8,128)(2,1)S(1)} collective-permute-done((bf16[384,256]{1,0:T(8,128)(2,1)S(1)}, bf16[384,256]{1,0:T(8,128)(2,1)S(1)}, u32[]{:S(2)}, u32[]{:S(2)}) %collective-permute-start.6) | collective-permute-done | bytes 196640 | tf_op jit(solution)/shard_map/ppermute | solution.py:216
  55.7 0.0 collective-permute-done.8.rest_2_
  55.7 8.1 %shard_map.65 = (f32[1536,256]{1,0:T(8,128)S(1)}, f32[1544,128]{1,0:T(8,128)S(1)}) custom-call(s32[1]{0:T(128)} %bitcast.my_ref, s32[384]{0:T(512)S(1)} %copy-done.2, s32[192]{0:T(256)S(1)} %copy-done.3, f32[2,64]{1,0:T(2,128)S(1)} %bitcast.7, f32[1]{0:T(128)} %bitcast.2.norm_ref, ...), custom_call_target="tpu_custom_call", output_to_operand_aliasing={{0}: (10, {}), {1}: (11, {})} | custom-call | flops 18119393280 | bytes 4194304 | tf_op jit(solution)/shard_map/pallas_call | solution.py:154
  63.8 0.0 collective-permute-done.7.rest_1_
  63.8 1.9 %collective-permute-start.9 = (bf16[2304,256]{1,0:T(8,128)(2,1)S(1)}, bf16[2304,256]{1,0:T(8,128)(2,1)S(1)}, u32[]{:S(2)}, u32[]{:S(2)}) collective-permute-start(bf16[2304,256]{1,0:T(8,128)(2,1)S(1)} %constant_dynamic-update-slice_fusion), channel_id=1, source_target_pairs={{0,8},{8,0},{16,24},{24,16},{32,40},{40,32},{48,56},{56,48},{64,72... | collective-permute-start | bytes 3538952 | tf_op jit(solution)/shard_map/ppermute | solution.py:185
  65.8 8.3 %shard_map.66 = (f32[1536,256]{1,0:T(8,128)S(1)}, f32[1544,128]{1,0:T(8,128)S(1)}) custom-call(s32[1]{0:T(128)} %bitcast.my_ref, s32[384]{0:T(512)S(1)} %copy-done.2, s32[192]{0:T(256)S(1)} %copy-done.3, f32[2,64]{1,0:T(2,128)S(1)} %bitcast.8, f32[1]{0:T(128)} %bitcast.2.norm_ref, ...), custom_call_target="tpu_custom_call", output_to_operand_aliasing={{0}: (11, {}), {1}: (12, {})} | custom-call | flops 15099494400 | bytes 4194304 | tf_op jit(solution)/shard_map/pallas_call | solution.py:154
  74.1 0.0 collective-permute-done.9.rest_0_
  74.1 0.0 copy-start.5
  74.1 8.4 %shard_map.67 = (f32[1536,256]{1,0:T(8,128)S(1)}, f32[1544,128]{1,0:T(8,128)S(1)}, bf16[384,512]{1,0:T(8,128)(2,1)S(1)}) custom-call(s32[1]{0:T(128)} %bitcast.my_ref, s32[384]{0:T(512)S(1)} %copy-done.2, s32[192]{0:T(256)S(1)} %copy-done.3, f32[2,64]{1,0:T(2,128)S(1)} %bitcast.9, f32[1]{0:T(128)} %bitcast.2.norm_ref, ...), custom_call_target="tpu_custom_call", output_to_operand_aliasing={{0}: (8, {}), {1}: (9, {})} | custom-call | flops 18119393280 | bytes 4194304 | tf_op jit(solution)/shard_map/pallas_call | solution.py:154
  82.5 0.0 copy-done.5
  82.5 1.8 %convolution_convert_fusion = bf16[384,4096]{1,0:T(8,128)(2,1)S(1)} fusion(bf16[384,512]{1,0:T(8,128)(2,1)S(1)} %get-tuple-element.26, bf16[512,4096]{1,0:T(8,128)(2,1)S(1)} %copy-done.5), kind=kOutput, calls=%fused_computation | convolution fusion | flops 1612185600 | bytes 7733248 | tf_op jit(solution)/shard_map/dot_general | solution.py:225
  84.3 43.1 %all_to_all.5 = bf16[8,48,4096]{2,1,0:T(8,128)(2,1)S(1)} all-to-all(bf16[8,48,4096]{2,1,0:T(8,128)(2,1)S(1)} %bitcast.10), channel_id=1, replica_groups=mesh['ctx'=64,'kvh'=8] {'kvh'}, dimensions={0} | all-to-all | bytes 6291456 | tf_op jit(solution)/shard_map/all_to_all | solution.py:226
  127.5 1.3 %reduce_sum.22 = bf16[48,4096]{1,0:T(8,128)(2,1)} reduce(bf16[8,48,4096]{2,1,0:T(8,128)(2,1)S(1)} %all_to_all.5, bf16[]{:T(256)} %constant.11.clone.1), dimensions={0}, to_apply=%region_2.0 | reduce | flops 1376256 | bytes 3538946 | tf_op jit(solution)/shard_map/reduce_sum | solution.py:227
  (6 shorter events, 0.1 us)
Async XLA Ops:
  0.0 16.0 %collective-permute-start = (bf16[384,256]{1,0:T(8,128)(2,1)}, bf16[384,256]{1,0:T(8,128)(2,1)S(1)}, u32[]{:S(2)}, u32[]{:S(2)}) collective-permute-start(bf16[384,256]{1,0:T(8,128)(2,1)} %rest_0_.1), channel_id=1, source_target_pairs={{0,32},{8,40},{16,48},{24,56},{32,64},{40,72},{48,80},{56,88},{64,... | collective-permute-start | bytes 589832 | tf_op jit(solution)/shard_map/ppermute | solution.py:182
  5.0 22.0 %collective-permute-start.4 = (bf16[384,256]{1,0:T(8,128)(2,1)}, bf16[384,256]{1,0:T(8,128)(2,1)S(1)}, u32[]{:S(2)}, u32[]{:S(2)}) collective-permute-start(bf16[384,256]{1,0:T(8,128)(2,1)} %rest_0_.1), channel_id=1, source_target_pairs={{0,16},{8,24},{16,0},{24,8},{32,48},{40,56},{48,32},{56,40},{64,80... | collective-permute-start | bytes 589832 | tf_op jit(solution)/shard_map/ppermute | solution.py:188
  10.0 14.6 %collective-permute-start.1 = (bf16[384,256]{1,0:T(8,128)(2,1)}, bf16[384,256]{1,0:T(8,128)(2,1)S(1)}, u32[]{:S(2)}, u32[]{:S(2)}) collective-permute-start(bf16[384,256]{1,0:T(8,128)(2,1)} %rest_0_.1), channel_id=1, source_target_pairs={{0,64},{8,72},{16,80},{24,88},{32,96},{40,104},{48,112},{56,120},{... | collective-permute-start | bytes 589832 | tf_op jit(solution)/shard_map/ppermute | solution.py:182
  14.5 1.6 %copy-start.2 = (s32[384]{0:T(512)S(1)}, s32[384]{0:T(512)}, u32[]{:S(2)}) copy-start(s32[384]{0:T(512)} %doc_ref.7) | copy-start | bytes 4612
  14.5 12.6 %copy-start = (bf16[384,512]{1,0:T(8,128)(2,1)S(1)}, bf16[384,512]{1,0:T(8,128)(2,1)}, u32[]{:S(2)}) copy-start(bf16[384,512]{1,0:T(8,128)(2,1)} %query_ref.7) | copy-start | bytes 1179652
  14.5 12.6 %copy-start.1 = (bf16[384,256]{1,0:T(8,128)(2,1)S(1)}, bf16[384,256]{1,0:T(8,128)(2,1)}, u32[]{:S(2)}) copy-start(bf16[384,256]{1,0:T(8,128)(2,1)} %rest_0_.1) | copy-start | bytes 589828
  14.5 12.6 %copy-start.3 = (s32[192]{0:T(256)S(1)}, s32[192]{0:T(256)}, u32[]{:S(2)}) copy-start(s32[192]{0:T(256)} %index_ref.7) | copy-start | bytes 2308
  14.5 12.6 %copy-start.4 = (f32[64,2]{0,1:T(2,128)S(1)}, f32[64,2]{0,1:T(2,128)}, u32[]{:S(2)}) copy-start(f32[64,2]{0,1:T(2,128)} %param.10) | copy-start | bytes 1540
  16.1 14.9 %collective-permute-start.3 = (bf16[384,256]{1,0:T(8,128)(2,1)S(1)}, bf16[384,256]{1,0:T(8,128)(2,1)S(1)}, u32[]{:S(2)}, u32[]{:S(2)}) collective-permute-start(bf16[384,256]{1,0:T(8,128)(2,1)S(1)} %collective-permute-done.rest_1_), channel_id=1, source_target_pairs={{0,64},{8,72},{16,80},{24,88},{32,96},{40,104},{48,112},{56,120},{... | collective-permute-start | bytes 589832 | tf_op jit(solution)/shard_map/ppermute | solution.py:182
  24.6 21.4 %collective-permute-start.2 = (bf16[768,256]{1,0:T(8,128)(2,1)S(1)}, bf16[768,256]{1,0:T(8,128)(2,1)S(1)}, u32[]{:S(2)}, u32[]{:S(2)}) collective-permute-start(bf16[768,256]{1,0:T(8,128)(2,1)S(1)} %pad_maximum_fusion.1), channel_id=1, source_target_pairs={{0,16},{8,24},{16,0},{24,8},{32,48},{40,56},{48,32},{56,40},{64,80... | collective-permute-start | bytes 1179656 | tf_op jit(solution)/shard_map/ppermute | solution.py:188
  31.1 24.5 %collective-permute-start.8 = (bf16[1536,256]{1,0:T(8,128)(2,1)S(1)}, bf16[1536,256]{1,0:T(8,128)(2,1)S(1)}, u32[]{:S(2)}, u32[]{:S(2)}) collective-permute-start(bf16[1536,256]{1,0:T(8,128)(2,1)S(1)} %pad_maximum_fusion), channel_id=1, source_target_pairs={{0,8},{8,0},{16,24},{24,16},{32,40},{40,32},{48,56},{56,48},{64,72... | collective-permute-start | bytes 2359304 | tf_op jit(solution)/shard_map/ppermute | solution.py:185
  33.0 30.8 %collective-permute-start.7 = (bf16[384,256]{1,0:T(8,128)(2,1)S(1)}, bf16[384,256]{1,0:T(8,128)(2,1)S(1)}, u32[]{:S(2)}, u32[]{:S(2)}) collective-permute-start(bf16[384,256]{1,0:T(8,128)(2,1)S(1)} %collective-permute-done.3.rest_1_), channel_id=1, source_target_pairs={{0,16},{8,24},{16,0},{24,8},{32,48},{40,56},{48,32},{56,40},{64,80... | collective-permute-start | bytes 589832 | tf_op jit(solution)/shard_map/ppermute | solution.py:188
  40.1 9.1 %collective-permute-start.5 = (bf16[384,256]{1,0:T(8,128)(2,1)S(1)}, bf16[384,256]{1,0:T(8,128)(2,1)S(1)}, u32[]{:S(2)}, u32[]{:S(2)}) collective-permute-start(bf16[384,256]{1,0:T(8,128)(2,1)S(1)} %collective-permute-done.3.rest_1_), channel_id=1, source_target_pairs={{0,32},{8,40},{16,48},{24,56},{32,64},{40,72},{48,80},{56,88},{64,... | collective-permute-start | bytes 589832 | tf_op jit(solution)/shard_map/ppermute | solution.py:182
  44.6 11.0 %collective-permute-start.6 = (bf16[384,256]{1,0:T(8,128)(2,1)S(1)}, bf16[384,256]{1,0:T(8,128)(2,1)S(1)}, u32[]{:S(2)}, u32[]{:S(2)}) collective-permute-start(bf16[384,256]{1,0:T(8,128)(2,1)S(1)} %collective-permute-done.3.rest_1_), channel_id=1, source_target_pairs={{16,32},{24,40},{48,64},{56,72},{80,96},{88,104},{112,128},{120,13... | collective-permute-start | bytes 589832 | tf_op jit(solution)/shard_map/ppermute | solution.py:216
  63.8 10.2 %collective-permute-start.9 = (bf16[2304,256]{1,0:T(8,128)(2,1)S(1)}, bf16[2304,256]{1,0:T(8,128)(2,1)S(1)}, u32[]{:S(2)}, u32[]{:S(2)}) collective-permute-start(bf16[2304,256]{1,0:T(8,128)(2,1)S(1)} %constant_dynamic-update-slice_fusion), channel_id=1, source_target_pairs={{0,8},{8,0},{16,24},{24,16},{32,40},{40,32},{48,56},{56,48},{64,72... | collective-permute-start | bytes 3538952 | tf_op jit(solution)/shard_map/ppermute | solution.py:185
  74.1 8.4 %copy-start.5 = (bf16[512,4096]{1,0:T(8,128)(2,1)S(1)}, bf16[512,4096]{1,0:T(8,128)(2,1)}, u32[]{:S(2)}) copy-start(bf16[512,4096]{1,0:T(8,128)(2,1)} %param.11) | copy-start | bytes 12582916

commit v11 on v10

--- a/solution.py
+++ b/solution.py
@@ -210,17 +210,18 @@
 
     state = attend(common, [keys_values, from_2, cross_0], own(0, 2) + cross(-1))
     from_6 = after(from_6, *state)
-    swap_024 = swapped(jnp.concatenate([keys_values, from_24, after(cross_0, from_6)]))
     cross_6 = crossed(from_6)
     from_8 = shifted(from_6, 4)
     from_7 = lax.ppermute(from_6, "ctx", last)
-    plan = own(4, 6) + others(own(0, 2, 4) + cross(-1))
-    state = attend(common, [from_4, from_6, swap_024], plan, state)
-    swap_6 = swapped(jnp.concatenate([cross_24, from_6, from_8, from_7, after(cross_6, *state)]))
-    plan = cross(1, 3, 5) + own(8) + cross(7)
-    state = attend(common, [cross_24, cross_6, from_8, from_7], plan, state)
-    plan = others(cross(1, 3) + own(6, 8) + cross(7, 5))
-    _, _, attn = attend(common, [swap_6], plan, state, True)
+    first = jnp.concatenate([keys_values, from_24, cross_0, cross_24])
+    first_swap = swapped(after(first, from_6))
+    state = attend(common, [from_4, from_6, cross_24], own(4, 6) + cross(1, 3), state)
+    state = attend(common, [first_swap], others(own(0, 2, 4) + cross(-1, 1, 3)), state)
+    from_8, from_7, cross_6, *_ = lax.optimization_barrier((from_8, from_7, cross_6, *state))
+    second_swap = swapped(jnp.concatenate([from_6, from_8, from_7, cross_6]))
+    state = attend(common, [cross_6, from_8, from_7], cross(5) + own(8) + cross(7), state)
+    plan = others(own(6, 8) + cross(7, 5))
+    _, _, attn = attend(common, [second_swap], plan, state, True)
     shares = lax.axis_size("kvh")
     partial = jnp.dot(attn, out_weight, preferred_element_type=jnp.float32).astype(jnp.bfloat16)
     pieces = lax.all_to_all(partial.reshape(shares, tok // shares, -1), "kvh", 0, 0)

time: 129 us -> 124 us (0.961)
  the two profiles are of different devices: /device:TPU:224 before, /device:TPU:160 now
where the time goes in v11:
time: 124 us; the launch traced here: 123 us
  blocking collectives  43.1 us (35%)
  starting transfers between devices  37.1 us (30%)
  Pallas kernels  28 us (23%)
  waiting for transfers between devices  8.67 us (7%)
  other arithmetic  3.64 us (3%)
  matrix products  1.8 us (1%)
    all_to_all x1, blocking collectives, local(): lax.all_to_all(partial.reshape(shares, tok // shares, -1), 'kvh', 0, 0)  43.1 us
    pallas_call x5, Pallas kernels, attend(): pl.pallas_call(functools.partial(attend_kernel, counts, plan, state is No...  28 us
    ppermute x4, starting transfers between devices, shifted(): lax.ppermute(block, 'ctx', [(i, i + distance) for i in range(ctx_count -...  16.4 us
    ppermute x3, starting transfers between devices, crossed(): return lax.ppermute(block, 'ctx', [(i, i ^ 2) for i in range(ctx_count)])  15.3 us
    ppermute x3, waiting for transfers between devices, crossed(): return lax.ppermute(block, 'ctx', [(i, i ^ 2) for i in range(ctx_count)])  4.7 us
    ppermute x2, starting transfers between devices, swapped(): return lax.ppermute(block, 'ctx', [(i, i ^ 1) for i in range(ctx_count)])  4.06 us
    ppermute x4, waiting for transfers between devices, shifted(): lax.ppermute(block, 'ctx', [(i, i + distance) for i in range(ctx_count -...  3.96 us
  transfers between devices with their start and end apart: 10, of which 2 were waited for; matrix products, arithmetic and copies ran while one was open for 2% of the time, Pallas kernels for 18%

profile of v11, /device:TPU:160, one launch (start us, length us, event | category | flops | bytes accessed | tf_op | source)
XLA Modules:
  0.0 123.2 jit_solution(18159003449131198336)
XLA Ops:
  0.0 3.8 %collective-permute-start = (bf16[384,256]{1,0:T(8,128)(2,1)}, bf16[384,256]{1,0:T(8,128)(2,1)S(1)}, u32[]{:S(2)}, u32[]{:S(2)}) collective-permute-start(bf16[384,256]{1,0:T(8,128)(2,1)} %rest_0_.1), channel_id=1, source_target_pairs={{0,32},{8,40},{16,48},{24,56},{32,64},{40,72},{48,80},{56,88},{64,... | collective-permute-start | bytes 589832 | tf_op jit(solution)/shard_map/ppermute | solution.py:182
  3.8 4.9 %collective-permute-start.2 = (bf16[384,256]{1,0:T(8,128)(2,1)}, bf16[384,256]{1,0:T(8,128)(2,1)S(1)}, u32[]{:S(2)}, u32[]{:S(2)}) collective-permute-start(bf16[384,256]{1,0:T(8,128)(2,1)} %rest_0_.1), channel_id=1, source_target_pairs={{0,16},{8,24},{16,0},{24,8},{32,48},{40,56},{48,32},{56,40},{64,80... | collective-permute-start | bytes 589832 | tf_op jit(solution)/shard_map/ppermute | solution.py:188
  8.8 6.4 %collective-permute-start.6 = (bf16[384,256]{1,0:T(8,128)(2,1)}, bf16[384,256]{1,0:T(8,128)(2,1)S(1)}, u32[]{:S(2)}, u32[]{:S(2)}) collective-permute-start(bf16[384,256]{1,0:T(8,128)(2,1)} %rest_0_.1), channel_id=1, source_target_pairs={{0,64},{8,72},{16,80},{24,88},{32,96},{40,104},{48,112},{56,120},{... | collective-permute-start | bytes 589832 | tf_op jit(solution)/shard_map/ppermute | solution.py:182
  15.2 1.1 convert_multiply_fusion
  16.3 0.0 copy-start.1
  16.3 0.0 copy-start.2
  16.3 0.3 reshape.7
  16.6 0.0 copy-start
  16.6 0.0 copy-start.3
  16.6 0.0 copy-start.4
  16.6 0.5 reduce_sum.21
  17.1 0.7 reduce_max.9
  17.8 0.0 copy-done.1
  17.8 0.0 collective-permute-done.rest_1_
  17.8 0.0 copy-done.2
  17.8 0.1 broadcast_in_dim.14.starts_ref
  17.9 3.4 %collective-permute-start.1 = (bf16[384,256]{1,0:T(8,128)(2,1)S(1)}, bf16[384,256]{1,0:T(8,128)(2,1)S(1)}, u32[]{:S(2)}, u32[]{:S(2)}) collective-permute-start(bf16[384,256]{1,0:T(8,128)(2,1)S(1)} %collective-permute-done.rest_1_), channel_id=1, source_target_pairs={{0,64},{8,72},{16,80},{24,88},{32,96},{40,104},{48,112},{56,120},{... | collective-permute-start | bytes 589832 | tf_op jit(solution)/shard_map/ppermute | solution.py:182
  21.3 4.0 %collective-permute-done.6.rest_0_ = bf16[384,256]{1,0:T(8,128)(2,1)S(1)} collective-permute-done((bf16[384,256]{1,0:T(8,128)(2,1)}, bf16[384,256]{1,0:T(8,128)(2,1)S(1)}, u32[]{:S(2)}, u32[]{:S(2)}) %collective-permute-start.6) | collective-permute-done | bytes 196640 | tf_op jit(solution)/shard_map/ppermute | solution.py:182
  25.3 2.4 %collective-permute-start.7 = (bf16[768,256]{1,0:T(8,128)(2,1)S(1)}, bf16[768,256]{1,0:T(8,128)(2,1)S(1)}, u32[]{:S(2)}, u32[]{:S(2)}) collective-permute-start(bf16[768,256]{1,0:T(8,128)(2,1)S(1)} %pad_maximum_fusion.1), channel_id=1, source_target_pairs={{0,16},{8,24},{16,0},{24,8},{32,48},{40,56},{48,32},{56,40},{64,80... | collective-permute-start | bytes 1179656 | tf_op jit(solution)/shard_map/ppermute | solution.py:188
  27.7 0.0 collective-permute-done.2.rest_2_
  27.7 0.0 copy-done
  27.7 0.0 copy-done.3
  27.7 0.0 copy-done.4
  27.8 3.9 %shard_map.64 = (f32[1536,256]{1,0:T(8,128)S(1)}, f32[1544,128]{1,0:T(8,128)S(1)}) custom-call(s32[1]{0:T(128)} %bitcast.my_ref, s32[384]{0:T(512)S(1)} %copy-done.2, s32[192]{0:T(256)S(1)} %copy-done.3, f32[2,64]{1,0:T(2,128)S(1)} %bitcast.6, f32[1]{0:T(128)} %bitcast.2.norm_ref, s32[384,128]{1,0:T(8,128)S(1)} %broadcast_in_dim.14.starts_ref, ...), custom_call_target="tpu_custom_call" | custom-call | flops 9059696640 | bytes 4194304 | tf_op jit(solution)/shard_map/pallas_call | solution.py:154
  31.8 0.0 collective-permute-done.1.rest_1_
  31.8 4.7 %collective-permute-done.7.rest_2_ = bf16[768,256]{1,0:T(8,128)(2,1)S(1)} collective-permute-done((bf16[768,256]{1,0:T(8,128)(2,1)S(1)}, bf16[768,256]{1,0:T(8,128)(2,1)S(1)}, u32[]{:S(2)}, u32[]{:S(2)}) %collective-permute-start.7) | collective-permute-done | bytes 393248 | tf_op jit(solution)/shard_map/ppermute | solution.py:188
  36.5 1.9 %collective-permute-start.8 = (bf16[2304,256]{1,0:T(8,128)(2,1)S(1)}, bf16[2304,256]{1,0:T(8,128)(2,1)S(1)}, u32[]{:S(2)}, u32[]{:S(2)}) collective-permute-start(bf16[2304,256]{1,0:T(8,128)(2,1)S(1)} %constant_dynamic-update-slice_fusion), channel_id=1, source_target_pairs={{0,8},{8,0},{16,24},{24,16},{32,40},{40,32},{48,56},{56,48},{64,72... | collective-permute-start | bytes 3538952 | tf_op jit(solution)/shard_map/ppermute | solution.py:185
  38.4 2.8 %collective-permute-start.3 = (bf16[384,256]{1,0:T(8,128)(2,1)S(1)}, bf16[384,256]{1,0:T(8,128)(2,1)S(1)}, u32[]{:S(2)}, u32[]{:S(2)}) collective-permute-start(bf16[384,256]{1,0:T(8,128)(2,1)S(1)} %collective-permute-done.1.rest_1_), channel_id=1, source_target_pairs={{0,32},{8,40},{16,48},{24,56},{32,64},{40,72},{48,80},{56,88},{64,... | collective-permute-start | bytes 589832 | tf_op jit(solution)/shard_map/ppermute | solution.py:182
  41.2 1.3 %collective-permute-start.4 = (bf16[384,256]{1,0:T(8,128)(2,1)S(1)}, bf16[384,256]{1,0:T(8,128)(2,1)S(1)}, u32[]{:S(2)}, u32[]{:S(2)}) collective-permute-start(bf16[384,256]{1,0:T(8,128)(2,1)S(1)} %collective-permute-done.1.rest_1_), channel_id=1, source_target_pairs={{16,32},{24,40},{48,64},{56,72},{80,96},{88,104},{112,128},{120,13... | collective-permute-start | bytes 589832 | tf_op jit(solution)/shard_map/ppermute | solution.py:215
  42.5 8.0 %collective-permute-start.5 = (bf16[384,256]{1,0:T(8,128)(2,1)S(1)}, bf16[384,256]{1,0:T(8,128)(2,1)S(1)}, u32[]{:S(2)}, u32[]{:S(2)}) collective-permute-start(bf16[384,256]{1,0:T(8,128)(2,1)S(1)} %collective-permute-done.1.rest_1_), channel_id=1, source_target_pairs={{0,16},{8,24},{16,0},{24,8},{32,48},{40,56},{48,32},{56,40},{64,80... | collective-permute-start | bytes 589832 | tf_op jit(solution)/shard_map/ppermute | solution.py:188
  50.5 5.9 %shard_map.65 = (f32[1536,256]{1,0:T(8,128)S(1)}, f32[1544,128]{1,0:T(8,128)S(1)}) custom-call(s32[1]{0:T(128)} %bitcast.my_ref, s32[384]{0:T(512)S(1)} %copy-done.2, s32[192]{0:T(256)S(1)} %copy-done.3, f32[2,64]{1,0:T(2,128)S(1)} %bitcast.7, f32[1]{0:T(128)} %bitcast.2.norm_ref, ...), custom_call_target="tpu_custom_call", output_to_operand_aliasing={{0}: (10, {}), {1}: (11, {})} | custom-call | flops 12079595520 | bytes 4194304 | tf_op jit(solution)/shard_map/pallas_call | solution.py:154
  56.5 0.0 collective-permute-done.8.rest_0_
  56.5 8.2 %shard_map.66 = (f32[1536,256]{1,0:T(8,128)S(1)}, f32[1544,128]{1,0:T(8,128)S(1)}) custom-call(s32[1]{0:T(128)} %bitcast.my_ref, s32[384]{0:T(512)S(1)} %copy-done.2, s32[192]{0:T(256)S(1)} %copy-done.3, f32[2,64]{1,0:T(2,128)S(1)} %bitcast.8, f32[1]{0:T(128)} %bitcast.2.norm_ref, ...), custom_call_target="tpu_custom_call", output_to_operand_aliasing={{0}: (8, {}), {1}: (9, {})} | custom-call | flops 18119393280 | bytes 4194304 | tf_op jit(solution)/shard_map/pallas_call | solution.py:154
  64.6 0.0 collective-permute-done.3.rest_1_
  64.6 0.0 collective-permute-done.4.rest_2_
  64.7 0.0 collective-permute-done.5.rest_0_
  64.7 0.1 pad_maximum_fusion
  64.7 2.1 %collective-permute-start.9 = (bf16[1536,256]{1,0:T(8,128)(2,1)S(1)}, bf16[1536,256]{1,0:T(8,128)(2,1)S(1)}, u32[]{:S(2)}, u32[]{:S(2)}) collective-permute-start(bf16[1536,256]{1,0:T(8,128)(2,1)S(1)} %pad_maximum_fusion), channel_id=1, source_target_pairs={{0,8},{8,0},{16,24},{24,16},{32,40},{40,32},{48,56},{56,48},{64,72... | collective-permute-start | bytes 2359304 | tf_op jit(solution)/shard_map/ppermute | solution.py:185
  66.9 3.8 %shard_map.67 = (f32[1536,256]{1,0:T(8,128)S(1)}, f32[1544,128]{1,0:T(8,128)S(1)}) custom-call(s32[1]{0:T(128)} %bitcast.my_ref, s32[384]{0:T(512)S(1)} %copy-done.2, s32[192]{0:T(256)S(1)} %copy-done.3, f32[2,64]{1,0:T(2,128)S(1)} %bitcast.9, f32[1]{0:T(128)} %bitcast.2.norm_ref, ...), custom_call_target="tpu_custom_call", output_to_operand_aliasing={{0}: (10, {}), {1}: (11, {})} | custom-call | flops 9059696640 | bytes 4194304 | tf_op jit(solution)/shard_map/pallas_call | solution.py:154
  70.7 0.0 collective-permute-done.9.rest_0_
  70.7 0.0 copy-start.5
  70.7 6.2 %shard_map.68 = (f32[1536,256]{1,0:T(8,128)S(1)}, f32[1544,128]{1,0:T(8,128)S(1)}, bf16[384,512]{1,0:T(8,128)(2,1)S(1)}) custom-call(s32[1]{0:T(128)} %bitcast.my_ref, s32[384]{0:T(512)S(1)} %copy-done.2, s32[192]{0:T(256)S(1)} %copy-done.3, f32[2,64]{1,0:T(2,128)S(1)} %bitcast.10, f32[1]{0:T(128)} %bitcast.2.norm_ref, ...), custom_call_target="tpu_custom_call", output_to_operand_aliasing={{0}: (8, {}), {1}: (9, {})} | custom-call | flops 12079595520 | bytes 4194304 | tf_op jit(solution)/shard_map/pallas_call | solution.py:154
  76.9 0.0 copy-done.5
  76.9 1.8 %convolution_convert_fusion = bf16[384,4096]{1,0:T(8,128)(2,1)S(1)} fusion(bf16[384,512]{1,0:T(8,128)(2,1)S(1)} %get-tuple-element.34, bf16[512,4096]{1,0:T(8,128)(2,1)S(1)} %copy-done.5), kind=kOutput, calls=%fused_computation | convolution fusion | flops 1612185600 | bytes 7733248 | tf_op jit(solution)/shard_map/dot_general | solution.py:226
  78.7 43.1 %all_to_all.5 = bf16[8,48,4096]{2,1,0:T(8,128)(2,1)S(1)} all-to-all(bf16[8,48,4096]{2,1,0:T(8,128)(2,1)S(1)} %bitcast.11), channel_id=1, replica_groups=mesh['ctx'=64,'kvh'=8] {'kvh'}, dimensions={0} | all-to-all | bytes 6291456 | tf_op jit(solution)/shard_map/all_to_all | solution.py:227
  121.8 1.3 %reduce_sum.22 = bf16[48,4096]{1,0:T(8,128)(2,1)} reduce(bf16[8,48,4096]{2,1,0:T(8,128)(2,1)S(1)} %all_to_all.5, bf16[]{:T(256)} %constant.11.clone.1), dimensions={0}, to_apply=%region_2.0 | reduce | flops 1376256 | bytes 3538946 | tf_op jit(solution)/shard_map/reduce_sum | solution.py:228
  (6 shorter events, 0.1 us)
Async XLA Ops:
  0.0 17.8 %collective-permute-start = (bf16[384,256]{1,0:T(8,128)(2,1)}, bf16[384,256]{1,0:T(8,128)(2,1)S(1)}, u32[]{:S(2)}, u32[]{:S(2)}) collective-permute-start(bf16[384,256]{1,0:T(8,128)(2,1)} %rest_0_.1), channel_id=1, source_target_pairs={{0,32},{8,40},{16,48},{24,56},{32,64},{40,72},{48,80},{56,88},{64,... | collective-permute-start | bytes 589832 | tf_op jit(solution)/shard_map/ppermute | solution.py:182
  3.8 23.9 %collective-permute-start.2 = (bf16[384,256]{1,0:T(8,128)(2,1)}, bf16[384,256]{1,0:T(8,128)(2,1)S(1)}, u32[]{:S(2)}, u32[]{:S(2)}) collective-permute-start(bf16[384,256]{1,0:T(8,128)(2,1)} %rest_0_.1), channel_id=1, source_target_pairs={{0,16},{8,24},{16,0},{24,8},{32,48},{40,56},{48,32},{56,40},{64,80... | collective-permute-start | bytes 589832 | tf_op jit(solution)/shard_map/ppermute | solution.py:188
  8.8 16.5 %collective-permute-start.6 = (bf16[384,256]{1,0:T(8,128)(2,1)}, bf16[384,256]{1,0:T(8,128)(2,1)S(1)}, u32[]{:S(2)}, u32[]{:S(2)}) collective-permute-start(bf16[384,256]{1,0:T(8,128)(2,1)} %rest_0_.1), channel_id=1, source_target_pairs={{0,64},{8,72},{16,80},{24,88},{32,96},{40,104},{48,112},{56,120},{... | collective-permute-start | bytes 589832 | tf_op jit(solution)/shard_map/ppermute | solution.py:182
  16.3 1.5 %copy-start.1 = (bf16[384,256]{1,0:T(8,128)(2,1)S(1)}, bf16[384,256]{1,0:T(8,128)(2,1)}, u32[]{:S(2)}) copy-start(bf16[384,256]{1,0:T(8,128)(2,1)} %rest_0_.1) | copy-start | bytes 589828
  16.3 1.5 %copy-start.2 = (s32[384]{0:T(512)S(1)}, s32[384]{0:T(512)}, u32[]{:S(2)}) copy-start(s32[384]{0:T(512)} %doc_ref.9) | copy-start | bytes 4612
  16.6 11.2 %copy-start = (bf16[384,512]{1,0:T(8,128)(2,1)S(1)}, bf16[384,512]{1,0:T(8,128)(2,1)}, u32[]{:S(2)}) copy-start(bf16[384,512]{1,0:T(8,128)(2,1)} %query_ref.9) | copy-start | bytes 1179652
  16.6 11.2 %copy-start.3 = (s32[192]{0:T(256)S(1)}, s32[192]{0:T(256)}, u32[]{:S(2)}) copy-start(s32[192]{0:T(256)} %index_ref.9) | copy-start | bytes 2308
  16.6 11.2 %copy-start.4 = (f32[64,2]{0,1:T(2,128)S(1)}, f32[64,2]{0,1:T(2,128)}, u32[]{:S(2)}) copy-start(f32[64,2]{0,1:T(2,128)} %param.10) | copy-start | bytes 1540
  17.9 13.8 %collective-permute-start.1 = (bf16[384,256]{1,0:T(8,128)(2,1)S(1)}, bf16[384,256]{1,0:T(8,128)(2,1)S(1)}, u32[]{:S(2)}, u32[]{:S(2)}) collective-permute-start(bf16[384,256]{1,0:T(8,128)(2,1)S(1)} %collective-permute-done.rest_1_), channel_id=1, source_target_pairs={{0,64},{8,72},{16,80},{24,88},{32,96},{40,104},{48,112},{56,120},{... | collective-permute-start | bytes 589832 | tf_op jit(solution)/shard_map/ppermute | solution.py:182
  25.3 11.2 %collective-permute-start.7 = (bf16[768,256]{1,0:T(8,128)(2,1)S(1)}, bf16[768,256]{1,0:T(8,128)(2,1)S(1)}, u32[]{:S(2)}, u32[]{:S(2)}) collective-permute-start(bf16[768,256]{1,0:T(8,128)(2,1)S(1)} %pad_maximum_fusion.1), channel_id=1, source_target_pairs={{0,16},{8,24},{16,0},{24,8},{32,48},{40,56},{48,32},{56,40},{64,80... | collective-permute-start | bytes 1179656 | tf_op jit(solution)/shard_map/ppermute | solution.py:188
  36.5 20.0 %collective-permute-start.8 = (bf16[2304,256]{1,0:T(8,128)(2,1)S(1)}, bf16[2304,256]{1,0:T(8,128)(2,1)S(1)}, u32[]{:S(2)}, u32[]{:S(2)}) collective-permute-start(bf16[2304,256]{1,0:T(8,128)(2,1)S(1)} %constant_dynamic-update-slice_fusion), channel_id=1, source_target_pairs={{0,8},{8,0},{16,24},{24,16},{32,40},{40,32},{48,56},{56,48},{64,72... | collective-permute-start | bytes 3538952 | tf_op jit(solution)/shard_map/ppermute | solution.py:185
  38.4 26.2 %collective-permute-start.3 = (bf16[384,256]{1,0:T(8,128)(2,1)S(1)}, bf16[384,256]{1,0:T(8,128)(2,1)S(1)}, u32[]{:S(2)}, u32[]{:S(2)}) collective-permute-start(bf16[384,256]{1,0:T(8,128)(2,1)S(1)} %collective-permute-done.1.rest_1_), channel_id=1, source_target_pairs={{0,32},{8,40},{16,48},{24,56},{32,64},{40,72},{48,80},{56,88},{64,... | collective-permute-start | bytes 589832 | tf_op jit(solution)/shard_map/ppermute | solution.py:182
  41.2 23.4 %collective-permute-start.4 = (bf16[384,256]{1,0:T(8,128)(2,1)S(1)}, bf16[384,256]{1,0:T(8,128)(2,1)S(1)}, u32[]{:S(2)}, u32[]{:S(2)}) collective-permute-start(bf16[384,256]{1,0:T(8,128)(2,1)S(1)} %collective-permute-done.1.rest_1_), channel_id=1, source_target_pairs={{16,32},{24,40},{48,64},{56,72},{80,96},{88,104},{112,128},{120,13... | collective-permute-start | bytes 589832 | tf_op jit(solution)/shard_map/ppermute | solution.py:215
  42.5 22.1 %collective-permute-start.5 = (bf16[384,256]{1,0:T(8,128)(2,1)S(1)}, bf16[384,256]{1,0:T(8,128)(2,1)S(1)}, u32[]{:S(2)}, u32[]{:S(2)}) collective-permute-start(bf16[384,256]{1,0:T(8,128)(2,1)S(1)} %collective-permute-done.1.rest_1_), channel_id=1, source_target_pairs={{0,16},{8,24},{16,0},{24,8},{32,48},{40,56},{48,32},{56,40},{64,80... | collective-permute-start | bytes 589832 | tf_op jit(solution)/shard_map/ppermute | solution.py:188
  64.7 5.9 %collective-permute-start.9 = (bf16[1536,256]{1,0:T(8,128)(2,1)S(1)}, bf16[1536,256]{1,0:T(8,128)(2,1)S(1)}, u32[]{:S(2)}, u32[]{:S(2)}) collective-permute-start(bf16[1536,256]{1,0:T(8,128)(2,1)S(1)} %pad_maximum_fusion), channel_id=1, source_target_pairs={{0,8},{8,0},{16,24},{24,16},{32,40},{40,32},{48,56},{56,48},{64,72... | collective-permute-start | bytes 2359304 | tf_op jit(solution)/shard_map/ppermute | solution.py:185
  70.7 6.2 %copy-start.5 = (bf16[512,4096]{1,0:T(8,128)(2,1)S(1)}, bf16[512,4096]{1,0:T(8,128)(2,1)}, u32[]{:S(2)}) copy-start(bf16[512,4096]{1,0:T(8,128)(2,1)} %param.11) | copy-start | bytes 12582916

commit v12 on v10

--- a/solution.py
+++ b/solution.py
@@ -209,16 +209,16 @@
         return tuple((True, k, True) for k in back)
 
     state = attend(common, [keys_values, from_2, cross_0], own(0, 2) + cross(-1))
-    from_6 = after(from_6, *state)
     swap_024 = swapped(jnp.concatenate([keys_values, from_24, after(cross_0, from_6)]))
+    from_6 = after(from_6, *state, cross_24)
     cross_6 = crossed(from_6)
     from_8 = shifted(from_6, 4)
     from_7 = lax.ppermute(from_6, "ctx", last)
-    plan = own(4, 6) + others(own(0, 2, 4) + cross(-1))
-    state = attend(common, [from_4, from_6, swap_024], plan, state)
-    swap_6 = swapped(jnp.concatenate([cross_24, from_6, from_8, from_7, after(cross_6, *state)]))
-    plan = cross(1, 3, 5) + own(8) + cross(7)
-    state = attend(common, [cross_24, cross_6, from_8, from_7], plan, state)
+    plan = own(4, 6) + cross(1, 3) + others(own(0, 2, 4) + cross(-1))
+    state = attend(common, [from_4, from_6, cross_24, swap_024], plan, state)
+    from_8, from_7, cross_6, *_ = lax.optimization_barrier((from_8, from_7, cross_6, *state))
+    swap_6 = swapped(jnp.concatenate([cross_24, from_6, from_8, from_7, cross_6]))
+    state = attend(common, [cross_6, from_8, from_7], cross(5) + own(8) + cross(7), state)
     plan = others(cross(1, 3) + own(6, 8) + cross(7, 5))
     _, _, attn = attend(common, [swap_6], plan, state, True)
     shares = lax.axis_size("kvh")

time: 129 us -> 123 us (0.953)
  the two profiles are of different devices: /device:TPU:224 before, /device:TPU:96 now
where the time goes in v12:
time: 123 us; the launch traced here: 122 us
  blocking collectives  43.1 us (35%)
  starting transfers between devices  41.5 us (34%)
  Pallas kernels  26.6 us (22%)
  waiting for transfers between devices  4.79 us (4%)
  other arithmetic  3.68 us (3%)
  matrix products  1.8 us (1%)
    all_to_all x1, blocking collectives, local(): lax.all_to_all(partial.reshape(shares, tok // shares, -1), 'kvh', 0, 0)  43.1 us
    pallas_call x4, Pallas kernels, attend(): pl.pallas_call(functools.partial(attend_kernel, counts, plan, state is No...  26.6 us
    ppermute x4, starting transfers between devices, shifted(): lax.ppermute(block, 'ctx', [(i, i + distance) for i in range(ctx_count -...  21.9 us
    ppermute x3, starting transfers between devices, crossed(): return lax.ppermute(block, 'ctx', [(i, i ^ 2) for i in range(ctx_count)])  14.5 us
    ppermute x2, starting transfers between devices, swapped(): return lax.ppermute(block, 'ctx', [(i, i ^ 1) for i in range(ctx_count)])  3.84 us
    ppermute x4, waiting for transfers between devices, shifted(): lax.ppermute(block, 'ctx', [(i, i + distance) for i in range(ctx_count -...  3.58 us
  transfers between devices with their start and end apart: 10, of which 2 were waited for; matrix products, arithmetic and copies ran while one was open for 2% of the time, Pallas kernels for 15%

profile of v12, /device:TPU:96, one launch (start us, length us, event | category | flops | bytes accessed | tf_op | source)
XLA Modules:
  0.0 122.3 jit_solution(17963870273100583982)
XLA Ops:
  0.0 5.0 %collective-permute-start = (bf16[384,256]{1,0:T(8,128)(2,1)}, bf16[384,256]{1,0:T(8,128)(2,1)S(1)}, u32[]{:S(2)}, u32[]{:S(2)}) collective-permute-start(bf16[384,256]{1,0:T(8,128)(2,1)} %rest_0_.1), channel_id=1, source_target_pairs={{0,32},{8,40},{16,48},{24,56},{32,64},{40,72},{48,80},{56,88},{64,... | collective-permute-start | bytes 589832 | tf_op jit(solution)/shard_map/ppermute | solution.py:182
  5.0 4.9 %collective-permute-start.4 = (bf16[384,256]{1,0:T(8,128)(2,1)}, bf16[384,256]{1,0:T(8,128)(2,1)S(1)}, u32[]{:S(2)}, u32[]{:S(2)}) collective-permute-start(bf16[384,256]{1,0:T(8,128)(2,1)} %rest_0_.1), channel_id=1, source_target_pairs={{0,16},{8,24},{16,0},{24,8},{32,48},{40,56},{48,32},{56,40},{64,80... | collective-permute-start | bytes 589832 | tf_op jit(solution)/shard_map/ppermute | solution.py:188
  10.0 5.2 %collective-permute-start.1 = (bf16[384,256]{1,0:T(8,128)(2,1)}, bf16[384,256]{1,0:T(8,128)(2,1)S(1)}, u32[]{:S(2)}, u32[]{:S(2)}) collective-permute-start(bf16[384,256]{1,0:T(8,128)(2,1)} %rest_0_.1), channel_id=1, source_target_pairs={{0,64},{8,72},{16,80},{24,88},{32,96},{40,104},{48,112},{56,120},{... | collective-permute-start | bytes 589832 | tf_op jit(solution)/shard_map/ppermute | solution.py:182
  15.2 1.1 convert_multiply_fusion
  16.3 0.0 copy-start.2
  16.3 0.0 copy-start.1
  16.3 0.3 reshape.7
  16.6 0.5 reduce_sum.21
  17.0 0.0 copy-start
  17.1 0.0 copy-start.3
  17.1 0.0 copy-start.4
  17.1 0.7 reduce_max.9
  17.8 0.0 collective-permute-done.rest_1_
  17.8 0.0 copy-done.2
  17.8 0.1 broadcast_in_dim.14.starts_ref
  17.9 6.4 %collective-permute-start.3 = (bf16[384,256]{1,0:T(8,128)(2,1)S(1)}, bf16[384,256]{1,0:T(8,128)(2,1)S(1)}, u32[]{:S(2)}, u32[]{:S(2)}) collective-permute-start(bf16[384,256]{1,0:T(8,128)(2,1)S(1)} %collective-permute-done.rest_1_), channel_id=1, source_target_pairs={{0,64},{8,72},{16,80},{24,88},{32,96},{40,104},{48,112},{56,120},{... | collective-permute-start | bytes 589832 | tf_op jit(solution)/shard_map/ppermute | solution.py:182
  24.3 0.0 collective-permute-done.1.rest_0_
  24.4 2.4 %collective-permute-start.2 = (bf16[768,256]{1,0:T(8,128)(2,1)S(1)}, bf16[768,256]{1,0:T(8,128)(2,1)S(1)}, u32[]{:S(2)}, u32[]{:S(2)}) collective-permute-start(bf16[768,256]{1,0:T(8,128)(2,1)S(1)} %pad_maximum_fusion.1), channel_id=1, source_target_pairs={{0,16},{8,24},{16,0},{24,8},{32,48},{40,56},{48,32},{56,40},{64,80... | collective-permute-start | bytes 1179656 | tf_op jit(solution)/shard_map/ppermute | solution.py:188
  26.8 0.0 collective-permute-done.4.rest_2_
  26.8 3.6 %collective-permute-done.3.rest_1_ = bf16[384,256]{1,0:T(8,128)(2,1)S(1)} collective-permute-done((bf16[384,256]{1,0:T(8,128)(2,1)S(1)}, bf16[384,256]{1,0:T(8,128)(2,1)S(1)}, u32[]{:S(2)}, u32[]{:S(2)}) %collective-permute-start.3) | collective-permute-done | bytes 196640 | tf_op jit(solution)/shard_map/ppermute | solution.py:182
  30.4 0.0 copy-done.1
  30.4 0.1 pad_maximum_fusion
  30.4 1.9 %collective-permute-start.8 = (bf16[1536,256]{1,0:T(8,128)(2,1)S(1)}, bf16[1536,256]{1,0:T(8,128)(2,1)S(1)}, u32[]{:S(2)}, u32[]{:S(2)}) collective-permute-start(bf16[1536,256]{1,0:T(8,128)(2,1)S(1)} %pad_maximum_fusion), channel_id=1, source_target_pairs={{0,8},{8,0},{16,24},{24,16},{32,40},{40,32},{48,56},{56,48},{64,72... | collective-permute-start | bytes 2359304 | tf_op jit(solution)/shard_map/ppermute | solution.py:185
  32.4 0.0 copy-done
  32.4 0.0 copy-done.3
  32.4 0.0 copy-done.4
  32.4 3.9 %shard_map.64 = (f32[1536,256]{1,0:T(8,128)S(1)}, f32[1544,128]{1,0:T(8,128)S(1)}) custom-call(s32[1]{0:T(128)} %bitcast.my_ref, s32[384]{0:T(512)S(1)} %copy-done.2, s32[192]{0:T(256)S(1)} %copy-done.3, f32[2,64]{1,0:T(2,128)S(1)} %bitcast.6, f32[1]{0:T(128)} %bitcast.2.norm_ref, s32[384,128]{1,0:T(8,128)S(1)} %broadcast_in_dim.14.starts_ref, ...), custom_call_target="tpu_custom_call" | custom-call | flops 9059696640 | bytes 4194304 | tf_op jit(solution)/shard_map/pallas_call | solution.py:154
  36.3 1.2 collective-permute-done.2.rest_2_
  37.5 5.3 %collective-permute-start.5 = (bf16[384,256]{1,0:T(8,128)(2,1)S(1)}, bf16[384,256]{1,0:T(8,128)(2,1)S(1)}, u32[]{:S(2)}, u32[]{:S(2)}) collective-permute-start(bf16[384,256]{1,0:T(8,128)(2,1)S(1)} %collective-permute-done.3.rest_1_), channel_id=1, source_target_pairs={{0,32},{8,40},{16,48},{24,56},{32,64},{40,72},{48,80},{56,88},{64,... | collective-permute-start | bytes 589832 | tf_op jit(solution)/shard_map/ppermute | solution.py:182
  42.8 1.3 %collective-permute-start.6 = (bf16[384,256]{1,0:T(8,128)(2,1)S(1)}, bf16[384,256]{1,0:T(8,128)(2,1)S(1)}, u32[]{:S(2)}, u32[]{:S(2)}) collective-permute-start(bf16[384,256]{1,0:T(8,128)(2,1)S(1)} %collective-permute-done.3.rest_1_), channel_id=1, source_target_pairs={{16,32},{24,40},{48,64},{56,72},{80,96},{88,104},{112,128},{120,13... | collective-permute-start | bytes 589832 | tf_op jit(solution)/shard_map/ppermute | solution.py:216
  44.1 7.1 %collective-permute-start.7 = (bf16[384,256]{1,0:T(8,128)(2,1)S(1)}, bf16[384,256]{1,0:T(8,128)(2,1)S(1)}, u32[]{:S(2)}, u32[]{:S(2)}) collective-permute-start(bf16[384,256]{1,0:T(8,128)(2,1)S(1)} %collective-permute-done.3.rest_1_), channel_id=1, source_target_pairs={{0,16},{8,24},{16,0},{24,8},{32,48},{40,56},{48,32},{56,40},{64,80... | collective-permute-start | bytes 589832 | tf_op jit(solution)/shard_map/ppermute | solution.py:188
  51.3 0.0 collective-permute-done.8.rest_3_
  51.3 10.3 %shard_map.65 = (f32[1536,256]{1,0:T(8,128)S(1)}, f32[1544,128]{1,0:T(8,128)S(1)}) custom-call(s32[1]{0:T(128)} %bitcast.my_ref, s32[384]{0:T(512)S(1)} %copy-done.2, s32[192]{0:T(256)S(1)} %copy-done.3, f32[2,64]{1,0:T(2,128)S(1)} %bitcast.7, f32[1]{0:T(128)} %bitcast.2.norm_ref, ...), custom_call_target="tpu_custom_call", output_to_operand_aliasing={{0}: (11, {}), {1}: (12, {})} | custom-call | flops 24159191040 | bytes 4194304 | tf_op jit(solution)/shard_map/pallas_call | solution.py:154
  61.6 0.0 collective-permute-done.5.rest_1_
  61.6 0.0 collective-permute-done.6.rest_2_
  61.7 0.0 collective-permute-done.7.rest_0_
  61.7 1.9 %collective-permute-start.9 = (bf16[2304,256]{1,0:T(8,128)(2,1)S(1)}, bf16[2304,256]{1,0:T(8,128)(2,1)S(1)}, u32[]{:S(2)}, u32[]{:S(2)}) collective-permute-start(bf16[2304,256]{1,0:T(8,128)(2,1)S(1)} %constant_dynamic-update-slice_fusion), channel_id=1, source_target_pairs={{0,8},{8,0},{16,24},{24,16},{32,40},{40,32},{48,56},{56,48},{64,72... | collective-permute-start | bytes 3538952 | tf_op jit(solution)/shard_map/ppermute | solution.py:185
  63.7 4.0 %shard_map.66 = (f32[1536,256]{1,0:T(8,128)S(1)}, f32[1544,128]{1,0:T(8,128)S(1)}) custom-call(s32[1]{0:T(128)} %bitcast.my_ref, s32[384]{0:T(512)S(1)} %copy-done.2, s32[192]{0:T(256)S(1)} %copy-done.3, f32[2,64]{1,0:T(2,128)S(1)} %bitcast.8, f32[1]{0:T(128)} %bitcast.2.norm_ref, ...), custom_call_target="tpu_custom_call", output_to_operand_aliasing={{0}: (10, {}), {1}: (11, {})} | custom-call | flops 9059696640 | bytes 4194304 | tf_op jit(solution)/shard_map/pallas_call | solution.py:154
  67.7 0.0 collective-permute-done.9.rest_0_
  67.7 0.0 copy-start.5
  67.7 8.4 %shard_map.67 = (f32[1536,256]{1,0:T(8,128)S(1)}, f32[1544,128]{1,0:T(8,128)S(1)}, bf16[384,512]{1,0:T(8,128)(2,1)S(1)}) custom-call(s32[1]{0:T(128)} %bitcast.my_ref, s32[384]{0:T(512)S(1)} %copy-done.2, s32[192]{0:T(256)S(1)} %copy-done.3, f32[2,64]{1,0:T(2,128)S(1)} %bitcast.9, f32[1]{0:T(128)} %bitcast.2.norm_ref, ...), custom_call_target="tpu_custom_call", output_to_operand_aliasing={{0}: (8, {}), {1}: (9, {})} | custom-call | flops 18119393280 | bytes 4194304 | tf_op jit(solution)/shard_map/pallas_call | solution.py:154
  76.1 0.0 copy-done.5
  76.1 1.8 %convolution_convert_fusion = bf16[384,4096]{1,0:T(8,128)(2,1)S(1)} fusion(bf16[384,512]{1,0:T(8,128)(2,1)S(1)} %get-tuple-element.30, bf16[512,4096]{1,0:T(8,128)(2,1)S(1)} %copy-done.5), kind=kOutput, calls=%fused_computation | convolution fusion | flops 1612185600 | bytes 7733248 | tf_op jit(solution)/shard_map/dot_general | solution.py:225
  77.9 43.1 %all_to_all.5 = bf16[8,48,4096]{2,1,0:T(8,128)(2,1)S(1)} all-to-all(bf16[8,48,4096]{2,1,0:T(8,128)(2,1)S(1)} %bitcast.10), channel_id=1, replica_groups=mesh['ctx'=64,'kvh'=8] {'kvh'}, dimensions={0} | all-to-all | bytes 6291456 | tf_op jit(solution)/shard_map/all_to_all | solution.py:226
  121.0 1.3 %reduce_sum.22 = bf16[48,4096]{1,0:T(8,128)(2,1)} reduce(bf16[8,48,4096]{2,1,0:T(8,128)(2,1)S(1)} %all_to_all.5, bf16[]{:T(256)} %constant.11.clone.1), dimensions={0}, to_apply=%region_2.0 | reduce | flops 1376256 | bytes 3538946 | tf_op jit(solution)/shard_map/reduce_sum | solution.py:227
  (6 shorter events, 0.1 us)
Async XLA Ops:
  0.0 17.8 %collective-permute-start = (bf16[384,256]{1,0:T(8,128)(2,1)}, bf16[384,256]{1,0:T(8,128)(2,1)S(1)}, u32[]{:S(2)}, u32[]{:S(2)}) collective-permute-start(bf16[384,256]{1,0:T(8,128)(2,1)} %rest_0_.1), channel_id=1, source_target_pairs={{0,32},{8,40},{16,48},{24,56},{32,64},{40,72},{48,80},{56,88},{64,... | collective-permute-start | bytes 589832 | tf_op jit(solution)/shard_map/ppermute | solution.py:182
  5.0 21.8 %collective-permute-start.4 = (bf16[384,256]{1,0:T(8,128)(2,1)}, bf16[384,256]{1,0:T(8,128)(2,1)S(1)}, u32[]{:S(2)}, u32[]{:S(2)}) collective-permute-start(bf16[384,256]{1,0:T(8,128)(2,1)} %rest_0_.1), channel_id=1, source_target_pairs={{0,16},{8,24},{16,0},{24,8},{32,48},{40,56},{48,32},{56,40},{64,80... | collective-permute-start | bytes 589832 | tf_op jit(solution)/shard_map/ppermute | solution.py:188
  10.0 14.3 %collective-permute-start.1 = (bf16[384,256]{1,0:T(8,128)(2,1)}, bf16[384,256]{1,0:T(8,128)(2,1)S(1)}, u32[]{:S(2)}, u32[]{:S(2)}) collective-permute-start(bf16[384,256]{1,0:T(8,128)(2,1)} %rest_0_.1), channel_id=1, source_target_pairs={{0,64},{8,72},{16,80},{24,88},{32,96},{40,104},{48,112},{56,120},{... | collective-permute-start | bytes 589832 | tf_op jit(solution)/shard_map/ppermute | solution.py:182
  16.3 1.5 %copy-start.2 = (s32[384]{0:T(512)S(1)}, s32[384]{0:T(512)}, u32[]{:S(2)}) copy-start(s32[384]{0:T(512)} %doc_ref.7) | copy-start | bytes 4612
  16.3 14.1 %copy-start.1 = (bf16[384,256]{1,0:T(8,128)(2,1)S(1)}, bf16[384,256]{1,0:T(8,128)(2,1)}, u32[]{:S(2)}) copy-start(bf16[384,256]{1,0:T(8,128)(2,1)} %rest_0_.1) | copy-start | bytes 589828
  17.0 15.3 %copy-start = (bf16[384,512]{1,0:T(8,128)(2,1)S(1)}, bf16[384,512]{1,0:T(8,128)(2,1)}, u32[]{:S(2)}) copy-start(bf16[384,512]{1,0:T(8,128)(2,1)} %query_ref.7) | copy-start | bytes 1179652
  17.1 15.3 %copy-start.3 = (s32[192]{0:T(256)S(1)}, s32[192]{0:T(256)}, u32[]{:S(2)}) copy-start(s32[192]{0:T(256)} %index_ref.7) | copy-start | bytes 2308
  17.1 15.3 %copy-start.4 = (f32[64,2]{0,1:T(2,128)S(1)}, f32[64,2]{0,1:T(2,128)}, u32[]{:S(2)}) copy-start(f32[64,2]{0,1:T(2,128)} %param.10) | copy-start | bytes 1540
  17.9 12.5 %collective-permute-start.3 = (bf16[384,256]{1,0:T(8,128)(2,1)S(1)}, bf16[384,256]{1,0:T(8,128)(2,1)S(1)}, u32[]{:S(2)}, u32[]{:S(2)}) collective-permute-start(bf16[384,256]{1,0:T(8,128)(2,1)S(1)} %collective-permute-done.rest_1_), channel_id=1, source_target_pairs={{0,64},{8,72},{16,80},{24,88},{32,96},{40,104},{48,112},{56,120},{... | collective-permute-start | bytes 589832 | tf_op jit(solution)/shard_map/ppermute | solution.py:182
  24.4 13.1 %collective-permute-start.2 = (bf16[768,256]{1,0:T(8,128)(2,1)S(1)}, bf16[768,256]{1,0:T(8,128)(2,1)S(1)}, u32[]{:S(2)}, u32[]{:S(2)}) collective-permute-start(bf16[768,256]{1,0:T(8,128)(2,1)S(1)} %pad_maximum_fusion.1), channel_id=1, source_target_pairs={{0,16},{8,24},{16,0},{24,8},{32,48},{40,56},{48,32},{56,40},{64,80... | collective-permute-start | bytes 1179656 | tf_op jit(solution)/shard_map/ppermute | solution.py:188
  30.4 20.9 %collective-permute-start.8 = (bf16[1536,256]{1,0:T(8,128)(2,1)S(1)}, bf16[1536,256]{1,0:T(8,128)(2,1)S(1)}, u32[]{:S(2)}, u32[]{:S(2)}) collective-permute-start(bf16[1536,256]{1,0:T(8,128)(2,1)S(1)} %pad_maximum_fusion), channel_id=1, source_target_pairs={{0,8},{8,0},{16,24},{24,16},{32,40},{40,32},{48,56},{56,48},{64,72... | collective-permute-start | bytes 2359304 | tf_op jit(solution)/shard_map/ppermute | solution.py:185
  37.5 24.1 %collective-permute-start.5 = (bf16[384,256]{1,0:T(8,128)(2,1)S(1)}, bf16[384,256]{1,0:T(8,128)(2,1)S(1)}, u32[]{:S(2)}, u32[]{:S(2)}) collective-permute-start(bf16[384,256]{1,0:T(8,128)(2,1)S(1)} %collective-permute-done.3.rest_1_), channel_id=1, source_target_pairs={{0,32},{8,40},{16,48},{24,56},{32,64},{40,72},{48,80},{56,88},{64,... | collective-permute-start | bytes 589832 | tf_op jit(solution)/shard_map/ppermute | solution.py:182
  42.8 18.9 %collective-permute-start.6 = (bf16[384,256]{1,0:T(8,128)(2,1)S(1)}, bf16[384,256]{1,0:T(8,128)(2,1)S(1)}, u32[]{:S(2)}, u32[]{:S(2)}) collective-permute-start(bf16[384,256]{1,0:T(8,128)(2,1)S(1)} %collective-permute-done.3.rest_1_), channel_id=1, source_target_pairs={{16,32},{24,40},{48,64},{56,72},{80,96},{88,104},{112,128},{120,13... | collective-permute-start | bytes 589832 | tf_op jit(solution)/shard_map/ppermute | solution.py:216
  44.1 17.6 %collective-permute-start.7 = (bf16[384,256]{1,0:T(8,128)(2,1)S(1)}, bf16[384,256]{1,0:T(8,128)(2,1)S(1)}, u32[]{:S(2)}, u32[]{:S(2)}) collective-permute-start(bf16[384,256]{1,0:T(8,128)(2,1)S(1)} %collective-permute-done.3.rest_1_), channel_id=1, source_target_pairs={{0,16},{8,24},{16,0},{24,8},{32,48},{40,56},{48,32},{56,40},{64,80... | collective-permute-start | bytes 589832 | tf_op jit(solution)/shard_map/ppermute | solution.py:188
  61.7 5.9 %collective-permute-start.9 = (bf16[2304,256]{1,0:T(8,128)(2,1)S(1)}, bf16[2304,256]{1,0:T(8,128)(2,1)S(1)}, u32[]{:S(2)}, u32[]{:S(2)}) collective-permute-start(bf16[2304,256]{1,0:T(8,128)(2,1)S(1)} %constant_dynamic-update-slice_fusion), channel_id=1, source_target_pairs={{0,8},{8,0},{16,24},{24,16},{32,40},{40,32},{48,56},{56,48},{64,72... | collective-permute-start | bytes 3538952 | tf_op jit(solution)/shard_map/ppermute | solution.py:185
  67.7 8.4 %copy-start.5 = (bf16[512,4096]{1,0:T(8,128)(2,1)S(1)}, bf16[512,4096]{1,0:T(8,128)(2,1)}, u32[]{:S(2)}) copy-start(bf16[512,4096]{1,0:T(8,128)(2,1)} %param.11) | copy-start | bytes 12582916
